TPU v7x, 32 devices: a whole 2x2x4 slice. The times are simulated.
32 devices in a mesh: seq: 8 (over z, x), rows: 4 (over y, core).
Axes of the slice: x: 2, y: 2, z: 4, core: 2. Of those that a mesh axis runs over, the one named last changes fastest.
Arguments:
- tokens: bfloat16 [8, 1024, 768], P('rows', 'seq'), may hold values from -12 to 12
- query_weight: bfloat16 [768, 768], P(('seq', 'rows')), may hold values from -0.21875 to 0.21875
- query_bias: bfloat16 [768], P(('seq', 'rows')), may hold values from -1 to 1
- key_weight: bfloat16 [768, 768], P(('seq', 'rows')), may hold values from -0.21875 to 0.21875
- key_bias: bfloat16 [768], P(('seq', 'rows')), may hold values from -1 to 1
- value_weight: bfloat16 [768, 768], P(('seq', 'rows')), may hold values from -0.21875 to 0.21875
- value_bias: bfloat16 [768], P(('seq', 'rows')), may hold values from -0.25 to 0.25
- output_weight: bfloat16 [768, 768], P(('seq', 'rows')), may hold values from -1.75 to 1.75
- output_bias: bfloat16 [768], P(('seq', 'rows')), may hold values from -1 to 1
- first_gain: bfloat16 [768], P(('seq', 'rows')), may hold values from 0.25 to 1.75
- first_shift: bfloat16 [768], P(('seq', 'rows')), may hold values from -1.5 to 1.5
- up_weight: bfloat16 [768, 3072], P(('seq', 'rows')), may hold values from -0.21875 to 0.21875
- up_bias: bfloat16 [3072], P(('seq', 'rows')), may hold values from -1 to 1
- down_weight: bfloat16 [3072, 768], P(('seq', 'rows')), may hold values from -0.109375 to 0.109375
- down_bias: bfloat16 [768], P(('seq', 'rows')), may hold values from -1 to 1
- second_gain: bfloat16 [768], P(('seq', 'rows')), may hold values from 0.25 to 1.75
- second_shift: bfloat16 [768], P(('seq', 'rows')), may hold values from -1.5 to 1.5
- position_bias: float32 [12, 129], replicated, may hold values from -1 to 3
- feature_matrix: float32 [12, 64, 64], replicated, may hold values from -4 to 4
- cotangent: bfloat16 [8, 1024, 768], P('rows', 'seq'), may hold values from -6 to 6
Outputs:
- layer_output: float32 [8, 1024, 768], P('rows', 'seq')
- token_grads: float32 [8, 1024, 768], P('rows', 'seq')
- query_weight_grad: float32 [768, 768], P(('seq', 'rows'))
- query_bias_grad: float32 [768], P(('seq', 'rows'))
- key_weight_grad: float32 [768, 768], P(('seq', 'rows'))
- key_bias_grad: float32 [768], P(('seq', 'rows'))
- value_weight_grad: float32 [768, 768], P(('seq', 'rows'))
- value_bias_grad: float32 [768], P(('seq', 'rows'))
- output_weight_grad: float32 [768, 768], P(('seq', 'rows'))
- output_bias_grad: float32 [768], P(('seq', 'rows'))
- first_gain_grad: float32 [768], P(('seq', 'rows'))
- first_shift_grad: float32 [768], P(('seq', 'rows'))
- up_weight_grad: float32 [768, 3072], P(('seq', 'rows'))
- up_bias_grad: float32 [3072], P(('seq', 'rows'))
- down_weight_grad: float32 [3072, 768], P(('seq', 'rows'))
- down_bias_grad: float32 [768], P(('seq', 'rows'))
- second_gain_grad: float32 [768], P(('seq', 'rows'))
- second_shift_grad: float32 [768], P(('seq', 'rows'))
- position_bias_grad: float32 [12, 129], replicated
All inputs are finite; a program needn't handle non-finite values.
Results may differ from a plain program's by a relative error of at most 0.029.
Values may be sent and summed in bfloat16 or wider, within the bound.
No kernel may reach another device: no remote copies, remote signals or barrier semaphores. Data moves between devices by JAX's collectives and lax.ppermute only.
A program may use at most 256 MiB of HBM per device.

v0:
```python
import math

import jax
import jax.numpy as jnp
from jax import lax
from jax.experimental import pallas as pl
from jax.experimental.pallas import tpu as pltpu
from jax.sharding import PartitionSpec as P

BOTH = ("seq", "rows")
EPS = 1e-06
BF = jnp.bfloat16
F32 = jnp.float32


class Place:
    def __init__(self):
        self.seq = lax.axis_size("seq")
        self.rows = lax.axis_size("rows")
        self.n = self.seq * self.rows
        self.fast = self.seq == 8 and self.rows == 4
        me = lax.axis_index(BOTH)
        self.c = me % 2
        self.y = (me // 2) % 2
        self.x = (me // 4) % 2
        self.z = me // 8
        self.s = lax.axis_index("seq")

    def flip(self, a, stride):
        return lax.ppermute(a, BOTH, [(d, d ^ stride) for d in range(self.n)])

    def swap_c(self, a):
        return self.flip(a, 1)

    def swap_y(self, a):
        return self.flip(a, 2)

    def swap_x(self, a):
        return self.flip(a, 4)

    def turn_z(self, a, by):
        return lax.ppermute(a, BOTH, [(d, (d + 8 * by) % self.n) for d in range(self.n)])

    def along(self, a, by):
        pairs = [(i, i + by) for i in range(self.seq) if 0 <= i + by < self.seq]
        return lax.ppermute(a, "seq", pairs)


def ordered(first, mine, other, axis):
    return jnp.where(
        first, jnp.stack([mine, other], axis=axis), jnp.stack([other, mine], axis=axis)
    )


def gather_halves(at, left, right):
    r, half = left.shape
    c0 = at.c == 0
    if not at.fast:
        left = lax.all_gather(left, BOTH, axis=0, tiled=True)
        right = lax.all_gather(right, BOTH, axis=0, tiled=True)
        return jnp.where(c0, left, right), jnp.where(c0, right, left)
    got = at.swap_c(jnp.where(c0, right, left))
    piece = ordered(c0, jnp.where(c0, left, right), got, 0).reshape(2 * r, half)
    turned = [at.turn_z(piece, by) for by in (1, 2, 3)]
    rel = jnp.stack([piece, turned[2], turned[1], turned[0]])
    by_z = lax.dynamic_slice_in_dim(jnp.concatenate([rel, rel]), (4 - at.z) % 4, 4)
    low, high = by_z[:2], by_z[2:]
    low_x = ordered(at.x == 0, low, at.swap_x(low), 1)
    high_y = ordered(at.y == 0, high, at.swap_y(high), 1)
    low_xy = ordered(at.y == 0, low_x, at.swap_y(low_x), 2)
    high_xy = ordered(at.x == 0, high_y, at.swap_x(high_y), 1)
    mine = jnp.concatenate([low_xy, high_xy]).reshape(at.n * r, half)
    return mine, at.swap_c(mine)


def half_at(a, index, axis):
    return lax.dynamic_index_in_dim(a, index, axis, keepdims=False)


def plus(kept, got):
    return (kept.astype(F32) + got.astype(F32)).astype(BF)


def scatter_halves(at, keep, send):
    total, half = keep.shape
    r = total // at.n
    c0 = at.c == 0
    if not at.fast:
        left, right = jnp.where(c0, keep, send).astype(F32), jnp.where(c0, send, keep).astype(F32)
        return (
            lax.psum_scatter(left, BOTH, scatter_dimension=0, tiled=True),
            lax.psum_scatter(right, BOTH, scatter_dimension=0, tiled=True),
        )
    mine = plus(keep, at.swap_c(send)).reshape(4, 2, 2, 2 * r, half)
    low, high = mine[:2], mine[2:]
    low = plus(half_at(low, at.y, 2), at.swap_y(half_at(low, 1 - at.y, 2)))
    high = plus(half_at(high, at.x, 1), at.swap_x(half_at(high, 1 - at.x, 1)))
    low = plus(half_at(low, at.x, 1), at.swap_x(half_at(low, 1 - at.x, 1)))
    high = plus(half_at(high, at.y, 1), at.swap_y(half_at(high, 1 - at.y, 1)))
    by_z = jnp.concatenate([low, high])
    got = [at.turn_z(half_at(by_z, (at.z + by) % 4, 0), by).astype(F32) for by in (1, 2, 3)]
    piece = (half_at(by_z, at.z, 0).astype(F32) + got[0] + got[1] + got[2]).reshape(2, r, half)
    stays = half_at(piece, at.c, 0)
    got = at.swap_c(half_at(piece, 1 - at.c, 0))
    return jnp.where(c0, stays, got), jnp.where(c0, got, stays)


def sum_before(at, a, reverse):
    if not at.fast:
        everything = lax.all_gather(a, "seq").astype(F32)
        index = jnp.arange(at.seq).reshape((-1,) + (1,) * a.ndim)
        reached = index > at.s if reverse else index < at.s
        return jnp.sum(jnp.where(reached, everything, 0.0), axis=0)
    beside = at.swap_x(a).astype(F32)
    pair = plus(a, beside)
    before = jnp.where((at.x == 0) if reverse else (at.x == 1), beside, 0.0)
    for by in (1, 2, 3):
        if reverse:
            got = lax.ppermute(pair, BOTH, [(d, d - 8 * by) for d in range(8 * by, at.n)])
        else:
            got = lax.ppermute(pair, BOTH, [(d, d + 8 * by) for d in range(at.n - 8 * by)])
        before = before + got.astype(F32)
    return before


def sum_everywhere(at, a):
    if not at.fast:
        return lax.psum(a, BOTH)
    a = a + at.swap_c(a)
    a = a + at.swap_y(a)
    a = a + at.swap_x(a)
    a = a + at.flip(a, 8)
    return a + at.flip(a, 16)


VMEM = pltpu.VMEM
SCALAR = pl.BlockSpec(memory_space=pltpu.SMEM)
WHOLE = pl.BlockSpec(memory_space=VMEM)


def params(mib):
    return pltpu.CompilerParams(vmem_limit_bytes=mib * 2**20)


def cost(flops, moved):
    return pl.CostEstimate(flops=int(flops), bytes_accessed=int(moved), transcendentals=0)


def tdot(a, b):
    return lax.dot_general(a, b, (((0,), (0,)), ((), ())), preferred_element_type=F32)


def dot_t(a, b):
    return lax.dot_general(a, b, (((1,), (1,)), ((), ())), preferred_element_type=F32)


def dot(a, b):
    return jnp.dot(a, b, preferred_element_type=F32)


def parts(a):
    high = a.astype(BF)
    return high, (a - high.astype(F32)).astype(BF)


def left_lanes(shape):
    return lax.broadcasted_iota(jnp.int32, shape, len(shape) - 1) % 128 < 64


def two_heads(a):
    first = left_lanes(a.shape)
    wide = a.astype(F32)
    return jnp.concatenate(
        [jnp.where(first, wide, 0.0), jnp.where(first, 0.0, wide)], axis=0
    ).astype(BF)


def fold(a):
    half = a.shape[0] // 2
    return jnp.where(left_lanes((half, a.shape[1])), a[:half], a[half:])


def head_ones():
    row = lax.broadcasted_iota(jnp.int32, (128, 128), 0) // 64
    col = lax.broadcasted_iota(jnp.int32, (128, 128), 1) // 64
    return jnp.where(row == col, 1.0, 0.0).astype(BF)


def head_sums(a, ones):
    high, low = parts(a)
    return dot(high, ones) + dot(low, ones)


def features(s, g_high, g_low):
    high, low = parts(jnp.concatenate([s, s * s], axis=1))
    return jnp.exp(dot(high, g_high) + dot(high, g_low) + dot(low, g_high)) * 0.125


def features_back(t, s, g_high, g_low, ones, scale):
    high, low = parts(t)
    f_high, f_low = g_high[:128], g_low[:128]
    back = dot_t(high, f_high) + dot_t(high, f_low) + dot_t(low, f_high)
    return ((back - s * (dot(high, ones) + dot(low, ones))) * scale).astype(BF)


def lanes(p):
    return slice(p * 128, (p + 1) * 128)


def key_kernel(c_ref, tok, mine, other, gh, gl, s_out, phi_out, feat_out, v_out, state_out, vec_out):
    first = c_ref[0] == 0
    pairs, block = gh.shape[0], 128
    hw = pairs * 64
    eye = jnp.where(
        lax.broadcasted_iota(jnp.int32, (128, 128), 0) == lax.broadcasted_iota(jnp.int32, (128, 128), 1), 1.0, 0.0
    ).astype(BF)
    vecs = dot_t(eye, mine[:, 3 * hw :])[:16]
    vec_out[...] = vecs
    a = dot(tok[...], mine[:, hw : 3 * hw])
    b = dot(tok[...], other[:, hw : 3 * hw])
    left, right = jnp.where(first, a, b), jnp.where(first, b, a)
    scale = 64 ** (-0.25)
    for p in range(pairs):
        half, at = (left, p * 128) if p < pairs // 2 else (right, p * 128 - hw)
        s = (half[:, at : at + 128] + vecs[1:2, lanes(p)]) * scale
        v = (half[:, hw + at : hw + at + 128] + vecs[2:3, lanes(p)]).astype(BF)
        phi = features(s, gh[p], gl[p])
        k = phi.astype(BF)
        s_out[:, lanes(p)] = s
        phi_out[:, lanes(p)] = phi
        feat_out[:, lanes(p)] = k
        v_out[:, lanes(p)] = v
        for r in range(tok.shape[0] // block):
            rows = slice(r * block, (r + 1) * block)
            state_out[r, :64, lanes(p)] = fold(tdot(k[rows], v[rows])).astype(BF)
            total = jnp.sum(k[rows].astype(F32), axis=0, keepdims=True)
            state_out[r, 64:, lanes(p)] = jnp.broadcast_to(total, (16, 128)).astype(BF)


def query_kernel(c_ref, tok, halo, mine, other, vec, gh, gl, s_out, phi_out, feat_out, hk_out, hv_out):
    first, inner = c_ref[0] == 0, c_ref[1] > 0
    pairs = gh.shape[0]
    hw = pairs * 64
    scale = 64 ** (-0.25)
    a, b = dot(tok[...], mine[:, :hw]), dot(tok[...], other[:, :hw])
    left, right = jnp.where(first, a, b), jnp.where(first, b, a)
    for p in range(pairs):
        half, at = (left, p * 128) if p < pairs // 2 else (right, p * 128 - hw)
        s = (half[:, at : at + 128] + vec[0:1, lanes(p)]) * scale
        phi = features(s, gh[p], gl[p])
        s_out[:, lanes(p)] = s
        phi_out[:, lanes(p)] = phi
        feat_out[:, lanes(p)] = phi.astype(BF)
    a, b = dot(halo[...], mine[:, hw : 3 * hw]), dot(halo[...], other[:, hw : 3 * hw])
    left, right = jnp.where(first, a, b), jnp.where(first, b, a)
    for p in range(pairs):
        half, at = (left, p * 128) if p < pairs // 2 else (right, p * 128 - hw)
        s = (half[:, at : at + 128] + vec[1:2, lanes(p)]) * scale
        v = half[:, hw + at : hw + at + 128] + vec[2:3, lanes(p)]
        hk_out[:, lanes(p)] = jnp.where(inner, features(s, gh[p], gl[p]), 0.0).astype(BF)
        hv_out[:, lanes(p)] = jnp.where(inner, v, 0.0).astype(BF)


def block_diagonal(packed):
    return two_heads(packed)


def attention_kernel(q, k, v, hk, hv, table, state, far, context_out, ratio_out, denom_out):
    ones = head_ones()
    wmat = table[...].reshape(256, 256)
    far_row = far[0:1]
    for r in range(q.shape[0] // 128):
        rows = slice(r * 128, (r + 1) * 128)
        qr = q[rows]
        kw = jnp.concatenate([hk[rows], k[rows]], axis=0)
        vw = jnp.concatenate([hv[rows], v[rows]], axis=0)
        weighted = dot_t(two_heads(qr), kw) * wmat
        numer = fold(dot(weighted.astype(BF), vw))
        near = jnp.sum(weighted, axis=1, keepdims=True)
        near = fold(jnp.broadcast_to(near, (256, 128)))
        bd = block_diagonal(state[r, :64])
        total = state[r, 64:80].astype(F32)[0:1]
        numer = numer + far_row * dot(qr, bd)
        denom = near + far_row * head_sums(qr.astype(F32) * total, ones)
        ratio = numer / denom
        context_out[rows] = ratio.astype(BF)
        ratio_out[rows] = ratio
        denom_out[rows] = denom


def normed(x):
    centred = x - jnp.mean(x, axis=-1, keepdims=True)
    rstd = lax.rsqrt(jnp.mean(centred * centred, axis=-1, keepdims=True) + EPS)
    return centred * rstd, rstd


def norm_back(dy, xhat, rstd, gain):
    d = dy * gain
    return rstd * (
        d - jnp.mean(d, axis=-1, keepdims=True) - xhat * jnp.mean(d * xhat, axis=-1, keepdims=True)
    )


def col_sums(a):
    return jnp.sum(a, axis=0, keepdims=True)


def forward_kernel(
    c_ref, context, tok, m2, o2, m3, o3, cot, vec, bu,
    out, dlower_out, dlow_out, hlow_out, xhat_out, rstd_out, gp_out, keep_out, send_out, sums_out,
):
    c = c_ref[0]
    first = c == 0
    hw = m3.shape[1]
    hf = bu.shape[1] // 2
    a, b = dot(context[...], m2[:, :hw]), dot(context[...], o2[:, :hw])
    attn = jnp.concatenate([jnp.where(first, a, b), jnp.where(first, b, a)], axis=1)
    xhat, rstd = normed(tok[...].astype(F32) + attn + vec[3:4])
    hidden = xhat * vec[4:5] + vec[5:6]
    xhat_out[...] = xhat
    rstd_out[...] = jnp.broadcast_to(rstd, rstd_out.shape)
    h_low = hidden.astype(BF)
    hlow_out[...] = h_low
    my_rows, its_rows = pl.ds(pl.multiple_of(c * hf, hf), hf), pl.ds(pl.multiple_of((1 - c) * hf, hf), hf)
    actives = []
    for w, at, flip in ((m2, 0, False), (o2, 1, True)):
        b_left, b_right = (bu[:, hf:], bu[:, :hf]) if flip else (bu[:, :hf], bu[:, hf:])
        bias = jnp.where(first, b_left, b_right)
        upper = dot(h_low, w[:, hw:]) + bias
        cdf = 0.5 * (1.0 + lax.erf(upper * 2.0 ** (-0.5)))
        pdf = jnp.exp(-0.5 * upper * upper) * (2.0 * math.pi) ** (-0.5)
        gp_out[at] = (cdf + upper * pdf).astype(BF)
        actives.append((upper * cdf).astype(BF))
    a = dot(actives[0], m3[my_rows]) + dot(actives[1], m3[its_rows])
    b = dot(actives[0], o3[my_rows]) + dot(actives[1], o3[its_rows])
    lower = jnp.concatenate([jnp.where(first, a, b), jnp.where(first, b, a)], axis=1)
    xhat2, rstd2 = normed(hidden + lower + vec[6:7])
    gain2 = vec[7:8]
    out[...] = xhat2 * gain2 + vec[8:9]
    dy = cot[...].astype(F32)
    d_lower = norm_back(dy, xhat2, rstd2, gain2)
    dlower_out[...] = d_lower
    d_low = d_lower.astype(BF)
    dlow_out[...] = d_low
    wide = d_low.astype(F32)
    sums_out[0:1] = col_sums(wide)
    sums_out[1:2] = col_sums(dy * xhat2)
    sums_out[2:3] = col_sums(dy)
    keep = jnp.where(first, wide[:, :hw], wide[:, hw:]).astype(BF)
    send = jnp.where(first, wide[:, hw:], wide[:, :hw]).astype(BF)
    send_out[my_rows] = tdot(actives[0], send).astype(BF)
    send_out[its_rows] = tdot(actives[1], send).astype(BF)
    keep_out[my_rows] = tdot(actives[0], keep).astype(BF)
    keep_out[its_rows] = tdot(actives[1], keep).astype(BF)


def middle_kernel(
    c_ref, dlower, dlow, hlow, xhat, rstd, gp, m2, o2, m3, o3, vec, context, ratio, denom, q, state, far,
    dresid_out, dn_out, later_out, keep_out, send_out, sums_out, du_sums_out, near_out,
):
    c = c_ref[0]
    first = c == 0
    hw = m3.shape[1]
    hf = gp.shape[2]
    my_rows, its_rows = pl.ds(pl.multiple_of(c * hf, hf), hf), pl.ds(pl.multiple_of((1 - c) * hf, hf), hf)
    wide = dlow[...].astype(F32)
    keep = jnp.where(first, wide[:, :hw], wide[:, hw:]).astype(BF)
    send = jnp.where(first, wide[:, hw:], wide[:, :hw]).astype(BF)
    h_low = hlow[...]
    d_hidden = dlower[...]
    for rows, w, at, g_out in ((its_rows, o2, 1, send_out), (my_rows, m2, 0, keep_out)):
        d_active = dot_t(keep, m3[rows]) + dot_t(send, o3[rows])
        d_upper = (d_active * gp[at].astype(F32)).astype(BF)
        du_sums_out[at] = jnp.broadcast_to(col_sums(d_upper.astype(F32)), du_sums_out.shape[1:])
        g_out[:, hw:] = tdot(h_low, d_upper).astype(BF)
        d_hidden = d_hidden + dot_t(d_upper, w[:, hw:])
    xh = xhat[...]
    d_resid = norm_back(d_hidden, xh, rstd[:, 0:1], vec[4:5])
    dresid_out[...] = d_resid
    d_attn = d_resid.astype(BF)
    wide = d_attn.astype(F32)
    sums_out[0:1] = col_sums(wide)
    sums_out[1:2] = col_sums(d_hidden * xh)
    sums_out[2:3] = col_sums(d_hidden)
    keep = jnp.where(first, wide[:, :hw], wide[:, hw:]).astype(BF)
    send = jnp.where(first, wide[:, hw:], wide[:, :hw]).astype(BF)
    send_out[:, :hw] = tdot(context[...], send).astype(BF)
    keep_out[:, :hw] = tdot(context[...], keep).astype(BF)
    d_context = dot_t(keep, m2[:, :hw]) + dot_t(send, o2[:, :hw])
    ones = head_ones()
    width = 2 * hw
    pick = jnp.where(
        lax.broadcasted_iota(jnp.int32, (width, 128), 0) == 64 * lax.broadcasted_iota(jnp.int32, (width, 128), 1), 1.0, 0.0
    ).astype(BF)
    all_denoms = []
    for p in range(width // 128):
        dc = d_context[:, lanes(p)]
        inverse = 1.0 / denom[:, lanes(p)]
        dn = (dc * inverse).astype(BF)
        dd = (-head_sums(dc * ratio[:, lanes(p)], ones) * inverse).astype(BF)
        dn_out[:, lanes(p)] = dn
        all_denoms.append(dd)
        near = jnp.zeros((1, 128), F32)
        for r in range(dlow.shape[0] // 128):
            rows = slice(r * 128, (r + 1) * 128)
            qr = q[rows, lanes(p)]
            packed = fold(tdot(qr, dn[rows]))
            total = col_sums(qr.astype(F32) * dd[rows].astype(F32))
            far_row = far[0:1, lanes(p)]
            later_out[r, :64, lanes(p)] = (far_row * packed).astype(BF)
            later_out[r, 64:, lanes(p)] = jnp.broadcast_to(far_row * total, (16, 128)).astype(BF)
            held = state[r, :, lanes(p)].astype(F32)
            near = near + col_sums(held[:64] * packed) + held[64:65] * total
        near_out[:, lanes(p)] = jnp.broadcast_to(near, (8, 128))
    dn_out[:, width:] = dot(jnp.concatenate(all_denoms, axis=1), pick).astype(BF)


def spread(dn, p):
    lane = lax.broadcasted_iota(jnp.int32, dn.shape, 1)
    wide = dn.astype(F32)
    return [jnp.sum(jnp.where(lane == 2 * p + h, wide, 0.0), axis=1, keepdims=True) for h in (0, 1)]


def query_back_kernel(
    c_ref, tok, q, k, v, hk, hv, dn, dd, table, state, far, phi, s, gh, gl,
    dq_out, g_out, pos_out, sums_out,
):
    p = pl.program_id(0)
    ones = head_ones()
    wmat = table[...].reshape(256, 256)
    far_row = far[0:1]
    first = left_lanes((128, 128))
    pieces = jnp.zeros((256, 256), F32)
    grads = []
    for r in range(q.shape[0] // 128):
        rows = slice(r * 128, (r + 1) * 128)
        kw = jnp.concatenate([hk[rows], k[rows]], axis=0)
        vw = jnp.concatenate([hv[rows], v[rows]], axis=0)
        scores = dot_t(two_heads(q[rows]), kw)
        d0, d1 = spread(dd[rows], p)
        dnr = dn[rows]
        dw = dot_t(two_heads(dnr), vw) + jnp.concatenate([d0, d1], axis=0)
        pieces = pieces + dw * scores
        ds = (dw * wmat).astype(BF)
        bd = block_diagonal(state[r, :64])
        total = state[r, 64:80].astype(F32)[0:1]
        dq = fold(dot(ds, kw)) + far_row * (dot_t(dnr, bd) + jnp.where(first, d0, d1) * total)
        grads.append(
            features_back(dq * phi[rows], s[rows], gh[0], gl[0], ones, 64 ** (-0.25))
        )
    dq = jnp.concatenate(grads, axis=0)
    dq_out[...] = dq
    sums_out[...] = jnp.broadcast_to(col_sums(dq.astype(F32)), sums_out.shape)
    g_out[0] = tdot(tok[...], dq).astype(BF)
    row = lax.broadcasted_iota(jnp.int32, (256, 256), 0)
    col = lax.broadcasted_iota(jnp.int32, (256, 256), 1)
    upside = jnp.where(row + col == 255, 1.0, 0.0).astype(BF)
    high, low = parts(jnp.where(col <= row % 128 + 128, pieces, 0.0))
    turned = dot(upside, high) + dot(upside, low)
    for h in (0, 1):
        pos_out[0, 2 + h : 3 + h] = col_sums(pieces[h * 128 : (h + 1) * 128])
        skewed = pltpu.roll(turned[(1 - h) * 128 : (2 - h) * 128], 0, 1, stride=1, stride_axis=0)
        pos_out[0, h : h + 1] = col_sums(skewed)


def key_back_kernel(
    c_ref, tok, q, k, v, dn, dd, qn, dnn, ddn, table, later, phi, s, gh, gl,
    dk_out, dv_out, gk_out, gv_out, sums_out,
):
    p = pl.program_id(0)
    ones = head_ones()
    tables = jnp.concatenate(
        [table[0, :, 128:], table[1, :, 128:], table[0, :, :128], table[1, :, :128]], axis=0
    )
    dks, dvs = [], []
    for r in range(q.shape[0] // 128):
        rows = slice(r * 128, (r + 1) * 128)
        kr, vr = k[rows], v[rows]
        q4 = jnp.concatenate([two_heads(q[rows]), two_heads(qn[rows])], axis=0)
        dn4 = jnp.concatenate([two_heads(dn[rows]), two_heads(dnn[rows])], axis=0)
        dd4 = jnp.concatenate(spread(dd[rows], p) + spread(ddn[rows], p), axis=0)
        w = (dot_t(q4, kr) * tables).astype(BF)
        ds = ((dot_t(dn4, vr) + dd4) * tables).astype(BF)
        bd = block_diagonal(later[r, :64])
        total = later[r, 64:80].astype(F32)[0:1]
        dk = tdot(ds, q4) + dot_t(vr, bd) + total
        dvs.append((tdot(w, dn4) + dot(kr, bd)).astype(BF))
        dks.append(features_back(dk * phi[rows], s[rows], gh[0], gl[0], ones, 64 ** (-0.25)))
    dk, dv = jnp.concatenate(dks, axis=0), jnp.concatenate(dvs, axis=0)
    dk_out[...] = dk
    dv_out[...] = dv
    sums_out[0:8] = jnp.broadcast_to(col_sums(dk.astype(F32)), (8, 128))
    sums_out[8:16] = jnp.broadcast_to(col_sums(dv.astype(F32)), (8, 128))
    gk_out[0] = tdot(tok[...], dk).astype(BF)
    gv_out[0] = tdot(tok[...], dv).astype(BF)


def tokens_kernel(c_ref, dresid, dq, dk, dv, mine, other, out):
    first = c_ref[0] == 0
    hw = dq.shape[1] // 2
    total = dresid[...]
    for i, d in enumerate((dq, dk, dv)):
        wide = d[...].astype(F32)
        a = jnp.where(first, wide[:, :hw], wide[:, hw:]).astype(BF)
        b = jnp.where(first, wide[:, hw:], wide[:, :hw]).astype(BF)
        cols = slice(i * hw, (i + 1) * hw)
        total = total + dot_t(a, mine[:, cols]) + dot_t(b, other[:, cols])
    out[...] = total


def window_table(exp_bias, window, block_len):
    head_count = exp_bias.shape[0]
    key_span = window + block_len
    period = key_span + block_len
    far_column = exp_bias[:, window : window + 1]
    periodic = jnp.concatenate(
        [
            exp_bias[:, ::-1],
            jnp.zeros((head_count, block_len - 1), F32),
            jnp.broadcast_to(far_column, (head_count, block_len)),
        ],
        axis=1,
    )
    tiled_rows = jnp.tile(periodic, (1, block_len))
    table = tiled_rows[:, : block_len * (period - 1)].reshape(head_count, block_len, period - 1)[
        :, :, :key_span
    ]
    column = lax.broadcasted_iota(jnp.int32, (1, 1, key_span), 2)
    return table - jnp.where(column < window, far_column[:, :, None], 0.0)


def feature_blocks(matrix):
    heads, size, feats = matrix.shape
    zero = jnp.zeros((heads // 2, size, feats), F32)
    even, odd = matrix[0::2], matrix[1::2]
    half = jnp.full(zero.shape, -0.5, F32)
    blocks = jnp.concatenate(
        [
            jnp.concatenate([even, zero], axis=2),
            jnp.concatenate([zero, odd], axis=2),
            jnp.concatenate([half, zero], axis=2),
            jnp.concatenate([zero, half], axis=2),
        ],
        axis=1,
    )
    high = lax.reduce_precision(blocks, 8, 7)
    return high.astype(BF), (blocks - high).astype(BF)


def on_device(
    tokens,
    query_weight,
    query_bias,
    key_weight,
    key_bias,
    value_weight,
    value_bias,
    output_weight,
    output_bias,
    first_gain,
    first_shift,
    up_weight,
    up_bias,
    down_weight,
    down_bias,
    second_gain,
    second_shift,
    position_bias,
    feature_matrix,
    cotangent,
):
    at = Place()
    rows, block, width = tokens.shape
    heads, size, feats = feature_matrix.shape
    window = position_bias.shape[1] - 1
    pairs = heads // 2
    n = rows * block
    hw = width // 2
    ff = up_weight.shape[1]
    hf = ff // 2
    own = query_weight.shape[0]
    up_own = up_bias.shape[0] // own
    tok = tokens.reshape(n, width)
    cot = cotangent.reshape(n, width)
    first = at.c == 0
    flags = jnp.stack([at.c, at.s]).astype(jnp.int32)

    def arr(shape, kind):
        return jax.ShapeDtypeStruct(shape, kind)

    halo_tok = at.along(tok, 1)

    vectors = (
        query_bias, key_bias, value_bias, output_bias, first_gain, first_shift,
        down_bias, second_gain, second_shift,
    )
    count = len(vectors)
    small = jnp.concatenate([v[:, None] for v in vectors] + [up_bias.reshape(own, up_own)], axis=1)
    small = jnp.pad(small, ((0, 0), (0, 128 - small.shape[1])))
    m1, o1 = gather_halves(
        at,
        jnp.concatenate([query_weight[:, :hw], key_weight[:, :hw], value_weight[:, :hw], small], axis=1),
        jnp.concatenate([query_weight[:, hw:], key_weight[:, hw:], value_weight[:, hw:], small], axis=1),
    )
    b_u = m1[:, 3 * hw + count : 3 * hw + count + up_own].reshape(1, ff).astype(F32)
    m2, o2 = gather_halves(
        at,
        jnp.concatenate([output_weight[:, :hw], up_weight[:, :hf]], axis=1),
        jnp.concatenate([output_weight[:, hw:], up_weight[:, hf:]], axis=1),
    )
    m3, o3 = gather_halves(at, down_weight[:, :hw], down_weight[:, hw:])

    exp_bias = jnp.exp(position_bias)
    table = window_table(exp_bias, window, block)
    far = jnp.broadcast_to(jnp.repeat(exp_bias[:, window], size)[None], (8, width))
    gh, gl = feature_blocks(feature_matrix)

    wide32, wide16 = arr((n, width), F32), arr((n, width), BF)
    sums = arr((rows, 80, width), BF)
    sk, k_phi, k, v, local, vec = pl.pallas_call(
        key_kernel,
        out_shape=(wide32, wide32, wide16, wide16, sums, arr((16, width), F32)),
        in_specs=[SCALAR] + [WHOLE] * 5,
        out_specs=(WHOLE,) * 6,
        compiler_params=params(48),
        cost_estimate=cost(2 * n * width * 2 * width, 10e6),
        name="keys",
    )(flags, tok, m1, o1, gh, gl)
    before = sum_before(at, local, False).astype(BF)
    sq, q_phi, q, hk, hv = pl.pallas_call(
        query_kernel,
        out_shape=(wide32, wide32, wide16, wide16, wide16),
        in_specs=[SCALAR] + [WHOLE] * 7,
        out_specs=(WHOLE,) * 5,
        compiler_params=params(48),
        cost_estimate=cost(2 * n * width * 3 * width, 12e6),
        name="queries",
    )(flags, tok, halo_tok, m1, o1, vec, gh, gl)
    q_next = at.along(q, -1)

    def columns(height=n):
        return pl.BlockSpec((height, 128), lambda p, *_: (0, p))

    table_spec = pl.BlockSpec((2, block, window + block), lambda p, *_: (p, 0, 0))
    sums_spec = pl.BlockSpec((rows, 80, 128), lambda p, *_: (0, 0, p))
    g_spec = pl.BlockSpec((1, 256, 128), lambda p, *_: (p, 0, 0))
    tok_spec = pl.BlockSpec((n, width), lambda p, *_: (0, 0))
    dd_spec = pl.BlockSpec((n, 128), lambda p, *_: (0, pairs))
    context, ratio, denom = pl.pallas_call(
        attention_kernel,
        grid=(pairs,),
        out_shape=(wide16, wide32, wide32),
        in_specs=[columns()] * 5 + [table_spec, sums_spec, columns(8)],
        out_specs=(columns(),) * 3,
        compiler_params=params(32),
        cost_estimate=cost(1e9, 8e6),
        name="attention",
    )(q, k, v, hk, hv, table, before, far)

    out, d_lower, d_low, h_low, xhat, rstd, gp, keep3, send3, sums3 = pl.pallas_call(
        forward_kernel,
        out_shape=(
            wide32, wide32, wide16, wide16, wide32, arr((n, 128), F32), arr((2, n, hf), BF),
            arr((ff, hw), BF), arr((ff, hw), BF), arr((8, width), F32),
        ),
        in_specs=[SCALAR] + [WHOLE] * 9,
        out_specs=(WHOLE,) * 10,
        compiler_params=params(56),
        cost_estimate=cost(2 * n * width * (width + 3 * ff), 24e6),
        name="forward",
    )(flags, context, tok, m2, o2, m3, o3, cot, vec, b_u)
    s_d = scatter_halves(at, keep3, send3)
    d_resid, dn, local, keep2, send2, sums2, du_sums, near = pl.pallas_call(
        middle_kernel,
        out_shape=(
            wide32, arr((n, width + 128), BF), sums, arr((width, hw + hf), BF), arr((width, hw + hf), BF),
            arr((8, width), F32), arr((2, 8, hf), F32), arr((8, width), F32),
        ),
        in_specs=[SCALAR] + [WHOLE] * 17,
        out_specs=(WHOLE,) * 8,
        compiler_params=params(56),
        cost_estimate=cost(2 * n * width * (2 * width + 3 * ff), 28e6),
        name="middle",
    )(flags, d_lower, d_low, h_low, xhat, rstd, gp, m2, o2, m3, o3, vec, context, ratio, denom, q, before, far)
    dn_next = at.along(dn, -1)
    after = sum_before(at, local, True).astype(BF)
    s_uo = scatter_halves(at, keep2, send2)

    def half_spec():
        return pl.BlockSpec((1, width, 128), lambda p, c: ((p // (pairs // 2)) ^ c[0], 0, p % (pairs // 2)))

    halves = arr((2, width, hw), BF)
    dq, gq, pos, sums_q = pl.pallas_call(
        query_back_kernel,
        grid_spec=pltpu.PrefetchScalarGridSpec(
            num_scalar_prefetch=1,
            grid=(pairs,),
            in_specs=[tok_spec] + [columns()] * 6 + [dd_spec, table_spec, sums_spec, columns(8)]
            + [columns()] * 2 + [g_spec] * 2,
            out_specs=(
                columns(), half_spec(), pl.BlockSpec((1, 8, 256), lambda p, c: (p, 0, 0)), columns(8),
            ),
        ),
        out_shape=(wide16, halves, arr((pairs, 8, 256), F32), arr((8, width), F32)),
        compiler_params=params(32),
        cost_estimate=cost(2e9, 10e6),
        name="query_back",
    )(flags, tok, q, k, v, hk, hv, dn, dn, table, before, far, q_phi, sq, gh, gl)
    s_q = scatter_halves(at, gq[0], gq[1])
    diag = pos[:, 0:2].reshape(heads, 2 * block)
    plain = pos[:, 2:4].reshape(heads, 2 * block)
    far_grad = (
        jnp.sum(diag[:, : 2 * block - window], axis=1)
        - jnp.sum(plain[:, :window], axis=1)
        + jnp.sum(near[0].reshape(heads, size), axis=1)
    )
    position_grad = sum_everywhere(
        at,
        jnp.concatenate(
            [exp_bias[:, :window] * diag[:, : 2 * block - window - 1 : -1], (exp_bias[:, window] * far_grad)[:, None]], axis=1
        ),
    )
    dk, dv, gk, gv, sums_kv = pl.pallas_call(
        key_back_kernel,
        grid_spec=pltpu.PrefetchScalarGridSpec(
            num_scalar_prefetch=1,
            grid=(pairs,),
            in_specs=[tok_spec] + [columns()] * 4 + [dd_spec] + [columns()] * 2
            + [dd_spec, table_spec, sums_spec] + [columns()] * 2 + [g_spec] * 2,
            out_specs=(columns(), columns(), half_spec(), half_spec(), columns(16)),
        ),
        out_shape=(wide16, wide16, halves, halves, arr((16, width), F32)),
        compiler_params=params(32),
        cost_estimate=cost(3e9, 12e6),
        name="key_back",
    )(flags, tok, q, k, v, dn, dn, q_next, dn_next, dn_next, table, after, k_phi, sk, gh, gl)

    g_small = jnp.stack(
        [sums_q[0], sums_kv[0], sums_kv[8], sums2[0], sums2[1], sums2[2], sums3[0], sums3[1], sums3[2]]
    ).T
    du = jnp.where(first, du_sums[:, 0], du_sums[::-1, 0]).reshape(width, up_own)
    g_small = jnp.concatenate([g_small, du], axis=1)
    g_small = jnp.pad(g_small, ((0, 0), (0, 128 - g_small.shape[1]))).astype(BF)
    s_kv = scatter_halves(
        at,
        jnp.concatenate([gk[0], gv[0], g_small], axis=1),
        jnp.concatenate([gk[1], gv[1], g_small], axis=1),
    )
    d_tokens = pl.pallas_call(
        tokens_kernel,
        out_shape=wide32,
        in_specs=[SCALAR] + [WHOLE] * 6,
        out_specs=WHOLE,
        compiler_params=params(40),
        cost_estimate=cost(2 * n * width * 3 * width, 8e6),
        name="tokens",
    )(flags, d_resid, dq, dk, dv, m1, o1)

    def both(pair, start, size):
        return jnp.concatenate([pair[0][:, start : start + size], pair[1][:, start : start + size]], axis=1)

    s_small = s_kv[0][:, 2 * hw :]
    bq, bk, bv, bo, sg1, ss1, bd, sg2, ss2 = [s_small[:, i] for i in range(count)]
    bu = s_small[:, count : count + up_own].reshape(-1)
    return (
        out.reshape(rows, block, width),
        d_tokens.reshape(rows, block, width),
        both(s_q, 0, hw),
        bq,
        both(s_kv, 0, hw),
        bk,
        both(s_kv, hw, hw),
        bv,
        both(s_uo, 0, hw),
        bo,
        sg1,
        ss1,
        both(s_uo, hw, hf),
        bu,
        both(s_d, 0, hw),
        bd,
        sg2,
        ss2,
        position_grad,
    )


def solution(mesh):
    matrix, vector, split = P(BOTH, None), P(BOTH), P("rows", "seq", None)
    return jax.shard_map(
        on_device,
        mesh=mesh,
        in_specs=(split,)
        + (matrix, vector) * 4
        + (vector, vector)
        + (matrix, vector) * 2
        + (vector, vector)
        + (P(), P(), split),
        out_specs=(split, split)
        + (matrix, vector) * 4
        + (vector, vector)
        + (matrix, vector) * 2
        + (vector, vector)
        + (P(),),
        check_vma=False,
    )
```

profile of v0, /device:TPU:0, one launch (start us, length us, event | category | flops | bytes accessed | tf_op | source)
XLA Modules:
  0.0 428.1 jit_solution(3143020095952962993)
XLA Ops:
  13.0 5.2 %collective-permute-start = (bf16[256,768]{1,0:T(8,128)(2,1)}, bf16[256,768]{1,0:T(8,128)(2,1)}, u32[]{:S(2)}, u32[]{:S(2)}) collective-permute-start(bf16[256,768]{1,0:T(8,128)(2,1)} %bitcast.2.tok), channel_id=1, source_target_pairs={{0,4},{4,8},{8,12},{12,16},{16,20},{20,24},{24,28},{1,5},{5,9},{9,... | collective-permute-start | bytes 1179656 | tf_op jit(solution)/shard_map/ppermute | solution.py:46
  26.7 6.6 %collective-permute-done.3 = bf16[48,1280]{1,0:T(8,128)(2,1)S(1)} collective-permute-done((bf16[48,1280]{1,0:T(8,128)(2,1)S(1)}, bf16[48,1280]{1,0:T(8,128)(2,1)S(1)}, u32[]{:S(2)}, u32[]{:S(2)}) %collective-permute-start.3) | collective-permute-done | bytes 122912 | tf_op jit(solution)/shard_map/ppermute | solution.py:42
  37.3 5.2 %collective-permute-start.16 = (bf16[48,1920]{1,0:T(8,128)(2,1)S(1)}, bf16[48,1920]{1,0:T(8,128)(2,1)S(1)}, u32[]{:S(2)}, u32[]{:S(2)}) collective-permute-start(bf16[48,1920]{1,0:T(8,128)(2,1)S(1)} %bitcast.339), channel_id=1, source_target_pairs={{0,16},{1,17},{2,18},{3,19},{4,20},{5,21},{6,22},{7,23},{8,24},{9,... | collective-permute-start | bytes 552968 | tf_op jit(solution)/shard_map/ppermute | solution.py:42
  51.2 7.0 %collective-permute-start.5 = (bf16[2,48,1280]{2,1,0:T(8,128)(2,1)S(1)}, bf16[2,48,1280]{2,1,0:T(8,128)(2,1)S(1)}, u32[]{:S(2)}, u32[]{:S(2)}) collective-permute-start(bf16[2,48,1280]{2,1,0:T(8,128)(2,1)S(1)} %get-tuple-element.166), channel_id=1, source_target_pairs={{0,4},{1,5},{2,6},{3,7},{4,0},{5,1},{6,2},{7,3},{8,12},{9,13},{10,... | collective-permute-start | bytes 737288 | tf_op jit(solution)/shard_map/ppermute | solution.py:30
  62.6 5.6 %collective-permute-start.27 = (bf16[2,192,384]{2,1,0:T(8,128)(2,1)S(1)}, bf16[2,192,384]{2,1,0:T(8,128)(2,1)S(1)}, u32[]{:S(2)}, u32[]{:S(2)}) collective-permute-start(bf16[2,192,384]{2,1,0:T(8,128)(2,1)S(1)} %get-tuple-element.164), channel_id=1, source_target_pairs={{0,4},{1,5},{2,6},{3,7},{4,0},{5,1},{6,2},{7,3},{8,12},{9,13},{10,... | collective-permute-start | bytes 884744 | tf_op jit(solution)/shard_map/ppermute | solution.py:30
  86.3 7.9 %collective-permute-done.8 = bf16[2,2,48,1280]{3,2,1,0:T(8,128)(2,1)S(1)} collective-permute-done((bf16[2,2,48,1280]{3,2,1,0:T(8,128)(2,1)S(1)}, bf16[2,2,48,1280]{3,2,1,0:T(8,128)(2,1)S(1)}, u32[]{:S(2)}, u32[]{:S(2)}) %collective-permute-start.8) | collective-permute-done | bytes 491552 | tf_op jit(solution)/shard_map/ppermute | solution.py:30
  96.7 21.1 %collective-permute-done.21 = bf16[2,2,48,1920]{3,2,1,0:T(8,128)(2,1)S(1)} collective-permute-done((bf16[2,2,48,1920]{3,2,1,0:T(8,128)(2,1)S(1)}, bf16[2,2,48,1920]{3,2,1,0:T(8,128)(2,1)S(1)}, u32[]{:S(2)}, u32[]{:S(2)}) %collective-permute-start.21) | collective-permute-done | bytes 737312 | tf_op jit(solution)/shard_map/ppermute | solution.py:30
  132.6 5.4 %keys.1 = (f32[256,768]{1,0:T(8,128)S(1)}, f32[256,768]{1,0:T(8,128)S(1)}, bf16[256,768]{1,0:T(8,128)(2,1)S(1)}, bf16[256,768]{1,0:T(8,128)(2,1)S(1)}, bf16[2,80...) custom-call(s32[2]{0:T(128)S(1)} %pad_add_fusion.c_ref, bf16[256,768]{1,0:T(8,128)(2,1)} %bitcast.2.tok, ...), custom_call_target="tpu_custom_call" | custom-call | flops 603979776 | bytes 10000000 | tf_op jit(solution)/shard_map/keys/pallas_call | solution.py:620
  144.1 6.6 %collective-permute-done.10 = bf16[2,80,768]{2,1,0:T(8,128)(2,1)} collective-permute-done((bf16[2,80,768]{2,1,0:T(8,128)(2,1)}, bf16[2,80,768]{2,1,0:T(8,128)(2,1)}, u32[]{:S(2)}, u32[]{:S(2)}) %collective-permute-start.10) | collective-permute-done | bytes 245792 | tf_op jit(solution)/shard_map/ppermute | solution.py:30
  152.5 7.4 %collective-permute-start.11 = (bf16[2,80,768]{2,1,0:T(8,128)(2,1)}, bf16[2,80,768]{2,1,0:T(8,128)(2,1)}, u32[]{:S(2)}, u32[]{:S(2)}) collective-permute-start(bf16[2,80,768]{2,1,0:T(8,128)(2,1)} %fusion.19), channel_id=1, source_target_pairs={{0,8},{1,9},{2,10},{3,11},{4,12},{5,13},{6,14},{7,15},{8,16},{9,17... | collective-permute-start | bytes 737288 | tf_op jit(solution)/shard_map/ppermute | solution.py:121
  171.2 5.2 %queries.1 = (f32[256,768]{1,0:T(8,128)S(1)}, f32[256,768]{1,0:T(8,128)S(1)}, bf16[256,768]{1,0:T(8,128)(2,1)S(1)}, bf16[256,768]{1,0:T(8,128)(2,1)S(1)}, bf16[256,768]{1,0:T(8,128)(2,1)S(1)}) custom-call(s32[2]{0:T(128)S(1)} %pad_add_fusion.c_ref, bf16[256,768]{1,0:T(8,128)(2,1)} %bitcast.2.tok, bf16[256,768]{1,0:T(8,128)(2,1)} %collective-permute-done.halo, ...), custom_call_target="tpu_custom_call" | custom-call | flops 905969664 | bytes 12000000 | tf_op jit(solution)/shard_map/queries/pallas_call | solution.py:630
  179.2 4.9 %attention.1 = (bf16[256,768]{1,0:T(8,128)(2,1)S(1)}, f32[256,768]{1,0:T(8,128)S(1)}, f32[256,768]{1,0:T(8,128)S(1)}) custom-call(bf16[256,768]{1,0:T(8,128)(2,1)S(1)} %get-tuple-element.61.q, bf16[256,768]{1,0:T(8,128)(2,1)S(1)} %copy-done.15, bf16[256,768]{1,0:T(8,128)(2,1)S(1)} %copy-done.18, bf16[256,768]{1,0:T(8,128)(2,1)S(1)} %get-tuple-element.64.hk, ...), custom_call_target="tpu_custom_call" | custom-call | flops 1000000000 | bytes 8000000 | tf_op jit(solution)/shard_map/attention/pallas_call | solution.py:649
  184.9 13.7 %forward.1 = (f32[256,768]{1,0:T(8,128)}, f32[256,768]{1,0:T(8,128)}, bf16[256,768]{1,0:T(8,128)(2,1)}, bf16[256,768]{1,0:T(8,128)(2,1)}, f32[256,768]{1,0:T(8,1...) custom-call(s32[2]{0:T(128)} %copy-done.43, ...), custom_call_target="tpu_custom_call" | custom-call | flops 3925868544 | bytes 24000000 | tf_op jit(solution)/shard_map/forward/pallas_call | solution.py:660
  198.7 14.5 %middle.1 = (f32[256,768]{1,0:T(8,128)}, bf16[256,896]{1,0:T(8,128)(2,1)}, bf16[2,80,768]{2,1,0:T(8,128)(2,1)}, bf16[768,1920]{1,0:T(8,128)(2,1)}, bf16[768,1920...) custom-call(s32[2]{0:T(128)} %copy-done.43, f32[256,768]{1,0:T(8,128)} %get-tuple-element.69.dlower, ...), custom_call_target="tpu_custom_call" | custom-call | flops 4227858432 | bytes 28000000 | tf_op jit(solution)/shard_map/middle/pallas_call | solution.py:673
  214.3 10.9 %query_back.1 = (bf16[256,768]{1,0:T(8,128)(2,1)S(1)}, bf16[2,768,384]{2,1,0:T(8,128)(2,1)S(1)}, f32[6,8,256]{2,1,0:T(8,128)S(1)}, f32[8,768]{1,0:T(8,128)S(1)}) custom-call(s32[2]{0:T(128)S(1)} %copy-done.44, bf16[256,768]{1,0:T(8,128)(2,1)} %bitcast.2.tok, bf16[256,768]{1,0:T(8,128)(2,1)S(1)} %copy-done.11, bf16[256,768]{1,0:T(8,128)(2,1)S(1)} %copy-done.15, ...), custom_call_target="tpu_custom_call" | custom-call | flops 2000000000 | bytes 10000000 | tf_op jit(solution)/shard_map/query_back/pallas_call | solution.py:693
  239.0 6.4 %collective-permute-start.77 = (f32[12,129]{1,0:T(8,128)S(1)}, f32[12,129]{1,0:T(8,128)S(1)}, u32[]{:S(2)}, u32[]{:S(2)}) collective-permute-start(f32[12,129]{1,0:T(8,128)S(1)} %add.383), channel_id=1, source_target_pairs={{0,8},{1,9},{2,10},{3,11},{4,12},{5,13},{6,14},{7,15},{8,0},{9,1},... | collective-permute-start | bytes 18584 | tf_op jit(solution)/shard_map/ppermute | solution.py:30
  248.1 12.8 %collective-permute-done.77 = f32[12,129]{1,0:T(8,128)S(1)} collective-permute-done((f32[12,129]{1,0:T(8,128)S(1)}, f32[12,129]{1,0:T(8,128)S(1)}, u32[]{:S(2)}, u32[]{:S(2)}) %collective-permute-start.77) | collective-permute-done | bytes 6224 | tf_op jit(solution)/shard_map/ppermute | solution.py:30
  274.7 13.5 %collective-permute-done.36 = bf16[2,80,768]{2,1,0:T(8,128)(2,1)S(1)} collective-permute-done((bf16[2,80,768]{2,1,0:T(8,128)(2,1)S(1)}, bf16[2,80,768]{2,1,0:T(8,128)(2,1)S(1)}, u32[]{:S(2)}, u32[]{:S(2)}) %collective-permute-start.36) | collective-permute-done | bytes 245792 | tf_op jit(solution)/shard_map/ppermute | solution.py:119
  288.5 11.9 %key_back.1 = (bf16[256,768]{1,0:T(8,128)(2,1)S(1)}, bf16[256,768]{1,0:T(8,128)(2,1)S(1)}, bf16[2,768,384]{2,1,0:T(8,128)(2,1)S(1)}, bf16[2,768,384]{2,1,0:T(8,128)(2,1)S(1)}, f32[16,768]{1,0:T(8,128)S(1)}) custom-call(s32[2]{0:T(128)S(1)} %copy-done.44, bf16[256,768]{1,0:T(8,128)(2,1)} %bitcast.2.tok, bf16[256,768]{1,0:T(8,128)(2,1)S(1)} %copy-done.11, ...), custom_call_target="tpu_custom_call" | custom-call | flops 3000000000 | bytes 12000000 | tf_op jit(solution)/shard_map/key_back/pallas_call | solution.py:723
  371.6 5.6 %collective-permute-done.66 = bf16[2,2,192,384]{3,2,0,1:T(8,128)(2,1)S(1)} collective-permute-done((bf16[2,2,192,384]{3,2,0,1:T(8,128)(2,1)}, bf16[2,2,192,384]{3,2,0,1:T(8,128)(2,1)S(1)}, u32[]{:S(2)}, u32[]{:S(2)}) %collective-permute-start.66) | collective-permute-done | bytes 589856 | tf_op jit(solution)/shard_map/ppermute | solution.py:30
  383.6 9.3 %collective-permute-done.67 = bf16[2,192,384]{2,1,0:T(8,128)(2,1)S(1)} collective-permute-done((bf16[2,192,384]{2,1,0:T(8,128)(2,1)S(1)}, bf16[2,192,384]{2,1,0:T(8,128)(2,1)S(1)}, u32[]{:S(2)}, u32[]{:S(2)}) %collective-permute-start.67) | collective-permute-done | bytes 294944 | tf_op jit(solution)/shard_map/ppermute | solution.py:30
  400.1 6.8 %collective-permute-done.60 = bf16[2,48,1920]{2,1,0:T(8,128)(2,1)S(1)} collective-permute-done((bf16[2,48,1920]{2,1,0:T(8,128)(2,1)S(1)}, bf16[2,48,1920]{2,1,0:T(8,128)(2,1)S(1)}, u32[]{:S(2)}, u32[]{:S(2)}) %collective-permute-start.60) | collective-permute-done | bytes 368672 | tf_op jit(solution)/shard_map/ppermute | solution.py:30
  414.0 5.3 %collective-permute-done.61 = bf16[48,1920]{1,0:T(8,128)(2,1)S(1)} collective-permute-done((bf16[48,1920]{1,0:T(8,128)(2,1)S(1)}, bf16[48,1920]{1,0:T(8,128)(2,1)S(1)}, u32[]{:S(2)}, u32[]{:S(2)}) %collective-permute-start.61) | collective-permute-done | bytes 184352 | tf_op jit(solution)/shard_map/ppermute | solution.py:42
  419.2 5.5 %collective-permute-done.62 = bf16[48,1920]{1,0:T(8,128)(2,1)S(1)} collective-permute-done((bf16[48,1920]{1,0:T(8,128)(2,1)S(1)}, bf16[48,1920]{1,0:T(8,128)(2,1)S(1)}, u32[]{:S(2)}, u32[]{:S(2)}) %collective-permute-start.62) | collective-permute-done | bytes 184352 | tf_op jit(solution)/shard_map/ppermute | solution.py:42
  (473 shorter events, 221.2 us)
Async XLA Ops:
  13.0 150.7 %collective-permute-start = (bf16[256,768]{1,0:T(8,128)(2,1)}, bf16[256,768]{1,0:T(8,128)(2,1)}, u32[]{:S(2)}, u32[]{:S(2)}) collective-permute-start(bf16[256,768]{1,0:T(8,128)(2,1)} %bitcast.2.tok), channel_id=1, source_target_pairs={{0,4},{4,8},{8,12},{12,16},{16,20},{20,24},{24,28},{1,5},{5,9},{9,... | collective-permute-start | bytes 1179656 | tf_op jit(solution)/shard_map/ppermute | solution.py:46
  25.5 21.1 %collective-permute-start.25 = (bf16[192,384]{1,0:T(8,128)(2,1)S(1)}, bf16[192,384]{1,0:T(8,128)(2,1)S(1)}, u32[]{:S(2)}, u32[]{:S(2)}) collective-permute-start(bf16[192,384]{1,0:T(8,128)(2,1)S(1)} %bitcast.350), channel_id=1, source_target_pairs={{0,16},{1,17},{2,18},{3,19},{4,20},{5,21},{6,22},{7,23},{8,24},{9,... | collective-permute-start | bytes 442376 | tf_op jit(solution)/shard_map/ppermute | solution.py:42
  33.3 25.1 %collective-permute-start.15 = (bf16[48,1920]{1,0:T(8,128)(2,1)S(1)}, bf16[48,1920]{1,0:T(8,128)(2,1)S(1)}, u32[]{:S(2)}, u32[]{:S(2)}) collective-permute-start(bf16[48,1920]{1,0:T(8,128)(2,1)S(1)} %bitcast.338), channel_id=1, source_target_pairs={{0,24},{1,25},{2,26},{3,27},{4,28},{5,29},{6,30},{7,31},{8,0},{9,1... | collective-permute-start | bytes 552968 | tf_op jit(solution)/shard_map/ppermute | solution.py:42
  37.3 23.8 %collective-permute-start.16 = (bf16[48,1920]{1,0:T(8,128)(2,1)S(1)}, bf16[48,1920]{1,0:T(8,128)(2,1)S(1)}, u32[]{:S(2)}, u32[]{:S(2)}) collective-permute-start(bf16[48,1920]{1,0:T(8,128)(2,1)S(1)} %bitcast.339), channel_id=1, source_target_pairs={{0,16},{1,17},{2,18},{3,19},{4,20},{5,21},{6,22},{7,23},{8,24},{9,... | collective-permute-start | bytes 552968 | tf_op jit(solution)/shard_map/ppermute | solution.py:42
  73.2 22.0 %collective-permute-start.6 = (bf16[2,2,48,1280]{3,2,0,1:T(8,128)(2,1)S(1)}, bf16[2,2,48,1280]{3,2,0,1:T(8,128)(2,1)S(1)}, u32[]{:S(2)}, u32[]{:S(2)}) collective-permute-start(bf16[2,2,48,1280]{3,2,0,1:T(8,128)(2,1)S(1)} %maximum_select_fusion.13), channel_id=1, source_target_pairs={{0,2},{1,3},{2,0},{3,1},{4,6},{5,7},{6,4},{7,5},{8,10},{9,11},{10,... | collective-permute-start | bytes 1474568 | tf_op jit(solution)/shard_map/ppermute | solution.py:30
  81.1 39.6 %collective-permute-start.30 = (bf16[2,2,192,384]{3,2,1,0:T(8,128)(2,1)S(1)}, bf16[2,2,192,384]{3,2,1,0:T(8,128)(2,1)S(1)}, u32[]{:S(2)}, u32[]{:S(2)}) collective-permute-start(bf16[2,2,192,384]{3,2,1,0:T(8,128)(2,1)S(1)} %maximum_select_fusion.11), channel_id=1, source_target_pairs={{0,4},{1,5},{2,6},{3,7},{4,0},{5,1},{6,2},{7,3},{8,12},{9,13},{10,... | collective-permute-start | bytes 1769480 | tf_op jit(solution)/shard_map/ppermute | solution.py:30
  84.8 33.0 %collective-permute-start.21 = (bf16[2,2,48,1920]{3,2,1,0:T(8,128)(2,1)S(1)}, bf16[2,2,48,1920]{3,2,1,0:T(8,128)(2,1)S(1)}, u32[]{:S(2)}, u32[]{:S(2)}) collective-permute-start(bf16[2,2,48,1920]{3,2,1,0:T(8,128)(2,1)S(1)} %maximum_select_fusion.8), channel_id=1, source_target_pairs={{0,4},{1,5},{2,6},{3,7},{4,0},{5,1},{6,2},{7,3},{8,12},{9,13},{10,... | collective-permute-start | bytes 2211848 | tf_op jit(solution)/shard_map/ppermute | solution.py:30
  94.3 23.8 %collective-permute-start.19 = (bf16[2,2,48,1920]{3,2,0,1:T(8,128)(2,1)S(1)}, bf16[2,2,48,1920]{3,2,0,1:T(8,128)(2,1)S(1)}, u32[]{:S(2)}, u32[]{:S(2)}) collective-permute-start(bf16[2,2,48,1920]{3,2,0,1:T(8,128)(2,1)S(1)} %maximum_select_fusion.7), channel_id=1, source_target_pairs={{0,2},{1,3},{2,0},{3,1},{4,6},{5,7},{6,4},{7,5},{8,10},{9,11},{10,... | collective-permute-start | bytes 2211848 | tf_op jit(solution)/shard_map/ppermute | solution.py:30
  95.2 25.7 %collective-permute-start.28 = (bf16[2,2,192,384]{3,2,0,1:T(8,128)(2,1)S(1)}, bf16[2,2,192,384]{3,2,0,1:T(8,128)(2,1)S(1)}, u32[]{:S(2)}, u32[]{:S(2)}) collective-permute-start(bf16[2,2,192,384]{3,2,0,1:T(8,128)(2,1)S(1)} %maximum_select_fusion.10), channel_id=1, source_target_pairs={{0,2},{1,3},{2,0},{3,1},{4,6},{5,7},{6,4},{7,5},{8,10},{9,11},{10,... | collective-permute-start | bytes 1769480 | tf_op jit(solution)/shard_map/ppermute | solution.py:30
  120.1 64.8 %collective-permute-start.22 = (bf16[768,1920]{1,0:T(8,128)(2,1)}, bf16[768,1920]{1,0:T(8,128)(2,1)}, u32[]{:S(2)}, u32[]{:S(2)}) collective-permute-start(bf16[768,1920]{1,0:T(8,128)(2,1)} %bitcast.57.m2), channel_id=1, source_target_pairs={{0,1},{1,0},{2,3},{3,2},{4,5},{5,4},{6,7},{7,6},{8,9},{9,8},{10,11... | collective-permute-start | bytes 8847368 | tf_op jit(solution)/shard_map/ppermute | solution.py:30
  122.7 62.2 %collective-permute-start.31 = (bf16[3072,384]{1,0:T(8,128)(2,1)}, bf16[3072,384]{1,0:T(8,128)(2,1)}, u32[]{:S(2)}, u32[]{:S(2)}) collective-permute-start(bf16[3072,384]{1,0:T(8,128)(2,1)} %bitcast.75.m3), channel_id=1, source_target_pairs={{0,1},{1,0},{2,3},{3,2},{4,5},{5,4},{6,7},{7,6},{8,9},{9,8},{10,11... | collective-permute-start | bytes 7077896 | tf_op jit(solution)/shard_map/ppermute | solution.py:30
  152.5 24.8 %collective-permute-start.11 = (bf16[2,80,768]{2,1,0:T(8,128)(2,1)}, bf16[2,80,768]{2,1,0:T(8,128)(2,1)}, u32[]{:S(2)}, u32[]{:S(2)}) collective-permute-start(bf16[2,80,768]{2,1,0:T(8,128)(2,1)} %fusion.19), channel_id=1, source_target_pairs={{0,8},{1,9},{2,10},{3,11},{4,12},{5,13},{6,14},{7,15},{8,16},{9,17... | collective-permute-start | bytes 737288 | tf_op jit(solution)/shard_map/ppermute | solution.py:121
  228.7 35.8 %collective-permute-start.34 = (bf16[2,80,768]{2,1,0:T(8,128)(2,1)}, bf16[2,80,768]{2,1,0:T(8,128)(2,1)S(1)}, u32[]{:S(2)}, u32[]{:S(2)}) collective-permute-start(bf16[2,80,768]{2,1,0:T(8,128)(2,1)} %get-tuple-element.82), channel_id=1, source_target_pairs={{0,4},{1,5},{2,6},{3,7},{4,0},{5,1},{6,2},{7,3},{8,12},{9,13},{10,... | collective-permute-start | bytes 737288 | tf_op jit(solution)/shard_map/ppermute | solution.py:30
  235.5 53.0 %collective-permute-start.32 = (bf16[256,768]{1,0:T(8,128)(2,1)S(1)}, bf16[256,768]{1,0:T(8,128)(2,1)}, u32[]{:S(2)}, u32[]{:S(2)}) collective-permute-start(bf16[256,768]{1,0:T(8,128)(2,1)S(1)} %copy-done.11), channel_id=1, source_target_pairs={{4,0},{8,4},{12,8},{16,12},{20,16},{24,20},{28,24},{5,1},{9,5},{13... | collective-permute-start | bytes 1179656 | tf_op jit(solution)/shard_map/ppermute | solution.py:46
  236.8 51.7 %collective-permute-start.33 = (bf16[256,896]{1,0:T(8,128)(2,1)S(1)}, bf16[256,896]{1,0:T(8,128)(2,1)}, u32[]{:S(2)}, u32[]{:S(2)}) collective-permute-start(bf16[256,896]{1,0:T(8,128)(2,1)S(1)} %copy-done.13), channel_id=1, source_target_pairs={{4,0},{8,4},{12,8},{16,12},{20,16},{24,20},{28,24},{5,1},{9,5},{13... | collective-permute-start | bytes 1376264 | tf_op jit(solution)/shard_map/ppermute | solution.py:46
  239.0 21.9 %collective-permute-start.77 = (f32[12,129]{1,0:T(8,128)S(1)}, f32[12,129]{1,0:T(8,128)S(1)}, u32[]{:S(2)}, u32[]{:S(2)}) collective-permute-start(f32[12,129]{1,0:T(8,128)S(1)} %add.383), channel_id=1, source_target_pairs={{0,8},{1,9},{2,10},{3,11},{4,12},{5,13},{6,14},{7,15},{8,0},{9,1},... | collective-permute-start | bytes 18584 | tf_op jit(solution)/shard_map/ppermute | solution.py:30
  266.9 21.4 %collective-permute-start.36 = (bf16[2,80,768]{2,1,0:T(8,128)(2,1)S(1)}, bf16[2,80,768]{2,1,0:T(8,128)(2,1)S(1)}, u32[]{:S(2)}, u32[]{:S(2)}) collective-permute-start(bf16[2,80,768]{2,1,0:T(8,128)(2,1)S(1)} %fusion.24), channel_id=1, source_target_pairs={{16,0},{17,1},{18,2},{19,3},{20,4},{21,5},{22,6},{23,7},{24,8},{25... | collective-permute-start | bytes 737288 | tf_op jit(solution)/shard_map/ppermute | solution.py:119
  268.2 20.1 %collective-permute-start.37 = (bf16[2,80,768]{2,1,0:T(8,128)(2,1)S(1)}, bf16[2,80,768]{2,1,0:T(8,128)(2,1)S(1)}, u32[]{:S(2)}, u32[]{:S(2)}) collective-permute-start(bf16[2,80,768]{2,1,0:T(8,128)(2,1)S(1)} %fusion.24), channel_id=1, source_target_pairs={{24,0},{25,1},{26,2},{27,3},{28,4},{29,5},{30,6},{31,7}} | collective-permute-start | bytes 737288 | tf_op jit(solution)/shard_map/ppermute | solution.py:119
  274.7 71.9 %collective-permute-start.65 = (bf16[3072,384]{1,0:T(8,128)(2,1)}, bf16[3072,384]{1,0:T(8,128)(2,1)}, u32[]{:S(2)}, u32[]{:S(2)}) collective-permute-start(bf16[3072,384]{1,0:T(8,128)(2,1)} %get-tuple-element.98), channel_id=1, source_target_pairs={{0,1},{1,0},{2,3},{3,2},{4,5},{5,4},{6,7},{7,6},{8,9},{9,8},{10,11... | collective-permute-start | bytes 7077896 | tf_op jit(solution)/shard_map/ppermute | solution.py:30
  308.8 20.7 %collective-permute-start.47 = (bf16[768,896]{1,0:T(8,128)(2,1)S(1)}, bf16[768,896]{1,0:T(8,128)(2,1)S(1)}, u32[]{:S(2)}, u32[]{:S(2)}) collective-permute-start(bf16[768,896]{1,0:T(8,128)(2,1)S(1)} %pad_maximum_fusion.3), channel_id=1, source_target_pairs={{0,1},{1,0},{2,3},{3,2},{4,5},{5,4},{6,7},{7,6},{8,9},{9,8},{10,11... | collective-permute-start | bytes 4128776 | tf_op jit(solution)/shard_map/ppermute | solution.py:30
  328.9 35.3 %collective-permute-start.56 = (bf16[768,1920]{1,0:T(8,128)(2,1)}, bf16[768,1920]{1,0:T(8,128)(2,1)}, u32[]{:S(2)}, u32[]{:S(2)}) collective-permute-start(bf16[768,1920]{1,0:T(8,128)(2,1)} %get-tuple-element.96), channel_id=1, source_target_pairs={{0,1},{1,0},{2,3},{3,2},{4,5},{5,4},{6,7},{7,6},{8,9},{9,8},{10,11... | collective-permute-start | bytes 8847368 | tf_op jit(solution)/shard_map/ppermute | solution.py:30
  367.9 29.3 %collective-permute-start.59 = (bf16[2,2,48,1920]{3,2,1,0:T(8,128)(2,1)S(1)}, bf16[2,2,48,1920]{3,2,1,0:T(8,128)(2,1)S(1)}, u32[]{:S(2)}, u32[]{:S(2)}) collective-permute-start(bf16[2,2,48,1920]{3,2,1,0:T(8,128)(2,1)S(1)} %dynamic-slice_bitcast_fusion), channel_id=1, source_target_pairs={{0,4},{1,5},{2,6},{3,7},{4,0},{5,1},{6,2},{7,3},{8,12},{9,13},{10,... | collective-permute-start | bytes 2211848 | tf_op jit(solution)/shard_map/ppermute | solution.py:30
  378.3 20.7 %collective-permute-start.57 = (bf16[2,2,48,1920]{3,2,0,1:T(8,128)(2,1)S(1)}, bf16[2,2,48,1920]{3,2,0,1:T(8,128)(2,1)S(1)}, u32[]{:S(2)}, u32[]{:S(2)}) collective-permute-start(bf16[2,2,48,1920]{3,2,0,1:T(8,128)(2,1)S(1)} %bitcast.374), channel_id=1, source_target_pairs={{0,2},{1,3},{2,0},{3,1},{4,6},{5,7},{6,4},{7,5},{8,10},{9,11},{10,... | collective-permute-start | bytes 2211848 | tf_op jit(solution)/shard_map/ppermute | solution.py:30
  393.2 20.5 %collective-permute-start.70 = (bf16[192,384]{1,0:T(8,128)(2,1)S(1)}, bf16[192,384]{1,0:T(8,128)(2,1)S(1)}, u32[]{:S(2)}, u32[]{:S(2)}) collective-permute-start(bf16[192,384]{1,0:T(8,128)(2,1)S(1)} %get-tuple-element.177), channel_id=1, source_target_pairs={{0,8},{1,9},{2,10},{3,11},{4,12},{5,13},{6,14},{7,15},{8,16},{9,17... | collective-permute-start | bytes 442376 | tf_op jit(solution)/shard_map/ppermute | solution.py:42
  (115 other events, 1329.6 us)
where the time goes:
time: 436 us; the launch traced here: 428 us
  waiting for transfers between devices  150 us (34%)
  starting transfers between devices  125 us (29%)
  Pallas kernels  70.3 us (16%)
  local copies, waits for them, and re-layouts  50.9 us (12%)
  other arithmetic  29.7 us (7%)
    ppermute x49, waiting for transfers between devices, flip(): return lax.ppermute(a, BOTH, [(d, d ^ stride) for d in range(self.n)])  109 us
    ppermute x49, starting transfers between devices, flip(): return lax.ppermute(a, BOTH, [(d, d ^ stride) for d in range(self.n)])  61.3 us
    ppermute x21, starting transfers between devices, turn_z(): lax.ppermute(a, BOTH, [(d, (d + 8 * by) % self.n) for d in range(self.n)])  38.7 us
    ppermute x21, waiting for transfers between devices, turn_z(): lax.ppermute(a, BOTH, [(d, (d + 8 * by) % self.n) for d in range(self.n)])  24.6 us
    unnamed x145, local copies, waits for them, and re-layouts  18.9 us
    ppermute x3, waiting for transfers between devices, sum_before(): lax.ppermute(pair, BOTH, [(d, d - 8 * by) for d in range(8 * by, at.n)])  16.2 us
    pallas_call x1, Pallas kernels, on_device(): pl.pallas_call(middle_kernel, out_shape=(wide32, arr((n, width + 128), BF...  14.5 us
    pallas_call x1, Pallas kernels, on_device(): pl.pallas_call(forward_kernel, out_shape=(wide32, wide32, wide16, wide16,...  13.7 us
  transfers between devices with their start and end apart: 79, of which 30 were waited for; matrix products, arithmetic and copies ran while one was open for 14% of the time, Pallas kernels for 7%

commit v1 on v0

v1 whole, which is shorter than its diff:
```python
import math

import jax
import jax.numpy as jnp
from jax import lax
from jax.experimental import pallas as pl
from jax.experimental.pallas import tpu as pltpu
from jax.sharding import PartitionSpec as P

BOTH = ("seq", "rows")
EPS = 1e-06
BF = jnp.bfloat16
F32 = jnp.float32


class Place:
    def __init__(self):
        self.seq = lax.axis_size("seq")
        self.rows = lax.axis_size("rows")
        self.n = self.seq * self.rows
        self.fast = self.seq == 8 and self.rows == 4
        me = lax.axis_index(BOTH)
        self.c = me % 2
        self.y = (me // 2) % 2
        self.x = (me // 4) % 2
        self.z = me // 8
        self.s = lax.axis_index("seq")

    def flip(self, a, stride):
        return lax.ppermute(a, BOTH, [(d, d ^ stride) for d in range(self.n)])

    def swap_c(self, a):
        return self.flip(a, 1)

    def swap_y(self, a):
        return self.flip(a, 2)

    def swap_x(self, a):
        return self.flip(a, 4)

    def turn_z(self, a, by):
        return lax.ppermute(a, BOTH, [(d, (d + 8 * by) % self.n) for d in range(self.n)])

    def along(self, a, by):
        pairs = [(i, i + by) for i in range(self.seq) if 0 <= i + by < self.seq]
        return lax.ppermute(a, "seq", pairs)


def after(a, *others):
    return lax.optimization_barrier((a, others))[0]


def ordered(first, mine, other, axis):
    return jnp.where(
        first, jnp.stack([mine, other], axis=axis), jnp.stack([other, mine], axis=axis)
    )


class Gather:
    def __init__(self, at, name, left, right, small):
        self.at, self.name = at, name
        self.r, self.half = left.shape
        self.first = at.c == 0
        self.left, self.right, self.small = left, right, small
        self.done = ()

    def step_core(self, *wait):
        if not self.at.fast:
            return
        with jax.named_scope(self.name + "_core"):
            got = self.at.swap_c(after(jnp.where(self.first, self.right, self.left), *wait))
            kept = jnp.where(self.first, self.left, self.right)
            piece = ordered(self.first, kept, got, 0)
            mine = after(self.small, piece)
            small = ordered(self.first, mine, self.at.swap_c(mine), 0)
            self.half += self.small.shape[1]
            self.piece = jnp.concatenate([piece, small], axis=2).reshape(2 * self.r, self.half)
            self.done = (got,)

    def step_z(self, *wait):
        if not self.at.fast:
            return
        at = self.at
        with jax.named_scope(self.name + "_z"):
            piece = after(self.piece, *wait)
            turned = [at.turn_z(piece, by) for by in (1, 2, 3)]
            rel = jnp.stack([piece, turned[2], turned[1], turned[0]])
            by_z = lax.dynamic_slice_in_dim(jnp.concatenate([rel, rel]), (4 - at.z) % 4, 4)
            self.low, self.high = by_z[:2], by_z[2:]
            self.done = tuple(turned)

    def step_one(self, *wait):
        if not self.at.fast:
            return
        at = self.at
        with jax.named_scope(self.name + "_one"):
            low, high = after(self.low, *wait), after(self.high, *wait)
            got = at.swap_x(low), at.swap_y(high)
            self.low = ordered(at.x == 0, low, got[0], 1)
            self.high = ordered(at.y == 0, high, got[1], 1)
            self.done = got

    def step_two(self, *wait):
        if not self.at.fast:
            return
        at = self.at
        with jax.named_scope(self.name + "_two"):
            low, high = after(self.low, *wait), after(self.high, *wait)
            got = at.swap_y(low), at.swap_x(high)
            low = ordered(at.y == 0, low, got[0], 2)
            high = ordered(at.x == 0, high, got[1], 1)
            self.mine = jnp.concatenate([low, high]).reshape(at.n * self.r, self.half)
            self.done = got

    def step_last(self, *wait):
        at = self.at
        with jax.named_scope(self.name + "_last"):
            if not at.fast:
                left = lax.all_gather(jnp.concatenate([self.left, self.small], axis=1), BOTH, axis=0, tiled=True)
                right = lax.all_gather(jnp.concatenate([self.right, self.small], axis=1), BOTH, axis=0, tiled=True)
                return jnp.where(self.first, left, right), jnp.where(self.first, right, left)
            mine = after(self.mine, *wait)
            other = at.swap_c(mine)
            self.done = (other,)
            return mine, other


def half_at(a, index, axis):
    return lax.dynamic_index_in_dim(a, index, axis, keepdims=False)


def plus(kept, got):
    return (kept.astype(F32) + got.astype(F32)).astype(BF)


class Scatter:
    def __init__(self, at, name, keeps, sends):
        self.at, self.name, self.keeps, self.sends = at, name, keeps, sends
        self.total = keeps[0].shape[0]
        self.half = sum(k.shape[1] for k in keeps)
        self.r = self.total // at.n
        self.first = at.c == 0
        self.done = ()

    def step_core(self, *wait):
        if not self.at.fast:
            return
        at = self.at
        with jax.named_scope(self.name + "_core"):
            got = [at.swap_c(after(send, *wait)) for send in self.sends]
            mine = jnp.concatenate([plus(k, g) for k, g in zip(self.keeps, got)], axis=1)
            mine = mine.reshape(4, 2, 2, 2 * self.r, self.half)
            self.low, self.high = mine[:2], mine[2:]
            self.done = tuple(got)

    def step_one(self, *wait):
        if not self.at.fast:
            return
        at = self.at
        with jax.named_scope(self.name + "_one"):
            low, high = after(self.low, *wait), after(self.high, *wait)
            got = at.swap_y(half_at(low, 1 - at.y, 2)), at.swap_x(half_at(high, 1 - at.x, 1))
            self.low = plus(half_at(low, at.y, 2), got[0])
            self.high = plus(half_at(high, at.x, 1), got[1])
            self.done = got

    def step_two(self, *wait):
        if not self.at.fast:
            return
        at = self.at
        with jax.named_scope(self.name + "_two"):
            low, high = after(self.low, *wait), after(self.high, *wait)
            got = at.swap_x(half_at(low, 1 - at.x, 1)), at.swap_y(half_at(high, 1 - at.y, 1))
            low = plus(half_at(low, at.x, 1), got[0])
            high = plus(half_at(high, at.y, 1), got[1])
            self.by_z = jnp.concatenate([low, high])
            self.done = got

    def step_z(self, *wait):
        if not self.at.fast:
            return
        at = self.at
        with jax.named_scope(self.name + "_z"):
            by_z = after(self.by_z, *wait)
            got = [at.turn_z(half_at(by_z, (at.z + by) % 4, 0), by) for by in (1, 2, 3)]
            total = half_at(by_z, at.z, 0).astype(F32) + got[0].astype(F32) + got[1].astype(F32) + got[2].astype(F32)
            self.piece = total.reshape(2, self.r, self.half)
            self.done = tuple(got)

    def step_last(self, *wait):
        at = self.at
        with jax.named_scope(self.name + "_last"):
            if not at.fast:
                keep, send = jnp.concatenate(self.keeps, axis=1), jnp.concatenate(self.sends, axis=1)
                left = jnp.where(self.first, keep, send).astype(F32)
                right = jnp.where(self.first, send, keep).astype(F32)
                return (
                    lax.psum_scatter(left, BOTH, scatter_dimension=0, tiled=True),
                    lax.psum_scatter(right, BOTH, scatter_dimension=0, tiled=True),
                )
            piece = after(self.piece, *wait)
            stays = half_at(piece, at.c, 0)
            got = at.swap_c(half_at(piece, 1 - at.c, 0))
            self.done = (got,)
            return jnp.where(self.first, stays, got), jnp.where(self.first, got, stays)


class Before:
    def __init__(self, at, name, a, reverse):
        self.at, self.name, self.a, self.reverse = at, name, a, reverse
        self.fast = at.fast and a.shape[0] == 2
        self.done = ()

    def step_beside(self):
        if self.fast:
            at = self.at
            with jax.named_scope(self.name + "_beside"):
                self.got = at.swap_x(half_at(self.a, 1 - at.x, 0))
                self.own = half_at(self.a, at.x, 0)
                self.pair = plus(self.own, self.got)
                self.done = (self.got,)

    def step_z(self, *wait):
        if self.fast:
            at = self.at
            with jax.named_scope(self.name + "_z"):
                pair = after(self.pair, *wait)
                got = []
                for by in (1, 2, 3):
                    if self.reverse:
                        pairs = [(d, d - 8 * by) for d in range(8 * by, at.n)]
                    else:
                        pairs = [(d, d + 8 * by) for d in range(at.n - 8 * by)]
                    got.append(lax.ppermute(pair, BOTH, pairs))
                self.done = tuple(got)

    def step_last(self, *wait):
        at, a, reverse = self.at, self.a, self.reverse
        with jax.named_scope(self.name + "_last"):
            if not self.fast:
                everything = lax.all_gather(a, "seq").astype(F32)
                index = jnp.arange(at.seq).reshape((-1,) + (1,) * a.ndim)
                reached = index > at.s if reverse else index < at.s
                return jnp.sum(jnp.where(reached, everything, 0.0), axis=0).astype(BF)
            inner = (at.x == 0) if reverse else (at.x == 1)
            got = [after(g, *wait).astype(F32) for g in self.done]
            self.total = got[0] + got[1] + got[2]
            mine = (self.total + jnp.where(inner, self.got.astype(F32), 0.0)).astype(BF)
            send = (self.total + jnp.where(inner, 0.0, self.own.astype(F32))).astype(BF)
            return ordered(at.x == 0, mine, at.swap_x(send), 0)


class Everywhere:
    def __init__(self, at, a):
        self.at, self.a, self.done = at, a, ()

    def step(self, stride, *wait):
        if self.at.fast:
            with jax.named_scope("everywhere"):
                got = self.at.flip(after(self.a, *wait), stride)
                self.a = self.a + got
                self.done = (got,)

    def step_z(self, *wait):
        at = self.at
        with jax.named_scope("everywhere"):
            if not at.fast:
                return lax.psum(self.a, BOTH)
            a = after(self.a, *wait)
            rel = jnp.stack([a] + [at.turn_z(a, by) for by in (3, 2, 1)])
            by_z = lax.dynamic_slice_in_dim(jnp.concatenate([rel, rel]), (4 - at.z) % 4, 4)
            return (by_z[0] + by_z[1]) + (by_z[2] + by_z[3])


VMEM = pltpu.VMEM
SCALAR = pl.BlockSpec(memory_space=pltpu.SMEM)
WHOLE = pl.BlockSpec(memory_space=VMEM)


def params(mib):
    return pltpu.CompilerParams(vmem_limit_bytes=60 * 2**20)


def cost(micros):
    return pl.CostEstimate(flops=int(micros * 1e9), bytes_accessed=int(micros * 1e6), transcendentals=0)


def tdot(a, b):
    return lax.dot_general(a, b, (((0,), (0,)), ((), ())), preferred_element_type=F32)


def dot_t(a, b):
    return lax.dot_general(a, b, (((1,), (1,)), ((), ())), preferred_element_type=F32)


def dot(a, b):
    return jnp.dot(a, b, preferred_element_type=F32)


def parts(a):
    high = a.astype(BF)
    return high, (a - high.astype(F32)).astype(BF)


def left_lanes(shape):
    return lax.broadcasted_iota(jnp.int32, shape, len(shape) - 1) % 128 < 64


def two_heads(a):
    first = left_lanes(a.shape)
    wide = a.astype(F32)
    return jnp.concatenate(
        [jnp.where(first, wide, 0.0), jnp.where(first, 0.0, wide)], axis=0
    ).astype(BF)


def fold(a):
    half = a.shape[0] // 2
    return jnp.where(left_lanes((half, a.shape[1])), a[:half], a[half:])


def head_ones():
    row = lax.broadcasted_iota(jnp.int32, (128, 128), 0) // 64
    col = lax.broadcasted_iota(jnp.int32, (128, 128), 1) // 64
    return jnp.where(row == col, 1.0, 0.0).astype(BF)


def head_sums(a, ones):
    high, low = parts(a)
    return dot(high, ones) + dot(low, ones)


def features(s, g_high, g_low):
    high, low = parts(jnp.concatenate([s, s * s], axis=1))
    return jnp.exp(dot(high, g_high) + dot(high, g_low) + dot(low, g_high)) * 0.125


def features_back(t, s, g_high, g_low, ones, scale):
    high, low = parts(t)
    f_high, f_low = g_high[:128], g_low[:128]
    back = dot_t(high, f_high) + dot_t(high, f_low) + dot_t(low, f_high)
    return ((back - s * (dot(high, ones) + dot(low, ones))) * scale).astype(BF)


def lanes(p):
    return slice(p * 128, (p + 1) * 128)


def key_kernel(c_ref, tok, mine, other, gh, gl, s_out, phi_out, feat_out, v_out, state_out, vec_out):
    first = c_ref[0] == 0
    pairs, block = gh.shape[0], 128
    hw = pairs * 64
    eye = jnp.where(
        lax.broadcasted_iota(jnp.int32, (128, 128), 0) == lax.broadcasted_iota(jnp.int32, (128, 128), 1), 1.0, 0.0
    ).astype(BF)
    vecs = dot_t(eye, mine[:, 3 * hw :])[:16]
    vec_out[...] = vecs
    a = dot(tok[...], mine[:, hw : 3 * hw])
    b = dot(tok[...], other[:, hw : 3 * hw])
    left, right = jnp.where(first, a, b), jnp.where(first, b, a)
    scale = 64 ** (-0.25)
    for p in range(pairs):
        half, at = (left, p * 128) if p < pairs // 2 else (right, p * 128 - hw)
        s = (half[:, at : at + 128] + vecs[1:2, lanes(p)]) * scale
        v = (half[:, hw + at : hw + at + 128] + vecs[2:3, lanes(p)]).astype(BF)
        phi = features(s, gh[p], gl[p])
        k = phi.astype(BF)
        s_out[:, lanes(p)] = s
        phi_out[:, lanes(p)] = phi
        feat_out[:, lanes(p)] = k
        v_out[:, lanes(p)] = v
        for r in range(tok.shape[0] // block):
            rows = slice(r * block, (r + 1) * block)
            state_out[r, :64, lanes(p)] = fold(tdot(k[rows], v[rows])).astype(BF)
            total = jnp.sum(k[rows].astype(F32), axis=0, keepdims=True)
            state_out[r, 64:, lanes(p)] = jnp.broadcast_to(total, (16, 128)).astype(BF)


def query_kernel(c_ref, tok, mine, other, vec, gh, gl, s_out, phi_out, feat_out):
    first = c_ref[0] == 0
    pairs = gh.shape[0]
    hw = pairs * 64
    a, b = dot(tok[...], mine[:, :hw]), dot(tok[...], other[:, :hw])
    left, right = jnp.where(first, a, b), jnp.where(first, b, a)
    for p in range(pairs):
        half, at = (left, p * 128) if p < pairs // 2 else (right, p * 128 - hw)
        s = (half[:, at : at + 128] + vec[0:1, lanes(p)]) * 64 ** (-0.25)
        phi = features(s, gh[p], gl[p])
        s_out[:, lanes(p)] = s
        phi_out[:, lanes(p)] = phi
        feat_out[:, lanes(p)] = phi.astype(BF)


def halo_kernel(c_ref, halo, mine, other, vec, gh, gl, hk_out, hv_out):
    first, inner = c_ref[0] == 0, c_ref[1] > 0
    pairs = gh.shape[0]
    hw = pairs * 64
    a, b = dot(halo[...], mine[:, hw : 3 * hw]), dot(halo[...], other[:, hw : 3 * hw])
    left, right = jnp.where(first, a, b), jnp.where(first, b, a)
    for p in range(pairs):
        half, at = (left, p * 128) if p < pairs // 2 else (right, p * 128 - hw)
        s = (half[:, at : at + 128] + vec[1:2, lanes(p)]) * 64 ** (-0.25)
        v = half[:, hw + at : hw + at + 128] + vec[2:3, lanes(p)]
        hk_out[:, lanes(p)] = jnp.where(inner, features(s, gh[p], gl[p]), 0.0).astype(BF)
        hv_out[:, lanes(p)] = jnp.where(inner, v, 0.0).astype(BF)


def window_weights(base):
    turned = pltpu.roll(jnp.broadcast_to(base, (128, 256)), 0, 1, stride=1, stride_axis=0)
    row = lax.broadcasted_iota(jnp.int32, (128, 256), 0)
    col = lax.broadcasted_iota(jnp.int32, (128, 256), 1)
    return jnp.where(col > row + 128, 0.0, turned - jnp.where(col < 128, base[:, 255:256], 0.0))


def pair_at(step, c, pairs):
    return (step + (pairs // 2) * (1 - c)) % pairs


def block_diagonal(packed):
    return two_heads(packed)


def attention_kernel(q, k, v, hk, hv, table, state, far, context_out, turned_out, ratio_out, denom_out):
    ones = head_ones()
    wmat = jnp.concatenate([window_weights(table[0, 0:1]), window_weights(table[0, 1:2])], axis=0)
    far_row = far[0:1]
    for r in range(q.shape[0] // 128):
        rows = slice(r * 128, (r + 1) * 128)
        qr = q[rows]
        kw = jnp.concatenate([hk[rows], k[rows]], axis=0)
        vw = jnp.concatenate([hv[rows], v[rows]], axis=0)
        weighted = dot_t(two_heads(qr), kw) * wmat
        numer = fold(dot(weighted.astype(BF), vw))
        near = jnp.sum(weighted, axis=1, keepdims=True)
        near = fold(jnp.broadcast_to(near, (256, 128)))
        bd = block_diagonal(state[r, :64])
        total = state[r, 64:80].astype(F32)[0:1]
        numer = numer + far_row * dot(qr, bd)
        denom = near + far_row * head_sums(qr.astype(F32) * total, ones)
        ratio = numer / denom
        context_out[rows] = ratio.astype(BF)
        turned_out[:, rows] = ratio.T.astype(BF)
        ratio_out[rows] = ratio
        denom_out[rows] = denom


def normed(x):
    centred = x - jnp.mean(x, axis=-1, keepdims=True)
    rstd = lax.rsqrt(jnp.mean(centred * centred, axis=-1, keepdims=True) + EPS)
    return centred * rstd, rstd


def norm_back(dy, xhat, rstd, gain):
    d = dy * gain
    return rstd * (
        d - jnp.mean(d, axis=-1, keepdims=True) - xhat * jnp.mean(d * xhat, axis=-1, keepdims=True)
    )


def col_sums(a):
    return jnp.sum(a, axis=0, keepdims=True)


def forward_kernel(
    context, tok, wu, wo, wd, cot, vec, bu,
    out, dlower_out, dlow_out, hlow_out, xhat_out, rstd_out, gp_out, grad_out, sums_out,
):
    attn = jnp.concatenate([dot(context[...], wo[i]) for i in range(wo.shape[0])], axis=1)
    xhat, rstd = normed(tok[...].astype(F32) + attn + vec[3:4])
    hidden = xhat * vec[4:5] + vec[5:6]
    xhat_out[...] = xhat
    rstd_out[...] = jnp.broadcast_to(rstd, rstd_out.shape)
    h_low = hidden.astype(BF)
    hlow_out[...] = h_low
    step = wu.shape[2]
    lower = hidden + vec[6:7]
    actives = []
    for i in range(wu.shape[0]):
        cols = slice(i * step, (i + 1) * step)
        upper = dot(h_low, wu[i]) + bu[:, cols]
        cdf = 0.5 * (1.0 + lax.erf(upper * 2.0 ** (-0.5)))
        pdf = jnp.exp(-0.5 * upper * upper) * (2.0 * math.pi) ** (-0.5)
        gp_out[:, cols] = (cdf + upper * pdf).astype(BF)
        actives.append((upper * cdf).astype(BF))
        lower = lower + dot(actives[-1], wd[cols])
    xhat2, rstd2 = normed(lower)
    gain2 = vec[7:8]
    out[...] = xhat2 * gain2 + vec[8:9]
    dy = cot[...].astype(F32)
    d_lower = norm_back(dy, xhat2, rstd2, gain2)
    dlower_out[...] = d_lower
    d_low = d_lower.astype(BF)
    dlow_out[...] = d_low
    sums_out[0:1] = col_sums(d_low.astype(F32))
    sums_out[1:2] = col_sums(dy * xhat2)
    sums_out[2:3] = col_sums(dy)
    for i in range(wu.shape[0]):
        grad_out[i * step : (i + 1) * step, : d_low.shape[1]] = tdot(actives[i], d_low).astype(BF)


def upper_back_kernel(dlow, hlow, gp, wd, du_out, grad_out, sums_out):
    d_low, h_low = dlow[...], hlow[...]
    step = grad_out.shape[2]
    for i in range(grad_out.shape[0]):
        cols = slice(i * step, (i + 1) * step)
        d_upper = (dot_t(d_low, wd[cols]) * gp[:, cols].astype(F32)).astype(BF)
        du_out[:, cols] = d_upper
        sums_out[:, cols] = jnp.broadcast_to(col_sums(d_upper.astype(F32)), (8, step))
        grad_out[i] = tdot(h_low, d_upper).astype(BF)


def middle_kernel(
    dlower, du, xhat, rstd, wu, wo, vec, ratio, denom, q, state, far,
    dresid_out, dattn_out, dn_out, later_out, sums_out, near_out,
):
    hw = dlower.shape[1] // 2
    d_hidden = dlower[...]
    step = wu.shape[2]
    for i in range(wu.shape[0]):
        d_hidden = d_hidden + dot_t(du[:, i * step : (i + 1) * step], wu[i])
    xh = xhat[...]
    d_resid = norm_back(d_hidden, xh, rstd[:, 0:1], vec[4:5])
    dresid_out[...] = d_resid
    d_attn = d_resid.astype(BF)
    dattn_out[...] = d_attn
    sums_out[0:1] = col_sums(d_attn.astype(F32))
    sums_out[1:2] = col_sums(d_hidden * xh)
    sums_out[2:3] = col_sums(d_hidden)
    step = wo.shape[2]
    d_context = sum(dot_t(d_resid[:, i * step : (i + 1) * step].astype(BF), wo[i]) for i in range(wo.shape[0]))
    ones = head_ones()
    width = 2 * hw
    pick = jnp.where(
        lax.broadcasted_iota(jnp.int32, (width, 128), 0) == 64 * lax.broadcasted_iota(jnp.int32, (width, 128), 1), 1.0, 0.0
    ).astype(BF)
    all_denoms = []
    for p in range(width // 128):
        dc = d_context[:, lanes(p)]
        inverse = 1.0 / denom[:, lanes(p)]
        dn = (dc * inverse).astype(BF)
        dd = (-head_sums(dc * ratio[:, lanes(p)], ones) * inverse).astype(BF)
        dn_out[:, lanes(p)] = dn
        all_denoms.append(dd)
        near = jnp.zeros((1, 128), F32)
        for r in range(dlower.shape[0] // 128):
            rows = slice(r * 128, (r + 1) * 128)
            qr = q[rows, lanes(p)]
            packed = fold(tdot(qr, dn[rows]))
            total = col_sums(qr.astype(F32) * dd[rows].astype(F32))
            far_row = far[0:1, lanes(p)]
            later_out[r, :64, lanes(p)] = (far_row * packed).astype(BF)
            later_out[r, 64:, lanes(p)] = jnp.broadcast_to(far_row * total, (16, 128)).astype(BF)
            held = state[r, :, lanes(p)].astype(F32)
            near = near + col_sums(held[:64] * packed) + held[64:65] * total
        near_out[:, lanes(p)] = jnp.broadcast_to(near, (8, 128))
    dn_out[:, width:] = dot(jnp.concatenate(all_denoms, axis=1), pick).astype(BF)


def spread(dn, p):
    lane = lax.broadcasted_iota(jnp.int32, dn.shape, 1)
    wide = dn.astype(F32)
    return [jnp.sum(jnp.where(lane == 2 * p + h, wide, 0.0), axis=1, keepdims=True) for h in (0, 1)]


def query_back_kernel(
    c_ref, tok, context, dattn, q, k, v, hk, hv, dn, dd, table, state, far, phi, s, gh, gl, near,
    dq_out, keep_out, send_out, pos_out, sums_out,
):
    steps = pl.num_programs(0)
    p = pair_at(pl.program_id(0), c_ref[0], steps)
    ones = head_ones()
    wmat = jnp.concatenate([window_weights(table[0, 0:1]), window_weights(table[0, 1:2])], axis=0)
    far_row = far[0:1]
    first = left_lanes((128, 128))
    pieces = jnp.zeros((256, 256), F32)
    grads = []
    for r in range(q.shape[0] // 128):
        rows = slice(r * 128, (r + 1) * 128)
        kw = jnp.concatenate([hk[rows], k[rows]], axis=0)
        vw = jnp.concatenate([hv[rows], v[rows]], axis=0)
        scores = dot_t(two_heads(q[rows]), kw)
        d0, d1 = spread(dd[rows], p)
        dnr = dn[rows]
        dw = dot_t(two_heads(dnr), vw) + jnp.concatenate([d0, d1], axis=0)
        pieces = pieces + dw * scores
        ds = (dw * wmat).astype(BF)
        bd = block_diagonal(state[r, :64])
        total = state[r, 64:80].astype(F32)[0:1]
        dq = fold(dot(ds, kw)) + far_row * (dot_t(dnr, bd) + jnp.where(first, d0, d1) * total)
        grads.append(
            features_back(dq * phi[rows], s[rows], gh[0], gl[0], ones, 64 ** (-0.25))
        )
    dq = jnp.concatenate(grads, axis=0)
    dq_out[...] = dq
    sums_out[...] = jnp.broadcast_to(col_sums(dq.astype(F32)), sums_out.shape)
    grad = jnp.concatenate([dot(tok[...], dq), dot(context[...], dattn[...])], axis=1).astype(BF)
    place_half(grad, keep_out, send_out)
    row = lax.broadcasted_iota(jnp.int32, (256, 256), 0)
    col = lax.broadcasted_iota(jnp.int32, (256, 256), 1)
    mirror = jnp.where(row + col == 255, 1.0, 0.0).astype(BF)
    high, low = parts(jnp.where(col <= row % 128 + 128, pieces, 0.0))
    mirrored = dot(high, mirror) + dot(low, mirror)
    lane = lax.broadcasted_iota(jnp.int32, (1, 256), 1)
    for h in (0, 1):
        rows = slice(h * 128, (h + 1) * 128)
        by_distance = col_sums(pltpu.roll(mirrored[rows], 129, 1, stride=1, stride_axis=0))
        plain = col_sums(pieces[rows])
        apart = jnp.where(lane >= 128, by_distance, 0.0) - jnp.where(lane < 128, plain, 0.0)
        state_part = jnp.where(lane[:, :128] // 64 == h, near[0:1], 0.0)
        far_sum = jnp.sum(apart, axis=1, keepdims=True) + jnp.sum(state_part, axis=1, keepdims=True)
        pos_out[0, h : h + 1] = jnp.where(lane < 128, by_distance, far_sum)


def place_half(grad, keep_out, send_out):
    early = pl.program_id(0) < pl.num_programs(0) // 2

    @pl.when(early)
    def _():
        send_out[...] = grad

    @pl.when(jnp.logical_not(early))
    def _():
        keep_out[...] = grad


def key_back_kernel(
    c_ref, tok, q, k, v, dn, dd, qn, dnn, ddn, table, later, phi, s, gh, gl, rows_in,
    dk_out, dv_out, keep_out, send_out, small_out,
):
    p = pair_at(pl.program_id(0), c_ref[0], pl.num_programs(0))
    ones = head_ones()
    first, second = window_weights(table[0, 0:1]), window_weights(table[0, 1:2])
    tables = jnp.concatenate([first[:, 128:], second[:, 128:], first[:, :128], second[:, :128]], axis=0)
    dks, dvs = [], []
    for r in range(q.shape[0] // 128):
        rows = slice(r * 128, (r + 1) * 128)
        kr, vr = k[rows], v[rows]
        q4 = jnp.concatenate([two_heads(q[rows]), two_heads(qn[rows])], axis=0)
        dn4 = jnp.concatenate([two_heads(dn[rows]), two_heads(dnn[rows])], axis=0)
        dd4 = jnp.concatenate(spread(dd[rows], p) + spread(ddn[rows], p), axis=0)
        w = (dot_t(q4, kr) * tables).astype(BF)
        ds = ((dot_t(dn4, vr) + dd4) * tables).astype(BF)
        bd = block_diagonal(later[r, :64])
        total = later[r, 64:80].astype(F32)[0:1]
        dk = tdot(ds, q4) + dot_t(vr, bd) + total
        dvs.append((tdot(w, dn4) + dot(kr, bd)).astype(BF))
        dks.append(features_back(dk * phi[rows], s[rows], gh[0], gl[0], ones, 64 ** (-0.25)))
    dk, dv = jnp.concatenate(dks, axis=0), jnp.concatenate(dvs, axis=0)
    dk_out[...] = dk
    dv_out[...] = dv
    place_half(jnp.concatenate([dot(tok[...], dk), dot(tok[...], dv)], axis=1).astype(BF), keep_out, send_out)
    row = lax.broadcasted_iota(jnp.int32, (16, 128), 0)
    lane = lax.broadcasted_iota(jnp.int32, (16, 128), 1)
    late = jnp.where(row == 1, col_sums(dk.astype(F32)), 0.0) + jnp.where(row == 2, col_sums(dv.astype(F32)), 0.0)
    small_out[...] = tdot((rows_in[...] + late).astype(BF), jnp.where(row == lane, 1.0, 0.0).astype(BF)).astype(BF)


def tokens_kernel(c_ref, dresid, dq, dk, dv, mine, other, out):
    first = c_ref[0] == 0
    hw = dq.shape[1] // 2
    total = dresid[...]
    for i, d in enumerate((dq, dk, dv)):
        wide = d[...].astype(F32)
        a = jnp.where(first, wide[:, :hw], wide[:, hw:]).astype(BF)
        b = jnp.where(first, wide[:, hw:], wide[:, :hw]).astype(BF)
        cols = slice(i * hw, (i + 1) * hw)
        total = total + dot_t(a, mine[:, cols]) + dot_t(b, other[:, cols])
    out[...] = total


def feature_blocks(matrix):
    heads, size, feats = matrix.shape
    zero = jnp.zeros((heads // 2, size, feats), F32)
    even, odd = matrix[0::2], matrix[1::2]
    half = jnp.full(zero.shape, -0.5, F32)
    blocks = jnp.concatenate(
        [
            jnp.concatenate([even, zero], axis=2),
            jnp.concatenate([zero, odd], axis=2),
            jnp.concatenate([half, zero], axis=2),
            jnp.concatenate([zero, half], axis=2),
        ],
        axis=1,
    )
    high = lax.reduce_precision(blocks, 8, 7)
    return high.astype(BF), (blocks - high).astype(BF)


def on_device(
    tokens,
    query_weight,
    query_bias,
    key_weight,
    key_bias,
    value_weight,
    value_bias,
    output_weight,
    output_bias,
    first_gain,
    first_shift,
    up_weight,
    up_bias,
    down_weight,
    down_bias,
    second_gain,
    second_shift,
    position_bias,
    feature_matrix,
    cotangent,
):
    at = Place()
    rows, block, width = tokens.shape
    heads, size, feats = feature_matrix.shape
    window = position_bias.shape[1] - 1
    pairs = heads // 2
    n = rows * block
    hw = width // 2
    ff = up_weight.shape[1]
    hf = ff // 2
    own = query_weight.shape[0]
    up_own = up_bias.shape[0] // own
    tok = tokens.reshape(n, width)
    cot = cotangent.reshape(n, width)
    flags = jnp.stack([at.c, at.s]).astype(jnp.int32)

    def arr(shape, kind):
        return jax.ShapeDtypeStruct(shape, kind)

    halo_tok = at.along(tok, 1)
    tok_t = tok.T

    vectors = (
        query_bias, key_bias, value_bias, output_bias, first_gain, first_shift,
        down_bias, second_gain, second_shift,
    )
    count = len(vectors)
    small = jnp.concatenate(vectors + (up_bias,)).reshape(count + up_own, own).T
    small = jnp.pad(small, ((0, 0), (0, 128 - small.shape[1])))
    slices = down_weight.shape[0] // own
    step, wo_step = ff // slices, width // slices

    def stacked(a):
        return jnp.concatenate(jnp.split(a, slices, axis=1), axis=0)

    rest = lax.all_gather(
        jnp.concatenate([down_weight, stacked(up_weight), stacked(output_weight)], axis=1), BOTH, axis=0, tiled=True
    )
    g1 = Gather(
        at,
        "qkv",
        jnp.concatenate([query_weight[:, :hw], key_weight[:, :hw], value_weight[:, :hw]], axis=1),
        jnp.concatenate([query_weight[:, hw:], key_weight[:, hw:], value_weight[:, hw:]], axis=1),
        small,
    )
    exp_bias = jnp.exp(position_bias)
    table = jnp.concatenate(
        [exp_bias[:, ::-1], jnp.broadcast_to(exp_bias[:, window:], (heads, block - 1))], axis=1
    ).reshape(pairs, 2, window + block)
    table = jnp.pad(table, ((0, 0), (0, 6), (0, 0)))
    far = jnp.broadcast_to(jnp.repeat(exp_bias[:, window], size)[None], (8, width))
    gh, gl = feature_blocks(feature_matrix)

    g1.step_core()
    g1.step_z()
    g1.step_one()
    g1.step_two()
    m1, o1 = g1.step_last(table, far, gh, gl, tok_t)

    wide32, wide16 = arr((n, width), F32), arr((n, width), BF)
    sums = arr((rows, 80, width), BF)
    sk, k_phi, k, v, local, vec = pl.pallas_call(
        key_kernel,
        out_shape=(wide32, wide32, wide16, wide16, sums, arr((16, width), F32)),
        in_specs=[SCALAR] + [WHOLE] * 5,
        out_specs=(WHOLE,) * 6,
        compiler_params=params(48),
        cost_estimate=cost(5),
        name="keys",
    )(flags, tok, m1, o1, gh, gl)
    scan = Before(at, "before", local, False)
    scan.step_beside()
    sq, q_phi, q = pl.pallas_call(
        query_kernel,
        out_shape=(wide32, wide32, wide16),
        in_specs=[SCALAR] + [WHOLE] * 6,
        out_specs=(WHOLE,) * 3,
        compiler_params=params(48),
        cost_estimate=cost(3),
        name="queries",
    )(flags, tok, m1, o1, vec, gh, gl)
    scan.step_z(q)
    hk, hv = pl.pallas_call(
        halo_kernel,
        out_shape=(wide16, wide16),
        in_specs=[SCALAR] + [WHOLE] * 6,
        out_specs=(WHOLE,) * 2,
        compiler_params=params(48),
        cost_estimate=cost(2),
        name="halo",
    )(flags, after(halo_tok, *scan.done), m1, o1, vec, gh, gl)
    before = scan.step_last(hk)
    b_u = m1[:, 3 * hw + count : 3 * hw + count + up_own].reshape(at.n, own, up_own)
    b_u = jnp.swapaxes(after(b_u, hk), 1, 2).reshape(1, ff).astype(F32)
    q_next = at.along(q, -1)

    def columns(height=n):
        return pl.BlockSpec((height, 128), lambda p, *_: (0, p))

    table_spec = pl.BlockSpec((1, 8, window + block), lambda p, *_: (p, 0, 0))
    sums_spec = pl.BlockSpec((rows, 80, 128), lambda p, *_: (0, 0, p))
    g_spec = pl.BlockSpec((1, 256, 128), lambda p, *_: (p, 0, 0))
    tok_spec = pl.BlockSpec((width, n), lambda p, *_: (0, 0))
    dd_spec = pl.BlockSpec((n, 128), lambda p, *_: (0, pairs))
    context, context_t, ratio, denom = pl.pallas_call(
        attention_kernel,
        grid=(pairs,),
        out_shape=(wide16, arr((width, n), BF), wide32, wide32),
        in_specs=[columns()] * 5 + [table_spec, sums_spec, columns(8)],
        out_specs=(columns(), pl.BlockSpec((128, n), lambda p, *_: (p, 0)), columns(), columns()),
        compiler_params=params(32),
        cost_estimate=cost(5),
        name="attention",
    )(q, k, v, hk, hv, table, before, far)

    split = rest.reshape(at.n, slices, own, rest.shape[1])
    wu = jnp.swapaxes(split[..., width : width + step], 0, 1).reshape(slices, width, step)
    wo = jnp.swapaxes(split[..., width + step :], 0, 1).reshape(slices, width, wo_step)
    wd_spec = pl.BlockSpec((ff, width), lambda i: (0, 0), pipeline_mode=pl.Buffered(1))
    out, d_lower, d_low, h_low, xhat, rstd, gp, g_down, sums3 = pl.pallas_call(
        forward_kernel,
        grid=(1,),
        out_shape=(
            wide32, wide32, wide16, wide16, wide32, arr((n, 128), F32), arr((n, ff), BF),
            arr((ff, width + step), BF), arr((8, width), F32),
        ),
        in_specs=[WHOLE] * 4 + [wd_spec] + [WHOLE] * 3,
        out_specs=(WHOLE,) * 9,
        compiler_params=params(56),
        cost_estimate=cost(13),
        name="forward",
    )(context, tok, wu, wo, rest, cot, vec, b_u)
    du, g_up, du_sums = pl.pallas_call(
        upper_back_kernel,
        grid=(1,),
        out_shape=(arr((n, ff), BF), arr((slices, width, step), BF), arr((8, ff), F32)),
        in_specs=[WHOLE] * 3 + [wd_spec],
        out_specs=(WHOLE,) * 3,
        compiler_params=params(48),
        cost_estimate=cost(7),
        name="upper_back",
    )(d_low, h_low, gp, rest)
    g_up = jnp.swapaxes(g_up.reshape(slices, at.n, own, step), 0, 1).reshape(ff, step)
    g_rest = lax.dynamic_update_slice(g_down, g_up, (0, width))
    s_rest = lax.psum_scatter(g_rest, BOTH, scatter_dimension=0, tiled=True).astype(F32)
    s_d = s_rest[:, :width]
    s_u = jnp.concatenate(jnp.split(s_rest[:, width:], slices, axis=0), axis=1)
    d_resid, d_attn, dn, local, sums2, near = pl.pallas_call(
        middle_kernel,
        out_shape=(wide32, wide16, arr((n, width + 128), BF), sums, arr((8, width), F32), arr((8, width), F32)),
        in_specs=[WHOLE] * 12,
        out_specs=(WHOLE,) * 6,
        compiler_params=params(48),
        cost_estimate=cost(7),
        name="middle",
    )(after(d_lower, g_rest), du, xhat, rstd, wu, wo, vec, ratio, denom, q, before, far)
    scan = Before(at, "later", local, True)
    scan.step_beside()
    dn_next = at.along(dn, -1)

    def turned(p, c):
        return pair_at(p, c[0], pairs)

    cols = pl.BlockSpec((n, 128), lambda p, c: (0, turned(p, c)))
    cols8 = pl.BlockSpec((8, 128), lambda p, c: (0, turned(p, c)))
    by_pair = pl.BlockSpec((1, 8, window + block), lambda p, c: (turned(p, c), 0, 0))
    sums_by_pair = pl.BlockSpec((rows, 80, 128), lambda p, c: (0, 0, turned(p, c)))
    g_by_pair = pl.BlockSpec((1, 256, 128), lambda p, c: (turned(p, c), 0, 0))
    kept = pl.BlockSpec((width, 256), lambda p, c: (0, jnp.maximum(p - pairs // 2, 0)))
    sent = pl.BlockSpec((width, 256), lambda p, c: (0, jnp.minimum(p, pairs // 2 - 1)))
    half = arr((width, 2 * hw), BF)
    dq, keep1, send1, pos, sums_q = pl.pallas_call(
        query_back_kernel,
        grid_spec=pltpu.PrefetchScalarGridSpec(
            num_scalar_prefetch=1,
            grid=(pairs,),
            in_specs=[tok_spec] * 2 + [cols] * 7 + [dd_spec, by_pair, sums_by_pair, cols8]
            + [cols] * 2 + [g_by_pair] * 2 + [cols8],
            out_specs=(cols, kept, sent, by_pair, cols8),
        ),
        out_shape=(wide16, half, half, arr((pairs, 8, 256), F32), arr((8, width), F32)),
        compiler_params=params(32),
        cost_estimate=cost(11),
        name="query_back",
    )(flags, after(tok_t, *scan.done), context_t, d_attn, q, k, v, hk, hv, dn, dn, table, before, far, q_phi, sq, gh, gl, near)
    scan.step_z()
    later = scan.step_last(dq, q_next, dn_next)
    everywhere = Everywhere(at, exp_bias * pos[:, :2, : window + 1].reshape(heads, window + 1))
    everywhere.step(1)
    du = du_sums[0].reshape(at.n, up_own, own)
    du = jnp.swapaxes(du, 0, 1).reshape(up_own, width)
    nil = jnp.zeros((2, width), F32)
    early = jnp.concatenate([sums_q[:1], nil, sums2[:3], sums3[:3], du], axis=0)
    early = jnp.pad(early, ((0, 16 - early.shape[0]), (0, 0)))
    dk, dv, keep0, send0, small = pl.pallas_call(
        key_back_kernel,
        grid_spec=pltpu.PrefetchScalarGridSpec(
            num_scalar_prefetch=1,
            grid=(pairs,),
            in_specs=[tok_spec] + [cols] * 4 + [dd_spec] + [cols] * 2
            + [dd_spec, by_pair, sums_by_pair] + [cols] * 2 + [g_by_pair] * 2
            + [pl.BlockSpec((16, 128), lambda p, c: (0, turned(p, c)))],
            out_specs=(cols, cols, kept, sent, pl.BlockSpec((128, 128), lambda p, c: (turned(p, c), 0))),
        ),
        out_shape=(wide16, wide16, half, half, arr((width, 128), BF)),
        compiler_params=params(32),
        cost_estimate=cost(12),
        name="key_back",
    )(flags, after(tok_t, *everywhere.done), q, k, v, dn, dn, q_next, dn_next, dn_next, table, later, k_phi, sk, gh, gl, early)

    r0 = Scatter(at, "d_qkv", (keep1, keep0, small), (send1, send0, small))
    r0.step_core()
    everywhere.step(2, dk)
    r0.step_one(*everywhere.done)
    everywhere.step(4, *r0.done)
    r0.step_two(*everywhere.done)
    two0 = r0.done
    r0.step_z()
    position_grad = everywhere.step_z(*two0)
    s_qkv = r0.step_last()
    d_tokens = pl.pallas_call(
        tokens_kernel,
        out_shape=wide32,
        in_specs=[SCALAR] + [WHOLE] * 6,
        out_specs=WHOLE,
        compiler_params=params(40),
        cost_estimate=cost(3),
        name="tokens",
    )(flags, d_resid, dq, dk, dv, m1, o1)

    def woven(pair, at):
        return jnp.concatenate(
            [half[:, at + p * 256 : at + p * 256 + 128] for half in pair for p in range(pairs // 2)], axis=1
        )

    s_small = s_qkv[0][:, 4 * hw :]
    bq, bk, bv, bo, sg1, ss1, bd, sg2, ss2 = [s_small[:, i] for i in range(count)]
    bu = s_small[:, count : count + up_own].T.reshape(-1)
    return (
        out.reshape(rows, block, width),
        d_tokens.reshape(rows, block, width),
        woven(s_qkv, 0),
        bq,
        woven(s_qkv, 2 * hw),
        bk,
        woven(s_qkv, 2 * hw + 128),
        bv,
        woven(s_qkv, 128),
        bo,
        sg1,
        ss1,
        s_u,
        bu,
        s_d,
        bd,
        sg2,
        ss2,
        position_grad,
    )


def solution(mesh):
    matrix, vector, split = P(BOTH, None), P(BOTH), P("rows", "seq", None)
    return jax.shard_map(
        on_device,
        mesh=mesh,
        in_specs=(split,)
        + (matrix, vector) * 4
        + (vector, vector)
        + (matrix, vector) * 2
        + (vector, vector)
        + (P(), P(), split),
        out_specs=(split, split)
        + (matrix, vector) * 4
        + (vector, vector)
        + (matrix, vector) * 2
        + (vector, vector)
        + (P(),),
        check_vma=False,
    )
```

time: 436 us -> 346 us (0.79); the launches traced: 428 us -> 345 us
  starting transfers between devices: 125 us -> 58.2 us
  Pallas kernels: 70.3 us -> 92.4 us
  waiting for transfers between devices: 150 us -> 131 us
  local copies, waits for them, and re-layouts: 50.9 us -> 34.4 us
  other arithmetic: 29.7 us -> 13.4 us
  between operations: 2.76 us -> 15.2 us
    ppermute x49 -> x22, waiting for transfers between devices: 109 us -> 56 us  [flip(): return lax.ppermute(a, BOTH, [(d, d ^ stride) for d in range(self.n)])]
    ppermute x49 -> x22, starting transfers between devices: 61.3 us -> 16.9 us  [flip(): return lax.ppermute(a, BOTH, [(d, d ^ stride) for d in range(self.n)])]
    reduce_scatter x0 -> x1, waiting for transfers between devices: none -> 20.3 us  [on_device(): lax.psum_scatter(g_rest, BOTH, scatter_dimension=0, tiled=True).astype(F32)]
    ppermute x21 -> x9, starting transfers between devices: 38.7 us -> 21.5 us  [turn_z(): lax.ppermute(a, BOTH, [(d, (d + 8 * by) % self.n) for d in range(self.n)])]
    unnamed x145 -> x95, local copies, waits for them, and re-layouts: 18.9 us -> 5.58 us
    pallas_call x4 -> x6, Pallas kernels: 38.2 us -> 48.5 us  [the longest x1 14.3 us: on_device(): pl.pallas_call(forward_kernel, grid=(1,), out_shape=(wide32, wide32, wide...]
    convert_element_type x22 -> x9, other arithmetic: 12.6 us -> 4.44 us  [plus(): return (kept.astype(F32) + got.astype(F32)).astype(BF)]
    ppermute x21 -> x9, waiting for transfers between devices: 24.6 us -> 31.7 us  [turn_z(): lax.ppermute(a, BOTH, [(d, (d + 8 * by) % self.n) for d in range(self.n)])]
  transfers between devices with their start and end apart: 79 -> 42, of which waited for: 30 -> 22; matrix products, arithmetic and copies ran while one was open for 14% -> 7% of each run, Pallas kernels for 7% -> 18%
where the time goes in v1:
time: 346 us; the launch traced here: 345 us
  waiting for transfers between devices  131 us (38%)
  Pallas kernels  92.4 us (27%)
  starting transfers between devices  58.2 us (17%)
  local copies, waits for them, and re-layouts  34.4 us (10%)
  between operations  15.2 us (4%)
  other arithmetic  13.4 us (4%)
    ppermute x22, waiting for transfers between devices, flip(): return lax.ppermute(a, BOTH, [(d, d ^ stride) for d in range(self.n)])  56 us
    ppermute x9, waiting for transfers between devices, turn_z(): lax.ppermute(a, BOTH, [(d, (d + 8 * by) % self.n) for d in range(self.n)])  31.7 us
    ppermute x6, waiting for transfers between devices, step_z(): got.append(lax.ppermute(pair, BOTH, pairs))  22.8 us
    ppermute x9, starting transfers between devices, turn_z(): lax.ppermute(a, BOTH, [(d, (d + 8 * by) % self.n) for d in range(self.n)])  21.5 us
    reduce_scatter x1, waiting for transfers between devices, on_device(): lax.psum_scatter(g_rest, BOTH, scatter_dimension=0, tiled=True).astype(F32)  20.3 us
    ppermute x22, starting transfers between devices, flip(): return lax.ppermute(a, BOTH, [(d, d ^ stride) for d in range(self.n)])  16.9 us
    pallas_call x1, Pallas kernels, on_device(): pl.pallas_call(query_back_kernel, grid_spec=pltpu.PrefetchScalarGridSpec(...  16.6 us
    pallas_call x1, Pallas kernels, on_device(): pl.pallas_call(key_back_kernel, grid_spec=pltpu.PrefetchScalarGridSpec(nu...  16.1 us
  transfers between devices with their start and end apart: 42, of which 22 were waited for; matrix products, arithmetic and copies ran while one was open for 7% of the time, Pallas kernels for 18%

profile of v1, /device:TPU:0, one launch (start us, length us, event | category | flops | bytes accessed | tf_op | source)
XLA Modules:
  0.0 344.7 jit_solution(16945302690512067819)
XLA Ops:
  14.0 4.8 %collective-permute-start.2 = (bf16[48,1280]{1,0:T(8,128)(2,1)S(1)}, bf16[48,1280]{1,0:T(8,128)(2,1)S(1)}, u32[]{:S(2)}, u32[]{:S(2)}) collective-permute-start(bf16[48,1280]{1,0:T(8,128)(2,1)S(1)} %pad_maximum_fusion.4), channel_id=1, source_target_pairs={{0,24},{1,25},{2,26},{3,27},{4,28},{5,29},{6,30},{7,31},{8,0},{9,1... | collective-permute-start | bytes 368648 | tf_op jit(solution)/shard_map/qkv_z/ppermute | solution.py:42
  22.5 13.2 %collective-permute-done.3 = bf16[48,1280]{1,0:T(8,128)(2,1)S(1)} collective-permute-done((bf16[48,1280]{1,0:T(8,128)(2,1)S(1)}, bf16[48,1280]{1,0:T(8,128)(2,1)S(1)}, u32[]{:S(2)}, u32[]{:S(2)}) %collective-permute-start.3) | collective-permute-done | bytes 122912 | tf_op jit(solution)/shard_map/qkv_z/ppermute | solution.py:42
  49.6 14.5 %collective-permute-done.8 = bf16[2,2,48,1280]{3,2,1,0:T(8,128)(2,1)S(1)} collective-permute-done((bf16[2,2,48,1280]{3,2,1,0:T(8,128)(2,1)S(1)}, bf16[2,2,48,1280]{3,2,1,0:T(8,128)(2,1)S(1)}, u32[]{:S(2)}, u32[]{:S(2)}) %collective-permute-start.8) | collective-permute-done | bytes 491552 | tf_op jit(solution)/shard_map/qkv_two/ppermute | solution.py:30
  69.3 6.1 %keys.1 = (f32[256,768]{1,0:T(8,128)}, f32[256,768]{1,0:T(8,128)}, bf16[256,768]{1,0:T(8,128)(2,1)}, bf16[256,768]{1,0:T(8,128)(2,1)}, bf16[2,80,768]{2,1,0:T(8,128)(2,1)}, /*index=5*/f32[16,768]{1,0:T(8,128)}) custom-call(s32[2]{0:T(128)} %pad_add_fusion.c_ref, bf16[256,768]{1,0:T(8,128)(2,1)} %bitcast.161, bf16[768,1280]{1,0:T(8,128)(2,1)} %bitcast.144, ...), custom_call_target="tpu_custom_call" | custom-call | flops 5000000000 | bytes 5000000 | tf_op jit(solution)/shard_map/keys/pallas_call | solution.py:771
  77.9 5.2 %queries.1 = (f32[256,768]{1,0:T(8,128)}, f32[256,768]{1,0:T(8,128)}, bf16[256,768]{1,0:T(8,128)(2,1)}) custom-call(s32[2]{0:T(128)} %pad_add_fusion.c_ref, bf16[256,768]{1,0:T(8,128)(2,1)} %bitcast.162, bf16[768,1280]{1,0:T(8,128)(2,1)} %bitcast.145, bf16[768,1280]{1,0:T(8,128)(2,1)} %collective-permute-done.9.other, f32[16,768]{1,0:T(8,128)} %get-tuple-element.83.vec, ...), custom_call_target="tpu_custom_call" | custom-call | flops 3000000000 | bytes 3000000 | tf_op jit(solution)/shard_map/queries/pallas_call | solution.py:782
  88.7 4.3 %collective-permute-start.13 = (bf16[80,768]{1,0:T(8,128)(2,1)S(1)}, bf16[80,768]{1,0:T(8,128)(2,1)S(1)}, u32[]{:S(2)}, u32[]{:S(2)}) collective-permute-start(bf16[80,768]{1,0:T(8,128)(2,1)S(1)} %fusion.14), channel_id=1, source_target_pairs={{0,16},{1,17},{2,18},{3,19},{4,20},{5,21},{6,22},{7,23},{8,24},{9,... | collective-permute-start | bytes 368648 | tf_op jit(solution)/shard_map/before_z/ppermute | solution.py:234
  95.4 4.8 %collective-permute-done.13 = bf16[80,768]{1,0:T(8,128)(2,1)S(1)} collective-permute-done((bf16[80,768]{1,0:T(8,128)(2,1)S(1)}, bf16[80,768]{1,0:T(8,128)(2,1)S(1)}, u32[]{:S(2)}, u32[]{:S(2)}) %collective-permute-start.13) | collective-permute-done | bytes 122912 | tf_op jit(solution)/shard_map/before_z/ppermute | solution.py:234
  100.2 5.0 %collective-permute-done.14 = bf16[80,768]{1,0:T(8,128)(2,1)S(1)} collective-permute-done((bf16[80,768]{1,0:T(8,128)(2,1)S(1)}, bf16[80,768]{1,0:T(8,128)(2,1)S(1)}, u32[]{:S(2)}, u32[]{:S(2)}) %collective-permute-start.14) | collective-permute-done | bytes 122912 | tf_op jit(solution)/shard_map/before_z/ppermute | solution.py:234
  106.1 4.8 %halo.1 = (bf16[256,768]{1,0:T(8,128)(2,1)}, bf16[256,768]{1,0:T(8,128)(2,1)}) custom-call(s32[2]{0:T(128)} %pad_add_fusion.c_ref, bf16[256,768]{1,0:T(8,128)(2,1)} %copy.108.halo, bf16[768,1280]{1,0:T(8,128)(2,1)} %bitcast.147, bf16[768,1280]{1,0:T(8,128)(2,1)} %collective-permute-done.9.other, f32[16,768]{1,0:T(8,128)} %get-tuple-element.83.vec, ...), custom_call_target="tpu_custom_call" | custom-call | flops 2000000000 | bytes 2000000 | tf_op jit(solution)/shard_map/halo/pallas_call | solution.py:792
  116.9 6.9 %attention.1 = (bf16[256,768]{1,0:T(8,128)(2,1)}, bf16[768,256]{1,0:T(8,128)(2,1)}, f32[256,768]{1,0:T(8,128)}, f32[256,768]{1,0:T(8,128)}) custom-call(bf16[256,768]{1,0:T(8,128)(2,1)} %get-tuple-element.84.q, bf16[256,768]{1,0:T(8,128)(2,1)} %get-tuple-element.85.k, bf16[256,768]{1,0:T(8,128)(2,1)} %get-tuple-element.86.v, ...), custom_call_target="tpu_custom_call" | custom-call | flops 5000000000 | bytes 5000000 | tf_op jit(solution)/shard_map/attention/pallas_call | solution.py:814
  131.8 14.3 %forward.1 = (f32[256,768]{1,0:T(8,128)}, f32[256,768]{1,0:T(8,128)}, bf16[256,768]{1,0:T(8,128)(2,1)}, bf16[256,768]{1,0:T(8,128)(2,1)}, f32[256,768]{1,0:T(8,1...) custom-call(bf16[256,768]{1,0:T(8,128)(2,1)} %get-tuple-element.95.context,, ...), custom_call_target="tpu_custom_call" | custom-call | flops 12999999488 | bytes 13000000 | tf_op jit(solution)/shard_map/forward/pallas_call | solution.py:829
  146.1 8.3 %upper_back.1 = (bf16[256,3072]{1,0:T(8,128)(2,1)}, bf16[4,768,768]{2,1,0:T(8,128)(2,1)}, f32[8,3072]{1,0:T(8,128)}) custom-call(bf16[256,768]{1,0:T(8,128)(2,1)} %get-tuple-element.100.dlow, bf16[256,768]{1,0:T(8,128)(2,1)} %get-tuple-element.101.hlow, bf16[256,3072]{1,0:T(8,128)(2,1)} %get-tuple-element.102.gp, ...), custom_call_target="tpu_custom_call" | custom-call | flops 7000000000 | bytes 7000000 | tf_op jit(solution)/shard_map/upper_back/pallas_call | solution.py:842
  159.8 9.1 %middle.1 = (f32[256,768]{1,0:T(8,128)}, bf16[256,768]{1,0:T(8,128)(2,1)}, bf16[256,896]{1,0:T(8,128)(2,1)}, bf16[2,80,768]{2,1,0:T(8,128)(2,1)}, f32[8,768]{1,0:T(8,128)}, /*index=5*/f32[8,768]{1,0:T(8,128)}) custom-call(f32[256,768]{1,0:T(8,128)} %get-tuple-element.104.dlower, bf16[256,3072]{1,0:T(8,128)(2,1)} %get-tuple-element.105.du, ...), custom_call_target="tpu_custom_call" | custom-call | flops 7000000000 | bytes 7000000 | tf_op jit(solution)/shard_map/middle/pallas_call | solution.py:857
  180.0 16.6 %query_back.1 = (bf16[256,768]{1,0:T(8,128)(2,1)}, bf16[768,768]{1,0:T(8,128)(2,1)}, bf16[768,768]{1,0:T(8,128)(2,1)}, f32[6,8,256]{2,1,0:T(8,128)}, f32[8,768]{1,0:T(8,128)}) custom-call(s32[2]{0:T(128)} %pad_add_fusion.c_ref, bf16[768,256]{1,0:T(8,128)(2,1)} %bitcast.165, bf16[768,256]{1,0:T(8,128)(2,1)} %get-tuple-element.113.context, ...), custom_call_target="tpu_custom_call" | custom-call | flops 11000000512 | bytes 11000000 | tf_op jit(solution)/shard_map/query_back/pallas_call | solution.py:881
  197.5 4.9 %collective-permute-done.20 = bf16[80,768]{1,0:T(8,128)(2,1)S(1)} collective-permute-done((bf16[80,768]{1,0:T(8,128)(2,1)S(1)}, bf16[80,768]{1,0:T(8,128)(2,1)S(1)}, u32[]{:S(2)}, u32[]{:S(2)}) %collective-permute-start.20) | collective-permute-done | bytes 122912 | tf_op jit(solution)/shard_map/later_z/ppermute | solution.py:234
  202.3 5.0 %collective-permute-done.21 = bf16[80,768]{1,0:T(8,128)(2,1)S(1)} collective-permute-done((bf16[80,768]{1,0:T(8,128)(2,1)S(1)}, bf16[80,768]{1,0:T(8,128)(2,1)S(1)}, u32[]{:S(2)}, u32[]{:S(2)}) %collective-permute-start.21) | collective-permute-done | bytes 122912 | tf_op jit(solution)/shard_map/later_z/ppermute | solution.py:234
  216.2 16.1 %key_back.1 = (bf16[256,768]{1,0:T(8,128)(2,1)}, bf16[256,768]{1,0:T(8,128)(2,1)}, bf16[768,768]{1,0:T(8,128)(2,1)}, bf16[768,768]{1,0:T(8,128)(2,1)}, bf16[768,128]{1,0:T(8,128)(2,1)}) custom-call(s32[2]{0:T(128)} %pad_add_fusion.c_ref, bf16[768,256]{1,0:T(8,128)(2,1)} %bitcast.166, bf16[256,768]{1,0:T(8,128)(2,1)} %get-tuple-element.84.q, ...), custom_call_target="tpu_custom_call" | custom-call | flops 12000000000 | bytes 12000000 | tf_op jit(solution)/shard_map/key_back/pallas_call | solution.py:904
  240.9 20.9 %collective-permute-done.28 = bf16[2,2,48,1664]{3,2,0,1:T(8,128)(2,1)} collective-permute-done((bf16[2,2,48,1664]{3,2,0,1:T(8,128)(2,1)S(1)}, bf16[2,2,48,1664]{3,2,0,1:T(8,128)(2,1)}, u32[]{:S(2)}, u32[]{:S(2)}) %collective-permute-start.28) | collective-permute-done | bytes 639008 | tf_op jit(solution)/shard_map/d_qkv_one/ppermute | solution.py:30
  268.1 5.0 %tokens.1 = f32[256,768]{1,0:T(8,128)} custom-call(s32[2]{0:T(128)} %pad_add_fusion.c_ref, f32[256,768]{1,0:T(8,128)} %get-tuple-element.110.dresid, bf16[256,768]{1,0:T(8,128)(2,1)} %get-tuple-element.119.dq, bf16[256,768]{1,0:T(8,128)(2,1)} %get-tuple-element.131.dk, bf16[256,768]{1,0:T(8,128)(2,1)} %get-tuple-element.132.dv, bf16[768,1280]{1,0:T(8,128)(2,1)} %bitcast.148, ...), custom_call_target="tpu_custom_call" | custom-call | flops 3000000000 | bytes 3000000 | tf_op jit(solution)/shard_map/tokens/pallas_call | solution.py:930
  273.1 5.9 %collective-permute-done.31 = bf16[2,48,1664]{2,1,0:T(8,128)(2,1)S(1)} collective-permute-done((bf16[2,48,1664]{2,1,0:T(8,128)(2,1)S(1)}, bf16[2,48,1664]{2,1,0:T(8,128)(2,1)S(1)}, u32[]{:S(2)}, u32[]{:S(2)}) %collective-permute-start.31) | collective-permute-done | bytes 319520 | tf_op jit(solution)/shard_map/d_qkv_two/ppermute | solution.py:30
  279.0 9.7 %collective-permute-start.37 = (f32[12,129]{1,0:T(8,128)S(1)}, f32[12,129]{1,0:T(8,128)S(1)}, u32[]{:S(2)}, u32[]{:S(2)}) collective-permute-start(f32[12,129]{1,0:T(8,128)S(1)} %add.228), channel_id=1, source_target_pairs={{0,24},{1,25},{2,26},{3,27},{4,28},{5,29},{6,30},{7,31},{8,0},{9,1... | collective-permute-start | bytes 18584 | tf_op jit(solution)/shard_map/everywhere/ppermute | solution.py:42
  295.1 6.8 %collective-permute-done.33 = bf16[48,1664]{1,0:T(8,128)(2,1)S(1)} collective-permute-done((bf16[48,1664]{1,0:T(8,128)(2,1)S(1)}, bf16[48,1664]{1,0:T(8,128)(2,1)S(1)}, u32[]{:S(2)}, u32[]{:S(2)}) %collective-permute-start.33) | collective-permute-done | bytes 159776 | tf_op jit(solution)/shard_map/d_qkv_z/ppermute | solution.py:42
  301.9 9.1 %collective-permute-done.34 = bf16[48,1664]{1,0:T(8,128)(2,1)S(1)} collective-permute-done((bf16[48,1664]{1,0:T(8,128)(2,1)S(1)}, bf16[48,1664]{1,0:T(8,128)(2,1)S(1)}, u32[]{:S(2)}, u32[]{:S(2)}) %collective-permute-start.34) | collective-permute-done | bytes 159776 | tf_op jit(solution)/shard_map/d_qkv_z/ppermute | solution.py:42
  314.3 20.3 %reduce-scatter.2.cloned.1.call-done = bf16[96,1536]{1,0:T(8,128)(2,1)} async-done(((bf16[3072,1536]{1,0:T(8,128)(2,1)}), bf16[96,1536]{1,0:T(8,128)(2,1)}) %reduce-scatter.2.cloned.1.call-update) | async-done | bytes 294928 | tf_op jit(solution)/shard_map/reduce_scatter | solution.py:854
  (263 shorter events, 107.9 us)
Async XLA Ops:
  7.3 116.6 %all-gather.2.cloned.1.call-start = ((), (), s32[]{:S(2)}) async-start(), calls=%async_computation.1 | async-start | bytes 11354112 | tf_op jit(solution)/shard_map/all_gather | solution.py:745
  10.8 323.8 %reduce-scatter.2.cloned.1.call-start = ((), (), s32[]{:S(2)}) async-start(), calls=%async_computation.2 | async-start | bytes 9732096 | tf_op jit(solution)/shard_map/reduce_scatter | solution.py:854
  18.8 16.9 %collective-permute-start.3 = (bf16[48,1280]{1,0:T(8,128)(2,1)S(1)}, bf16[48,1280]{1,0:T(8,128)(2,1)S(1)}, u32[]{:S(2)}, u32[]{:S(2)}) collective-permute-start(bf16[48,1280]{1,0:T(8,128)(2,1)S(1)} %pad_maximum_fusion.4), channel_id=1, source_target_pairs={{0,16},{1,17},{2,18},{3,19},{4,20},{5,21},{6,22},{7,23},{8,24},{9,... | collective-permute-start | bytes 368648 | tf_op jit(solution)/shard_map/qkv_z/ppermute | solution.py:42
  18.9 16.8 %collective-permute-start.4 = (bf16[48,1280]{1,0:T(8,128)(2,1)S(1)}, bf16[48,1280]{1,0:T(8,128)(2,1)S(1)}, u32[]{:S(2)}, u32[]{:S(2)}) collective-permute-start(bf16[48,1280]{1,0:T(8,128)(2,1)S(1)} %pad_maximum_fusion.4), channel_id=1, source_target_pairs={{0,8},{1,9},{2,10},{3,11},{4,12},{5,13},{6,14},{7,15},{8,16},{9,17... | collective-permute-start | bytes 368648 | tf_op jit(solution)/shard_map/qkv_z/ppermute | solution.py:42
  42.2 22.0 %collective-permute-start.8 = (bf16[2,2,48,1280]{3,2,1,0:T(8,128)(2,1)S(1)}, bf16[2,2,48,1280]{3,2,1,0:T(8,128)(2,1)S(1)}, u32[]{:S(2)}, u32[]{:S(2)}) collective-permute-start(bf16[2,2,48,1280]{3,2,1,0:T(8,128)(2,1)S(1)} %maximum_select_fusion.3), channel_id=1, source_target_pairs={{0,4},{1,5},{2,6},{3,7},{4,0},{5,1},{6,2},{7,3},{8,12},{9,13},{10,... | collective-permute-start | bytes 1474568 | tf_op jit(solution)/shard_map/qkv_two/ppermute | solution.py:30
  45.7 18.6 %collective-permute-start.6 = (bf16[2,2,48,1280]{3,2,0,1:T(8,128)(2,1)S(1)}, bf16[2,2,48,1280]{3,2,0,1:T(8,128)(2,1)S(1)}, u32[]{:S(2)}, u32[]{:S(2)}) collective-permute-start(bf16[2,2,48,1280]{3,2,0,1:T(8,128)(2,1)S(1)} %maximum_select_fusion.2), channel_id=1, source_target_pairs={{0,2},{1,3},{2,0},{3,1},{4,6},{5,7},{6,4},{7,5},{8,10},{9,11},{10,... | collective-permute-start | bytes 1474568 | tf_op jit(solution)/shard_map/qkv_two/ppermute | solution.py:30
  65.3 30.1 %collective-permute-start.10 = (bf16[256,768]{0,1:T(8,128)(2,1)S(1)}, bf16[256,768]{0,1:T(8,128)(2,1)S(1)}, u32[]{:S(2)}, u32[]{:S(2)}) collective-permute-start(bf16[256,768]{0,1:T(8,128)(2,1)S(1)} %copy-done.7), channel_id=1, source_target_pairs={{0,4},{4,8},{8,12},{12,16},{16,20},{20,24},{24,28},{1,5},{5,9},{9,... | collective-permute-start | bytes 1179656 | tf_op jit(solution)/shard_map/ppermute | solution.py:46
  84.5 10.9 %collective-permute-start.12 = (bf16[80,768]{1,0:T(8,128)(2,1)S(1)}, bf16[80,768]{1,0:T(8,128)(2,1)S(1)}, u32[]{:S(2)}, u32[]{:S(2)}) collective-permute-start(bf16[80,768]{1,0:T(8,128)(2,1)S(1)} %fusion.14), channel_id=1, source_target_pairs={{0,8},{1,9},{2,10},{3,11},{4,12},{5,13},{6,14},{7,15},{8,16},{9,17... | collective-permute-start | bytes 368648 | tf_op jit(solution)/shard_map/before_z/ppermute | solution.py:234
  88.7 11.5 %collective-permute-start.13 = (bf16[80,768]{1,0:T(8,128)(2,1)S(1)}, bf16[80,768]{1,0:T(8,128)(2,1)S(1)}, u32[]{:S(2)}, u32[]{:S(2)}) collective-permute-start(bf16[80,768]{1,0:T(8,128)(2,1)S(1)} %fusion.14), channel_id=1, source_target_pairs={{0,16},{1,17},{2,18},{3,19},{4,20},{5,21},{6,22},{7,23},{8,24},{9,... | collective-permute-start | bytes 368648 | tf_op jit(solution)/shard_map/before_z/ppermute | solution.py:234
  93.0 12.2 %collective-permute-start.14 = (bf16[80,768]{1,0:T(8,128)(2,1)S(1)}, bf16[80,768]{1,0:T(8,128)(2,1)S(1)}, u32[]{:S(2)}, u32[]{:S(2)}) collective-permute-start(bf16[80,768]{1,0:T(8,128)(2,1)S(1)} %fusion.14), channel_id=1, source_target_pairs={{0,24},{1,25},{2,26},{3,27},{4,28},{5,29},{6,30},{7,31}} | collective-permute-start | bytes 368648 | tf_op jit(solution)/shard_map/before_z/ppermute | solution.py:234
  171.1 26.3 %collective-permute-start.18 = (bf16[256,768]{1,0:T(8,128)(2,1)S(1)}, bf16[256,768]{1,0:T(8,128)(2,1)S(1)}, u32[]{:S(2)}, u32[]{:S(2)}) collective-permute-start(bf16[256,768]{1,0:T(8,128)(2,1)S(1)} %copy-done.34), channel_id=1, source_target_pairs={{4,0},{8,4},{12,8},{16,12},{20,16},{24,20},{28,24},{5,1},{9,5},{13... | collective-permute-start | bytes 1179656 | tf_op jit(solution)/shard_map/ppermute | solution.py:46
  172.4 29.9 %collective-permute-start.19 = (bf16[256,896]{1,0:T(8,128)(2,1)S(1)}, bf16[256,896]{1,0:T(8,128)(2,1)S(1)}, u32[]{:S(2)}, u32[]{:S(2)}) collective-permute-start(bf16[256,896]{1,0:T(8,128)(2,1)S(1)} %copy-done.32), channel_id=1, source_target_pairs={{4,0},{8,4},{12,8},{16,12},{20,16},{24,20},{28,24},{5,1},{9,5},{13... | collective-permute-start | bytes 1376264 | tf_op jit(solution)/shard_map/ppermute | solution.py:46
  176.1 26.3 %collective-permute-start.20 = (bf16[80,768]{1,0:T(8,128)(2,1)S(1)}, bf16[80,768]{1,0:T(8,128)(2,1)S(1)}, u32[]{:S(2)}, u32[]{:S(2)}) collective-permute-start(bf16[80,768]{1,0:T(8,128)(2,1)S(1)} %fusion.17), channel_id=1, source_target_pairs={{8,0},{9,1},{10,2},{11,3},{12,4},{13,5},{14,6},{15,7},{16,8},{17,9... | collective-permute-start | bytes 368648 | tf_op jit(solution)/shard_map/later_z/ppermute | solution.py:234
  177.4 30.0 %collective-permute-start.21 = (bf16[80,768]{1,0:T(8,128)(2,1)S(1)}, bf16[80,768]{1,0:T(8,128)(2,1)S(1)}, u32[]{:S(2)}, u32[]{:S(2)}) collective-permute-start(bf16[80,768]{1,0:T(8,128)(2,1)S(1)} %fusion.17), channel_id=1, source_target_pairs={{16,0},{17,1},{18,2},{19,3},{20,4},{21,5},{22,6},{23,7},{24,8},{25... | collective-permute-start | bytes 368648 | tf_op jit(solution)/shard_map/later_z/ppermute | solution.py:234
  178.7 31.8 %collective-permute-start.22 = (bf16[80,768]{1,0:T(8,128)(2,1)S(1)}, bf16[80,768]{1,0:T(8,128)(2,1)S(1)}, u32[]{:S(2)}, u32[]{:S(2)}) collective-permute-start(bf16[80,768]{1,0:T(8,128)(2,1)S(1)} %fusion.17), channel_id=1, source_target_pairs={{24,0},{25,1},{26,2},{27,3},{28,4},{29,5},{30,6},{31,7}} | collective-permute-start | bytes 368648 | tf_op jit(solution)/shard_map/later_z/ppermute | solution.py:234
  213.5 23.1 %collective-permute-start.24 = (bf16[768,768]{1,0:T(8,128)(2,1)}, bf16[768,768]{1,0:T(8,128)(2,1)S(1)}, u32[]{:S(2)}, u32[]{:S(2)}) collective-permute-start(bf16[768,768]{1,0:T(8,128)(2,1)} %get-tuple-element.134), channel_id=1, source_target_pairs={{0,1},{1,0},{2,3},{3,2},{4,5},{5,4},{6,7},{7,6},{8,9},{9,8},{10,11... | collective-permute-start | bytes 3538952 | tf_op jit(solution)/shard_map/d_qkv_core/ppermute | solution.py:30
  239.0 22.8 %collective-permute-start.28 = (bf16[2,2,48,1664]{3,2,0,1:T(8,128)(2,1)S(1)}, bf16[2,2,48,1664]{3,2,0,1:T(8,128)(2,1)}, u32[]{:S(2)}, u32[]{:S(2)}) collective-permute-start(bf16[2,2,48,1664]{3,2,0,1:T(8,128)(2,1)S(1)} %copy_bitcast_fusion), channel_id=1, source_target_pairs={{0,2},{1,3},{2,0},{3,1},{4,6},{5,7},{6,4},{7,5},{8,10},{9,11},{10,... | collective-permute-start | bytes 1916936 | tf_op jit(solution)/shard_map/d_qkv_one/ppermute | solution.py:30
  240.3 21.5 %collective-permute-start.29 = (bf16[2,2,48,1664]{3,2,1,0:T(8,128)(2,1)}, bf16[2,2,48,1664]{3,2,1,0:T(8,128)(2,1)}, u32[]{:S(2)}, u32[]{:S(2)}) collective-permute-start(bf16[2,2,48,1664]{3,2,1,0:T(8,128)(2,1)} %dynamic-slice_bitcast_fusion), channel_id=1, source_target_pairs={{0,4},{1,5},{2,6},{3,7},{4,0},{5,1},{6,2},{7,3},{8,12},{9,13},{10,... | collective-permute-start | bytes 1916936 | tf_op jit(solution)/shard_map/d_qkv_one/ppermute | solution.py:30
  265.9 13.2 %collective-permute-start.31 = (bf16[2,48,1664]{2,1,0:T(8,128)(2,1)S(1)}, bf16[2,48,1664]{2,1,0:T(8,128)(2,1)S(1)}, u32[]{:S(2)}, u32[]{:S(2)}) collective-permute-start(bf16[2,48,1664]{2,1,0:T(8,128)(2,1)S(1)} %dynamic-slice_bitcast_fusion.2), channel_id=1, source_target_pairs={{0,4},{1,5},{2,6},{3,7},{4,0},{5,1},{6,2},{7,3},{8,12},{9,13},{10,... | collective-permute-start | bytes 958472 | tf_op jit(solution)/shard_map/d_qkv_two/ppermute | solution.py:30
  267.3 11.7 %collective-permute-start.32 = (bf16[2,48,1664]{2,1,0:T(8,128)(2,1)S(1)}, bf16[2,48,1664]{2,1,0:T(8,128)(2,1)S(1)}, u32[]{:S(2)}, u32[]{:S(2)}) collective-permute-start(bf16[2,48,1664]{2,1,0:T(8,128)(2,1)S(1)} %dynamic-slice_bitcast_fusion.1), channel_id=1, source_target_pairs={{0,2},{1,3},{2,0},{3,1},{4,6},{5,7},{6,4},{7,5},{8,10},{9,11},{10,... | collective-permute-start | bytes 958472 | tf_op jit(solution)/shard_map/d_qkv_two/ppermute | solution.py:30
  279.0 14.4 %collective-permute-start.37 = (f32[12,129]{1,0:T(8,128)S(1)}, f32[12,129]{1,0:T(8,128)S(1)}, u32[]{:S(2)}, u32[]{:S(2)}) collective-permute-start(f32[12,129]{1,0:T(8,128)S(1)} %add.228), channel_id=1, source_target_pairs={{0,24},{1,25},{2,26},{3,27},{4,28},{5,29},{6,30},{7,31},{8,0},{9,1... | collective-permute-start | bytes 18584 | tf_op jit(solution)/shard_map/everywhere/ppermute | solution.py:42
  289.6 12.3 %collective-permute-start.33 = (bf16[48,1664]{1,0:T(8,128)(2,1)S(1)}, bf16[48,1664]{1,0:T(8,128)(2,1)S(1)}, u32[]{:S(2)}, u32[]{:S(2)}) collective-permute-start(bf16[48,1664]{1,0:T(8,128)(2,1)S(1)} %get-tuple-element.160), channel_id=1, source_target_pairs={{0,8},{1,9},{2,10},{3,11},{4,12},{5,13},{6,14},{7,15},{8,16},{9,17... | collective-permute-start | bytes 479240 | tf_op jit(solution)/shard_map/d_qkv_z/ppermute | solution.py:42
  292.6 18.4 %collective-permute-start.34 = (bf16[48,1664]{1,0:T(8,128)(2,1)S(1)}, bf16[48,1664]{1,0:T(8,128)(2,1)S(1)}, u32[]{:S(2)}, u32[]{:S(2)}) collective-permute-start(bf16[48,1664]{1,0:T(8,128)(2,1)S(1)} %get-tuple-element.162), channel_id=1, source_target_pairs={{0,16},{1,17},{2,18},{3,19},{4,20},{5,21},{6,22},{7,23},{8,24},{9,... | collective-permute-start | bytes 479240 | tf_op jit(solution)/shard_map/d_qkv_z/ppermute | solution.py:42
  293.5 17.5 %collective-permute-start.35 = (bf16[48,1664]{1,0:T(8,128)(2,1)S(1)}, bf16[48,1664]{1,0:T(8,128)(2,1)S(1)}, u32[]{:S(2)}, u32[]{:S(2)}) collective-permute-start(bf16[48,1664]{1,0:T(8,128)(2,1)S(1)} %get-tuple-element.161), channel_id=1, source_target_pairs={{0,24},{1,25},{2,26},{3,27},{4,28},{5,29},{6,30},{7,31},{8,0},{9,1... | collective-permute-start | bytes 479240 | tf_op jit(solution)/shard_map/d_qkv_z/ppermute | solution.py:42
  (54 other events, 493.4 us)
Sparse Core Ops, SparseCore 0:
  11.1 107.4 all-gather.1
  172.5 161.9 reduce-scatter.1

commit v2 on v1

--- a/solution.py
+++ b/solution.py
@@ -1,3 +1,4 @@
+import functools
 import math
 
 import jax
@@ -462,27 +463,37 @@
 
 
 def forward_kernel(
-    context, tok, wu, wo, wd, cot, vec, bu,
-    out, dlower_out, dlow_out, hlow_out, xhat_out, rstd_out, gp_out, grad_out, sums_out,
+    context, tok, cot, vec, bu, wu_hbm, wo_hbm, rest_hbm,
+    out, dlower_out, du_out, xhat_out, rstd_out, sums_out, du_sums_out, down_hbm, up_hbm,
+    wu, wo, wd, gp, grads, in_sems, out_sems,
 ):
-    attn = jnp.concatenate([dot(context[...], wo[i]) for i in range(wo.shape[0])], axis=1)
+    count, width, step = wu.shape
+    loads = [pltpu.make_async_copy(wo_hbm, wo, in_sems.at[2 * count])]
+    for i in range(count):
+        loads.append(pltpu.make_async_copy(wu_hbm.at[i], wu.at[i], in_sems.at[i]))
+        wd_block = rest_hbm.at[pl.ds(i * step, step), pl.ds(0, width)]
+        loads.append(pltpu.make_async_copy(wd_block, wd.at[i], in_sems.at[count + i]))
+    for load in loads:
+        load.start()
+    loads[0].wait()
+    attn = jnp.concatenate([dot(context[...], wo[i]) for i in range(count)], axis=1)
     xhat, rstd = normed(tok[...].astype(F32) + attn + vec[3:4])
     hidden = xhat * vec[4:5] + vec[5:6]
     xhat_out[...] = xhat
     rstd_out[...] = jnp.broadcast_to(rstd, rstd_out.shape)
     h_low = hidden.astype(BF)
-    hlow_out[...] = h_low
-    step = wu.shape[2]
     lower = hidden + vec[6:7]
     actives = []
-    for i in range(wu.shape[0]):
+    for i in range(count):
         cols = slice(i * step, (i + 1) * step)
+        loads[1 + 2 * i].wait()
         upper = dot(h_low, wu[i]) + bu[:, cols]
         cdf = 0.5 * (1.0 + lax.erf(upper * 2.0 ** (-0.5)))
         pdf = jnp.exp(-0.5 * upper * upper) * (2.0 * math.pi) ** (-0.5)
-        gp_out[:, cols] = (cdf + upper * pdf).astype(BF)
+        gp[:, cols] = (cdf + upper * pdf).astype(BF)
         actives.append((upper * cdf).astype(BF))
-        lower = lower + dot(actives[-1], wd[cols])
+        loads[2 + 2 * i].wait()
+        lower = lower + dot(actives[-1], wd[i])
     xhat2, rstd2 = normed(lower)
     gain2 = vec[7:8]
     out[...] = xhat2 * gain2 + vec[8:9]
@@ -490,33 +501,39 @@
     d_lower = norm_back(dy, xhat2, rstd2, gain2)
     dlower_out[...] = d_lower
     d_low = d_lower.astype(BF)
-    dlow_out[...] = d_low
     sums_out[0:1] = col_sums(d_low.astype(F32))
     sums_out[1:2] = col_sums(dy * xhat2)
     sums_out[2:3] = col_sums(dy)
-    for i in range(wu.shape[0]):
-        grad_out[i * step : (i + 1) * step, : d_low.shape[1]] = tdot(actives[i], d_low).astype(BF)
-
-
-def upper_back_kernel(dlow, hlow, gp, wd, du_out, grad_out, sums_out):
-    d_low, h_low = dlow[...], hlow[...]
-    step = grad_out.shape[2]
-    for i in range(grad_out.shape[0]):
+    stores = []
+    for i in range(count):
         cols = slice(i * step, (i + 1) * step)
-        d_upper = (dot_t(d_low, wd[cols]) * gp[:, cols].astype(F32)).astype(BF)
+        d_upper = (dot_t(d_low, wd[i]) * gp[:, cols].astype(F32)).astype(BF)
         du_out[:, cols] = d_upper
-        sums_out[:, cols] = jnp.broadcast_to(col_sums(d_upper.astype(F32)), (8, step))
-        grad_out[i] = tdot(h_low, d_upper).astype(BF)
+        du_sums_out[:, cols] = jnp.broadcast_to(col_sums(d_upper.astype(F32)), (8, step))
+        grads[2 * i] = tdot(h_low, d_upper).astype(BF)
+        stores.append(pltpu.make_async_copy(grads.at[2 * i], up_hbm.at[i], out_sems.at[2 * i]))
+        stores[-1].start()
+        grads[2 * i + 1] = tdot(actives[i], d_low).astype(BF)
+        block = down_hbm.at[pl.ds(i * step, step), pl.ds(0, width)]
+        stores.append(pltpu.make_async_copy(grads.at[2 * i + 1], block, out_sems.at[2 * i + 1]))
+        stores[-1].start()
+    for store in stores:
+        store.wait()
 
 
 def middle_kernel(
-    dlower, du, xhat, rstd, wu, wo, vec, ratio, denom, q, state, far,
+    dlower, du, xhat, rstd, wu_hbm, wo, vec, ratio, denom, q, state, far,
     dresid_out, dattn_out, dn_out, later_out, sums_out, near_out,
+    wu, sems,
 ):
     hw = dlower.shape[1] // 2
     d_hidden = dlower[...]
     step = wu.shape[2]
+    loads = [pltpu.make_async_copy(wu_hbm.at[i], wu.at[i], sems.at[i]) for i in range(wu.shape[0])]
+    for load in loads:
+        load.start()
     for i in range(wu.shape[0]):
+        loads[i].wait()
         d_hidden = d_hidden + dot_t(du[:, i * step : (i + 1) * step], wu[i])
     xh = xhat[...]
     d_resid = norm_back(d_hidden, xh, rstd[:, 0:1], vec[4:5])
@@ -668,6 +685,15 @@
     out[...] = total
 
 
+def unpack_kernel(packed, down_out, up_out):
+    own, width = up_out.shape[0], down_out.shape[1]
+    step = packed.shape[1] - width
+    wide = packed[...].astype(F32)
+    down_out[...] = wide[:, :width]
+    for i in range(packed.shape[0] // own):
+        up_out[:, i * step : (i + 1) * step] = wide[i * own : (i + 1) * own, width:]
+
+
 def feature_blocks(matrix):
     heads, size, feats = matrix.shape
     zero = jnp.zeros((heads // 2, size, feats), F32)
@@ -798,10 +824,10 @@
         cost_estimate=cost(2),
         name="halo",
     )(flags, after(halo_tok, *scan.done), m1, o1, vec, gh, gl)
-    before = scan.step_last(hk)
+    q_next = at.along(q, -1)
+    before = scan.step_last(hk, q_next)
     b_u = m1[:, 3 * hw + count : 3 * hw + count + up_own].reshape(at.n, own, up_own)
     b_u = jnp.swapaxes(after(b_u, hk), 1, 2).reshape(1, ff).astype(F32)
-    q_next = at.along(q, -1)
 
     def columns(height=n):
         return pl.BlockSpec((height, 128), lambda p, *_: (0, p))
@@ -825,40 +851,50 @@
     split = rest.reshape(at.n, slices, own, rest.shape[1])
     wu = jnp.swapaxes(split[..., width : width + step], 0, 1).reshape(slices, width, step)
     wo = jnp.swapaxes(split[..., width + step :], 0, 1).reshape(slices, width, wo_step)
-    wd_spec = pl.BlockSpec((ff, width), lambda i: (0, 0), pipeline_mode=pl.Buffered(1))
-    out, d_lower, d_low, h_low, xhat, rstd, gp, g_down, sums3 = pl.pallas_call(
+    away = pl.BlockSpec(memory_space=pl.ANY)
+    out, d_lower, du, xhat, rstd, sums3, du_sums, g_down, g_up = pl.pallas_call(
         forward_kernel,
-        grid=(1,),
         out_shape=(
-            wide32, wide32, wide16, wide16, wide32, arr((n, 128), F32), arr((n, ff), BF),
-            arr((ff, width + step), BF), arr((8, width), F32),
+            wide32, wide32, arr((n, ff), BF), wide32, arr((n, 128), F32), arr((8, width), F32), arr((8, ff), F32),
+            arr((ff, width + step), BF), arr((slices, width, step), BF),
         ),
-        in_specs=[WHOLE] * 4 + [wd_spec] + [WHOLE] * 3,
-        out_specs=(WHOLE,) * 9,
+        in_specs=[WHOLE] * 5 + [away] * 3,
+        out_specs=(WHOLE,) * 7 + (away,) * 2,
+        scratch_shapes=[
+            VMEM((slices, width, step), BF),
+            VMEM((slices, width, wo_step), BF),
+            VMEM((slices, step, width), BF),
+            VMEM((n, ff), BF),
+            VMEM((2 * slices, width, step), BF),
+            pltpu.SemaphoreType.DMA((2 * slices + 1,)),
+            pltpu.SemaphoreType.DMA((2 * slices,)),
+        ],
         compiler_params=params(56),
-        cost_estimate=cost(13),
+        cost_estimate=cost(18),
         name="forward",
-    )(context, tok, wu, wo, rest, cot, vec, b_u)
-    du, g_up, du_sums = pl.pallas_call(
-        upper_back_kernel,
-        grid=(1,),
-        out_shape=(arr((n, ff), BF), arr((slices, width, step), BF), arr((8, ff), F32)),
-        in_specs=[WHOLE] * 3 + [wd_spec],
-        out_specs=(WHOLE,) * 3,
-        compiler_params=params(48),
-        cost_estimate=cost(7),
-        name="upper_back",
-    )(d_low, h_low, gp, rest)
+    )(context, tok, cot, vec, b_u, wu, wo, rest)
     g_up = jnp.swapaxes(g_up.reshape(slices, at.n, own, step), 0, 1).reshape(ff, step)
     g_rest = lax.dynamic_update_slice(g_down, g_up, (0, width))
-    s_rest = lax.psum_scatter(g_rest, BOTH, scatter_dimension=0, tiled=True).astype(F32)
-    s_d = s_rest[:, :width]
-    s_u = jnp.concatenate(jnp.split(s_rest[:, width:], slices, axis=0), axis=1)
+    s_rest = lax.psum_scatter(g_rest, BOTH, scatter_dimension=0, tiled=True)
+    if own % 8 == 0:
+        s_d, s_u = pl.pallas_call(
+            unpack_kernel,
+            out_shape=(arr((slices * own, width), F32), arr((own, ff), F32)),
+            in_specs=[WHOLE],
+            out_specs=(WHOLE,) * 2,
+            compiler_params=params(48),
+            cost_estimate=cost(1),
+            name="unpack",
+        )(s_rest)
+    else:
+        s_d = s_rest[:, :width].astype(F32)
+        s_u = jnp.concatenate(jnp.split(s_rest[:, width:].astype(F32), slices, axis=0), axis=1)
     d_resid, d_attn, dn, local, sums2, near = pl.pallas_call(
         middle_kernel,
         out_shape=(wide32, wide16, arr((n, width + 128), BF), sums, arr((8, width), F32), arr((8, width), F32)),
-        in_specs=[WHOLE] * 12,
+        in_specs=[WHOLE] * 4 + [away] + [WHOLE] * 7,
         out_specs=(WHOLE,) * 6,
+        scratch_shapes=[VMEM((slices, width, step), BF), pltpu.SemaphoreType.DMA((slices,))],
         compiler_params=params(48),
         cost_estimate=cost(7),
         name="middle",
@@ -893,7 +929,7 @@
         name="query_back",
     )(flags, after(tok_t, *scan.done), context_t, d_attn, q, k, v, hk, hv, dn, dn, table, before, far, q_phi, sq, gh, gl, near)
     scan.step_z()
-    later = scan.step_last(dq, q_next, dn_next)
+    later = scan.step_last(dq, dn_next)
     everywhere = Everywhere(at, exp_bias * pos[:, :2, : window + 1].reshape(heads, window + 1))
     everywhere.step(1)
     du = du_sums[0].reshape(at.n, up_own, own)

time: 346 us -> 328 us (0.948)
  waiting for transfers between devices: 131 us -> 125 us
  starting transfers between devices: 58.2 us -> 52.3 us
  Pallas kernels: 92.4 us -> 88.1 us
    ppermute x6, waiting for transfers between devices: 22.8 us -> 5.69 us  [step_z(): got.append(lax.ppermute(pair, BOTH, pairs))]
    ppermute x9, starting transfers between devices: 21.5 us -> 14.4 us  [turn_z(): lax.ppermute(a, BOTH, [(d, (d + 8 * by) % self.n) for d in range(self.n)])]
    all_gather x1, waiting for transfers between devices: 0.02 us -> 5.85 us  [on_device(): lax.all_gather(jnp.concatenate([down_weight, stacked(up_weight), stacked(...]
    reduce_scatter x1, waiting for transfers between devices: 20.3 us -> 25.8 us  [on_device(): s_rest = lax.psum_scatter(g_rest, BOTH, scatter_dimension=0, tiled=True)]
    pallas_call x2, Pallas kernels: 22.6 us -> 17.9 us  [the longest x1 16.1 us: on_device(): pl.pallas_call(forward_kernel, out_shape=(wide32, wide32, arr((n, ff), BF...]
  transfers between devices with their start and end apart: 42 -> 42, of which waited for: 22 -> 20; matrix products, arithmetic and copies ran while one was open for 7% -> 8% of each run, Pallas kernels for 18% -> 19%
where the time goes in v2:
time: 328 us; the launch traced here: 327 us
  waiting for transfers between devices  125 us (38%)
  Pallas kernels  88.1 us (27%)
  starting transfers between devices  52.3 us (16%)
  local copies, waits for them, and re-layouts  32.7 us (10%)
  between operations  15.2 us (5%)
  other arithmetic  12.7 us (4%)
    ppermute x22, waiting for transfers between devices, flip(): return lax.ppermute(a, BOTH, [(d, d ^ stride) for d in range(self.n)])  57.4 us
    ppermute x9, waiting for transfers between devices, turn_z(): lax.ppermute(a, BOTH, [(d, (d + 8 * by) % self.n) for d in range(self.n)])  30.7 us
    reduce_scatter x1, waiting for transfers between devices, on_device(): s_rest = lax.psum_scatter(g_rest, BOTH, scatter_dimension=0, tiled=True)  25.8 us
    pallas_call x1, Pallas kernels, on_device(): pl.pallas_call(query_back_kernel, grid_spec=pltpu.PrefetchScalarGridSpec(...  16.9 us
    ppermute x22, starting transfers between devices, flip(): return lax.ppermute(a, BOTH, [(d, d ^ stride) for d in range(self.n)])  16.5 us
    pallas_call x1, Pallas kernels, on_device(): pl.pallas_call(forward_kernel, out_shape=(wide32, wide32, arr((n, ff), BF...  16.1 us
    pallas_call x1, Pallas kernels, on_device(): pl.pallas_call(key_back_kernel, grid_spec=pltpu.PrefetchScalarGridSpec(nu...  16.1 us
    ppermute x6, starting transfers between devices, step_z(): got.append(lax.ppermute(pair, BOTH, pairs))  15.3 us
  transfers between devices with their start and end apart: 42, of which 20 were waited for; matrix products, arithmetic and copies ran while one was open for 8% of the time, Pallas kernels for 19%

profile of v2, /device:TPU:0, one launch (start us, length us, event | category | flops | bytes accessed | tf_op | source)
XLA Modules:
  0.0 326.6 jit_solution(2514544928775321890)
XLA Ops:
  14.0 4.8 %collective-permute-start.2 = (bf16[48,1280]{1,0:T(8,128)(2,1)S(1)}, bf16[48,1280]{1,0:T(8,128)(2,1)S(1)}, u32[]{:S(2)}, u32[]{:S(2)}) collective-permute-start(bf16[48,1280]{1,0:T(8,128)(2,1)S(1)} %pad_maximum_fusion.3), channel_id=1, source_target_pairs={{0,24},{1,25},{2,26},{3,27},{4,28},{5,29},{6,30},{7,31},{8,0},{9,1... | collective-permute-start | bytes 368648 | tf_op jit(solution)/shard_map/qkv_z/ppermute | solution.py:43
  22.5 13.2 %collective-permute-done.3 = bf16[48,1280]{1,0:T(8,128)(2,1)S(1)} collective-permute-done((bf16[48,1280]{1,0:T(8,128)(2,1)S(1)}, bf16[48,1280]{1,0:T(8,128)(2,1)S(1)}, u32[]{:S(2)}, u32[]{:S(2)}) %collective-permute-start.3) | collective-permute-done | bytes 122912 | tf_op jit(solution)/shard_map/qkv_z/ppermute | solution.py:43
  39.1 3.1 collective-permute-done.7
  49.7 14.5 %collective-permute-done.8 = bf16[2,2,48,1280]{3,2,1,0:T(8,128)(2,1)S(1)} collective-permute-done((bf16[2,2,48,1280]{3,2,1,0:T(8,128)(2,1)S(1)}, bf16[2,2,48,1280]{3,2,1,0:T(8,128)(2,1)S(1)}, u32[]{:S(2)}, u32[]{:S(2)}) %collective-permute-start.8) | collective-permute-done | bytes 491552 | tf_op jit(solution)/shard_map/qkv_two/ppermute | solution.py:31
  65.3 3.4 %collective-permute-start.10 = (bf16[256,768]{0,1:T(8,128)(2,1)S(1)}, bf16[256,768]{0,1:T(8,128)(2,1)S(1)}, u32[]{:S(2)}, u32[]{:S(2)}) collective-permute-start(bf16[256,768]{0,1:T(8,128)(2,1)S(1)} %copy-done.7), channel_id=1, source_target_pairs={{0,4},{4,8},{8,12},{12,16},{16,20},{20,24},{24,28},{1,5},{5,9},{9,... | collective-permute-start | bytes 1179656 | tf_op jit(solution)/shard_map/ppermute | solution.py:47
  69.3 6.1 %keys.1 = (f32[256,768]{1,0:T(8,128)}, f32[256,768]{1,0:T(8,128)}, bf16[256,768]{1,0:T(8,128)(2,1)}, bf16[256,768]{1,0:T(8,128)(2,1)}, bf16[2,80,768]{2,1,0:T(8,128)(2,1)}, /*index=5*/f32[16,768]{1,0:T(8,128)}) custom-call(s32[2]{0:T(128)} %pad_add_fusion.c_ref, bf16[256,768]{1,0:T(8,128)(2,1)} %bitcast.161, bf16[768,1280]{1,0:T(8,128)(2,1)} %bitcast.144, ...), custom_call_target="tpu_custom_call" | custom-call | flops 5000000000 | bytes 5000000 | tf_op jit(solution)/shard_map/keys/pallas_call | solution.py:797
  77.8 5.2 %queries.1 = (f32[256,768]{1,0:T(8,128)}, f32[256,768]{1,0:T(8,128)}, bf16[256,768]{1,0:T(8,128)(2,1)}) custom-call(s32[2]{0:T(128)} %pad_add_fusion.c_ref, bf16[256,768]{1,0:T(8,128)(2,1)} %bitcast.162, bf16[768,1280]{1,0:T(8,128)(2,1)} %bitcast.145, bf16[768,1280]{1,0:T(8,128)(2,1)} %collective-permute-done.9.other, f32[16,768]{1,0:T(8,128)} %get-tuple-element.82.vec, ...), custom_call_target="tpu_custom_call" | custom-call | flops 3000000000 | bytes 3000000 | tf_op jit(solution)/shard_map/queries/pallas_call | solution.py:808
  84.5 5.7 %collective-permute-start.12 = (bf16[80,768]{1,0:T(8,128)(2,1)S(1)}, bf16[80,768]{1,0:T(8,128)(2,1)S(1)}, u32[]{:S(2)}, u32[]{:S(2)}) collective-permute-start(bf16[80,768]{1,0:T(8,128)(2,1)S(1)} %fusion.14), channel_id=1, source_target_pairs={{0,8},{1,9},{2,10},{3,11},{4,12},{5,13},{6,14},{7,15},{8,16},{9,17... | collective-permute-start | bytes 368648 | tf_op jit(solution)/shard_map/before_z/ppermute | solution.py:235
  90.2 4.4 %collective-permute-start.13 = (bf16[80,768]{1,0:T(8,128)(2,1)S(1)}, bf16[80,768]{1,0:T(8,128)(2,1)S(1)}, u32[]{:S(2)}, u32[]{:S(2)}) collective-permute-start(bf16[80,768]{1,0:T(8,128)(2,1)S(1)} %fusion.14), channel_id=1, source_target_pairs={{0,16},{1,17},{2,18},{3,19},{4,20},{5,21},{6,22},{7,23},{8,24},{9,... | collective-permute-start | bytes 368648 | tf_op jit(solution)/shard_map/before_z/ppermute | solution.py:235
  97.0 3.7 %collective-permute-done.13 = bf16[80,768]{1,0:T(8,128)(2,1)S(1)} collective-permute-done((bf16[80,768]{1,0:T(8,128)(2,1)S(1)}, bf16[80,768]{1,0:T(8,128)(2,1)S(1)}, u32[]{:S(2)}, u32[]{:S(2)}) %collective-permute-start.13) | collective-permute-done | bytes 122912 | tf_op jit(solution)/shard_map/before_z/ppermute | solution.py:235
  103.6 4.7 %halo.1 = (bf16[256,768]{1,0:T(8,128)(2,1)}, bf16[256,768]{1,0:T(8,128)(2,1)}) custom-call(s32[2]{0:T(128)} %pad_add_fusion.c_ref, bf16[256,768]{1,0:T(8,128)(2,1)} %copy.108.halo, bf16[768,1280]{1,0:T(8,128)(2,1)} %bitcast.147, bf16[768,1280]{1,0:T(8,128)(2,1)} %collective-permute-done.9.other, f32[16,768]{1,0:T(8,128)} %get-tuple-element.82.vec, ...), custom_call_target="tpu_custom_call" | custom-call | flops 2000000000 | bytes 2000000 | tf_op jit(solution)/shard_map/halo/pallas_call | solution.py:818
  114.9 6.9 %attention.1 = (bf16[256,768]{1,0:T(8,128)(2,1)}, bf16[768,256]{1,0:T(8,128)(2,1)}, f32[256,768]{1,0:T(8,128)}, f32[256,768]{1,0:T(8,128)}) custom-call(bf16[256,768]{1,0:T(8,128)(2,1)} %get-tuple-element.83.q, bf16[256,768]{1,0:T(8,128)(2,1)} %get-tuple-element.84.k, bf16[256,768]{1,0:T(8,128)(2,1)} %get-tuple-element.85.v, ...), custom_call_target="tpu_custom_call" | custom-call | flops 5000000000 | bytes 5000000 | tf_op jit(solution)/shard_map/attention/pallas_call | solution.py:840
  121.7 5.8 %all-gather.2.cloned.1.call-done.rest_hbm = bf16[3072,1728]{1,0:T(8,128)(2,1)} async-done(((bf16[96,1728]{1,0:T(8,128)(2,1)}), bf16[3072,1728]{1,0:T(8,128)(2,1)}) %all-gather.2.cloned.1.call-update) | async-done | bytes 10616848 | tf_op jit(solution)/shard_map/all_gather | solution.py:771
  135.5 16.1 %forward.1 = (f32[256,768]{1,0:T(8,128)}, f32[256,768]{1,0:T(8,128)}, bf16[256,3072]{1,0:T(8,128)(2,1)}, f32[256,768]{1,0:T(8,128)}, f32[256,128]{1,0:T(8,128)},...) custom-call(bf16[256,768]{1,0:T(8,128)(2,1)} %get-tuple-element.94.context, ...), custom_call_target="tpu_custom_call" | custom-call | flops 17999998976 | bytes 18000000 | tf_op jit(solution)/shard_map/forward/pallas_call | solution.py:855
  157.2 9.1 %middle.1 = (f32[256,768]{1,0:T(8,128)}, bf16[256,768]{1,0:T(8,128)(2,1)}, bf16[256,896]{1,0:T(8,128)(2,1)}, bf16[2,80,768]{2,1,0:T(8,128)(2,1)}, f32[8,768]{1,0:T(8,128)}, /*index=5*/f32[8,768]{1,0:T(8,128)}) custom-call(f32[256,768]{1,0:T(8,128)} %get-tuple-element.100.dlower, bf16[256,3072]{1,0:T(8,128)(2,1)} %get-tuple-element.101.du, ...), custom_call_target="tpu_custom_call" | custom-call | flops 7000000000 | bytes 7000000 | tf_op jit(solution)/shard_map/middle/pallas_call | solution.py:892
  169.5 3.3 collective-permute-done.17
  176.8 16.9 %query_back.1 = (bf16[256,768]{1,0:T(8,128)(2,1)}, bf16[768,768]{1,0:T(8,128)(2,1)}, bf16[768,768]{1,0:T(8,128)(2,1)}, f32[6,8,256]{2,1,0:T(8,128)}, f32[8,768]{1,0:T(8,128)}) custom-call(s32[2]{0:T(128)} %pad_add_fusion.c_ref, bf16[768,256]{1,0:T(8,128)(2,1)} %bitcast.165, bf16[768,256]{1,0:T(8,128)(2,1)} %get-tuple-element.109.context, ...), custom_call_target="tpu_custom_call" | custom-call | flops 11000000512 | bytes 11000000 | tf_op jit(solution)/shard_map/query_back/pallas_call | solution.py:917
  200.3 16.1 %key_back.1 = (bf16[256,768]{1,0:T(8,128)(2,1)}, bf16[256,768]{1,0:T(8,128)(2,1)}, bf16[768,768]{1,0:T(8,128)(2,1)}, bf16[768,768]{1,0:T(8,128)(2,1)}, bf16[768,128]{1,0:T(8,128)(2,1)}) custom-call(s32[2]{0:T(128)} %pad_add_fusion.c_ref, bf16[768,256]{1,0:T(8,128)(2,1)} %bitcast.166, bf16[256,768]{1,0:T(8,128)(2,1)} %get-tuple-element.83.q, ...), custom_call_target="tpu_custom_call" | custom-call | flops 12000000000 | bytes 12000000 | tf_op jit(solution)/shard_map/key_back/pallas_call | solution.py:940
  224.5 21.7 %collective-permute-done.28 = bf16[2,2,48,1664]{3,2,0,1:T(8,128)(2,1)} collective-permute-done((bf16[2,2,48,1664]{3,2,0,1:T(8,128)(2,1)S(1)}, bf16[2,2,48,1664]{3,2,0,1:T(8,128)(2,1)}, u32[]{:S(2)}, u32[]{:S(2)}) %collective-permute-start.28) | collective-permute-done | bytes 639008 | tf_op jit(solution)/shard_map/d_qkv_one/ppermute | solution.py:31
  252.4 5.2 %tokens.1 = f32[256,768]{1,0:T(8,128)} custom-call(s32[2]{0:T(128)} %pad_add_fusion.c_ref, f32[256,768]{1,0:T(8,128)} %get-tuple-element.106.dresid, bf16[256,768]{1,0:T(8,128)(2,1)} %get-tuple-element.115.dq, bf16[256,768]{1,0:T(8,128)(2,1)} %get-tuple-element.127.dk, bf16[256,768]{1,0:T(8,128)(2,1)} %get-tuple-element.128.dv, bf16[768,1280]{1,0:T(8,128)(2,1)} %bitcast.148, ...), custom_call_target="tpu_custom_call" | custom-call | flops 3000000000 | bytes 3000000 | tf_op jit(solution)/shard_map/tokens/pallas_call | solution.py:966
  257.7 7.3 %collective-permute-done.31 = bf16[2,48,1664]{2,1,0:T(8,128)(2,1)S(1)} collective-permute-done((bf16[2,48,1664]{2,1,0:T(8,128)(2,1)S(1)}, bf16[2,48,1664]{2,1,0:T(8,128)(2,1)S(1)}, u32[]{:S(2)}, u32[]{:S(2)}) %collective-permute-start.31) | collective-permute-done | bytes 319520 | tf_op jit(solution)/shard_map/d_qkv_two/ppermute | solution.py:31
  273.9 3.8 %collective-permute-done.38 = f32[12,129]{1,0:T(8,128)S(1)} collective-permute-done((f32[12,129]{1,0:T(8,128)S(1)}, f32[12,129]{1,0:T(8,128)S(1)}, u32[]{:S(2)}, u32[]{:S(2)}) %collective-permute-start.38) | collective-permute-done | bytes 6224 | tf_op jit(solution)/shard_map/everywhere/ppermute | solution.py:43
  277.8 11.0 %collective-permute-done.34 = bf16[48,1664]{1,0:T(8,128)(2,1)S(1)} collective-permute-done((bf16[48,1664]{1,0:T(8,128)(2,1)S(1)}, bf16[48,1664]{1,0:T(8,128)(2,1)S(1)}, u32[]{:S(2)}, u32[]{:S(2)}) %collective-permute-start.34) | collective-permute-done | bytes 159776 | tf_op jit(solution)/shard_map/d_qkv_z/ppermute | solution.py:43
  292.1 25.8 %reduce-scatter.2.cloned.1.call-done.packed = bf16[96,1536]{1,0:T(8,128)(2,1)} async-done(((bf16[3072,1536]{1,0:T(8,128)(2,1)}), bf16[96,1536]{1,0:T(8,128)(2,1)}) %reduce-scatter.2.cloned.1.call-update) | async-done | bytes 294928 | tf_op jit(solution)/shard_map/reduce_scatter | solution.py:878
  (258 shorter events, 93.4 us)
Async XLA Ops:
  7.3 120.3 %all-gather.2.cloned.1.call-start = ((), (), s32[]{:S(2)}) async-start(), calls=%async_computation.1 | async-start | bytes 11354112 | tf_op jit(solution)/shard_map/all_gather | solution.py:771
  10.8 307.1 %reduce-scatter.2.cloned.1.call-start = ((), (), s32[]{:S(2)}) async-start(), calls=%async_computation.2 | async-start | bytes 9732096 | tf_op jit(solution)/shard_map/reduce_scatter | solution.py:878
  18.8 16.9 %collective-permute-start.3 = (bf16[48,1280]{1,0:T(8,128)(2,1)S(1)}, bf16[48,1280]{1,0:T(8,128)(2,1)S(1)}, u32[]{:S(2)}, u32[]{:S(2)}) collective-permute-start(bf16[48,1280]{1,0:T(8,128)(2,1)S(1)} %pad_maximum_fusion.3), channel_id=1, source_target_pairs={{0,16},{1,17},{2,18},{3,19},{4,20},{5,21},{6,22},{7,23},{8,24},{9,... | collective-permute-start | bytes 368648 | tf_op jit(solution)/shard_map/qkv_z/ppermute | solution.py:43
  18.9 16.8 %collective-permute-start.4 = (bf16[48,1280]{1,0:T(8,128)(2,1)S(1)}, bf16[48,1280]{1,0:T(8,128)(2,1)S(1)}, u32[]{:S(2)}, u32[]{:S(2)}) collective-permute-start(bf16[48,1280]{1,0:T(8,128)(2,1)S(1)} %pad_maximum_fusion.3), channel_id=1, source_target_pairs={{0,8},{1,9},{2,10},{3,11},{4,12},{5,13},{6,14},{7,15},{8,16},{9,17... | collective-permute-start | bytes 368648 | tf_op jit(solution)/shard_map/qkv_z/ppermute | solution.py:43
  42.2 22.0 %collective-permute-start.8 = (bf16[2,2,48,1280]{3,2,1,0:T(8,128)(2,1)S(1)}, bf16[2,2,48,1280]{3,2,1,0:T(8,128)(2,1)S(1)}, u32[]{:S(2)}, u32[]{:S(2)}) collective-permute-start(bf16[2,2,48,1280]{3,2,1,0:T(8,128)(2,1)S(1)} %maximum_select_fusion.3), channel_id=1, source_target_pairs={{0,4},{1,5},{2,6},{3,7},{4,0},{5,1},{6,2},{7,3},{8,12},{9,13},{10,... | collective-permute-start | bytes 1474568 | tf_op jit(solution)/shard_map/qkv_two/ppermute | solution.py:31
  45.7 18.6 %collective-permute-start.6 = (bf16[2,2,48,1280]{3,2,0,1:T(8,128)(2,1)S(1)}, bf16[2,2,48,1280]{3,2,0,1:T(8,128)(2,1)S(1)}, u32[]{:S(2)}, u32[]{:S(2)}) collective-permute-start(bf16[2,2,48,1280]{3,2,0,1:T(8,128)(2,1)S(1)} %maximum_select_fusion.2), channel_id=1, source_target_pairs={{0,2},{1,3},{2,0},{3,1},{4,6},{5,7},{6,4},{7,5},{8,10},{9,11},{10,... | collective-permute-start | bytes 1474568 | tf_op jit(solution)/shard_map/qkv_two/ppermute | solution.py:31
  65.3 31.7 %collective-permute-start.10 = (bf16[256,768]{0,1:T(8,128)(2,1)S(1)}, bf16[256,768]{0,1:T(8,128)(2,1)S(1)}, u32[]{:S(2)}, u32[]{:S(2)}) collective-permute-start(bf16[256,768]{0,1:T(8,128)(2,1)S(1)} %copy-done.7), channel_id=1, source_target_pairs={{0,4},{4,8},{8,12},{12,16},{16,20},{20,24},{24,28},{1,5},{5,9},{9,... | collective-permute-start | bytes 1179656 | tf_op jit(solution)/shard_map/ppermute | solution.py:47
  83.1 25.5 %collective-permute-start.15 = (bf16[256,768]{1,0:T(8,128)(2,1)}, bf16[256,768]{1,0:T(8,128)(2,1)S(1)}, u32[]{:S(2)}, u32[]{:S(2)}) collective-permute-start(bf16[256,768]{1,0:T(8,128)(2,1)} %get-tuple-element.83.q), channel_id=1, source_target_pairs={{4,0},{8,4},{12,8},{16,12},{20,16},{24,20},{28,24},{5,1},{9,5},{13... | collective-permute-start | bytes 1179656 | tf_op jit(solution)/shard_map/ppermute | solution.py:47
  84.5 12.5 %collective-permute-start.12 = (bf16[80,768]{1,0:T(8,128)(2,1)S(1)}, bf16[80,768]{1,0:T(8,128)(2,1)S(1)}, u32[]{:S(2)}, u32[]{:S(2)}) collective-permute-start(bf16[80,768]{1,0:T(8,128)(2,1)S(1)} %fusion.14), channel_id=1, source_target_pairs={{0,8},{1,9},{2,10},{3,11},{4,12},{5,13},{6,14},{7,15},{8,16},{9,17... | collective-permute-start | bytes 368648 | tf_op jit(solution)/shard_map/before_z/ppermute | solution.py:235
  90.2 10.5 %collective-permute-start.13 = (bf16[80,768]{1,0:T(8,128)(2,1)S(1)}, bf16[80,768]{1,0:T(8,128)(2,1)S(1)}, u32[]{:S(2)}, u32[]{:S(2)}) collective-permute-start(bf16[80,768]{1,0:T(8,128)(2,1)S(1)} %fusion.14), channel_id=1, source_target_pairs={{0,16},{1,17},{2,18},{3,19},{4,20},{5,21},{6,22},{7,23},{8,24},{9,... | collective-permute-start | bytes 368648 | tf_op jit(solution)/shard_map/before_z/ppermute | solution.py:235
  168.2 26.2 %collective-permute-start.19 = (bf16[256,896]{1,0:T(8,128)(2,1)S(1)}, bf16[256,896]{1,0:T(8,128)(2,1)S(1)}, u32[]{:S(2)}, u32[]{:S(2)}) collective-permute-start(bf16[256,896]{1,0:T(8,128)(2,1)S(1)} %copy-done.32), channel_id=1, source_target_pairs={{4,0},{8,4},{12,8},{16,12},{20,16},{24,20},{28,24},{5,1},{9,5},{13... | collective-permute-start | bytes 1376264 | tf_op jit(solution)/shard_map/ppermute | solution.py:47
  172.8 21.6 %collective-permute-start.20 = (bf16[80,768]{1,0:T(8,128)(2,1)S(1)}, bf16[80,768]{1,0:T(8,128)(2,1)S(1)}, u32[]{:S(2)}, u32[]{:S(2)}) collective-permute-start(bf16[80,768]{1,0:T(8,128)(2,1)S(1)} %fusion.17), channel_id=1, source_target_pairs={{8,0},{9,1},{10,2},{11,3},{12,4},{13,5},{14,6},{15,7},{16,8},{17,9... | collective-permute-start | bytes 368648 | tf_op jit(solution)/shard_map/later_z/ppermute | solution.py:235
  174.1 20.4 %collective-permute-start.21 = (bf16[80,768]{1,0:T(8,128)(2,1)S(1)}, bf16[80,768]{1,0:T(8,128)(2,1)S(1)}, u32[]{:S(2)}, u32[]{:S(2)}) collective-permute-start(bf16[80,768]{1,0:T(8,128)(2,1)S(1)} %fusion.17), channel_id=1, source_target_pairs={{16,0},{17,1},{18,2},{19,3},{20,4},{21,5},{22,6},{23,7},{24,8},{25... | collective-permute-start | bytes 368648 | tf_op jit(solution)/shard_map/later_z/ppermute | solution.py:235
  175.4 19.1 %collective-permute-start.22 = (bf16[80,768]{1,0:T(8,128)(2,1)S(1)}, bf16[80,768]{1,0:T(8,128)(2,1)S(1)}, u32[]{:S(2)}, u32[]{:S(2)}) collective-permute-start(bf16[80,768]{1,0:T(8,128)(2,1)S(1)} %fusion.17), channel_id=1, source_target_pairs={{24,0},{25,1},{26,2},{27,3},{28,4},{29,5},{30,6},{31,7}} | collective-permute-start | bytes 368648 | tf_op jit(solution)/shard_map/later_z/ppermute | solution.py:235
  197.7 22.9 %collective-permute-start.24 = (bf16[768,768]{1,0:T(8,128)(2,1)}, bf16[768,768]{1,0:T(8,128)(2,1)S(1)}, u32[]{:S(2)}, u32[]{:S(2)}) collective-permute-start(bf16[768,768]{1,0:T(8,128)(2,1)} %get-tuple-element.130), channel_id=1, source_target_pairs={{0,1},{1,0},{2,3},{3,2},{4,5},{5,4},{6,7},{7,6},{8,9},{9,8},{10,11... | collective-permute-start | bytes 3538952 | tf_op jit(solution)/shard_map/d_qkv_core/ppermute | solution.py:31
  222.7 23.4 %collective-permute-start.28 = (bf16[2,2,48,1664]{3,2,0,1:T(8,128)(2,1)S(1)}, bf16[2,2,48,1664]{3,2,0,1:T(8,128)(2,1)}, u32[]{:S(2)}, u32[]{:S(2)}) collective-permute-start(bf16[2,2,48,1664]{3,2,0,1:T(8,128)(2,1)S(1)} %copy_bitcast_fusion), channel_id=1, source_target_pairs={{0,2},{1,3},{2,0},{3,1},{4,6},{5,7},{6,4},{7,5},{8,10},{9,11},{10,... | collective-permute-start | bytes 1916936 | tf_op jit(solution)/shard_map/d_qkv_one/ppermute | solution.py:31
  223.9 22.2 %collective-permute-start.29 = (bf16[2,2,48,1664]{3,2,1,0:T(8,128)(2,1)}, bf16[2,2,48,1664]{3,2,1,0:T(8,128)(2,1)}, u32[]{:S(2)}, u32[]{:S(2)}) collective-permute-start(bf16[2,2,48,1664]{3,2,1,0:T(8,128)(2,1)} %dynamic-slice_bitcast_fusion), channel_id=1, source_target_pairs={{0,4},{1,5},{2,6},{3,7},{4,0},{5,1},{6,2},{7,3},{8,12},{9,13},{10,... | collective-permute-start | bytes 1916936 | tf_op jit(solution)/shard_map/d_qkv_one/ppermute | solution.py:31
  250.1 14.9 %collective-permute-start.31 = (bf16[2,48,1664]{2,1,0:T(8,128)(2,1)S(1)}, bf16[2,48,1664]{2,1,0:T(8,128)(2,1)S(1)}, u32[]{:S(2)}, u32[]{:S(2)}) collective-permute-start(bf16[2,48,1664]{2,1,0:T(8,128)(2,1)S(1)} %dynamic-slice_bitcast_fusion.2), channel_id=1, source_target_pairs={{0,4},{1,5},{2,6},{3,7},{4,0},{5,1},{6,2},{7,3},{8,12},{9,13},{10,... | collective-permute-start | bytes 958472 | tf_op jit(solution)/shard_map/d_qkv_two/ppermute | solution.py:31
  251.5 13.5 %collective-permute-start.32 = (bf16[2,48,1664]{2,1,0:T(8,128)(2,1)S(1)}, bf16[2,48,1664]{2,1,0:T(8,128)(2,1)S(1)}, u32[]{:S(2)}, u32[]{:S(2)}) collective-permute-start(bf16[2,48,1664]{2,1,0:T(8,128)(2,1)S(1)} %dynamic-slice_bitcast_fusion.1), channel_id=1, source_target_pairs={{0,2},{1,3},{2,0},{3,1},{4,6},{5,7},{6,4},{7,5},{8,10},{9,11},{10,... | collective-permute-start | bytes 958472 | tf_op jit(solution)/shard_map/d_qkv_two/ppermute | solution.py:31
  267.5 10.2 %collective-permute-start.38 = (f32[12,129]{1,0:T(8,128)S(1)}, f32[12,129]{1,0:T(8,128)S(1)}, u32[]{:S(2)}, u32[]{:S(2)}) collective-permute-start(f32[12,129]{1,0:T(8,128)S(1)} %add.228), channel_id=1, source_target_pairs={{0,16},{1,17},{2,18},{3,19},{4,20},{5,21},{6,22},{7,23},{8,24},{9,... | collective-permute-start | bytes 18584 | tf_op jit(solution)/shard_map/everywhere/ppermute | solution.py:43
  267.5 10.2 %collective-permute-start.39 = (f32[12,129]{1,0:T(8,128)S(1)}, f32[12,129]{1,0:T(8,128)S(1)}, u32[]{:S(2)}, u32[]{:S(2)}) collective-permute-start(f32[12,129]{1,0:T(8,128)S(1)} %add.228), channel_id=1, source_target_pairs={{0,8},{1,9},{2,10},{3,11},{4,12},{5,13},{6,14},{7,15},{8,16},{9,17... | collective-permute-start | bytes 18584 | tf_op jit(solution)/shard_map/everywhere/ppermute | solution.py:43
  268.4 9.3 %collective-permute-start.33 = (bf16[48,1664]{1,0:T(8,128)(2,1)S(1)}, bf16[48,1664]{1,0:T(8,128)(2,1)S(1)}, u32[]{:S(2)}, u32[]{:S(2)}) collective-permute-start(bf16[48,1664]{1,0:T(8,128)(2,1)S(1)} %get-tuple-element.158), channel_id=1, source_target_pairs={{0,8},{1,9},{2,10},{3,11},{4,12},{5,13},{6,14},{7,15},{8,16},{9,17... | collective-permute-start | bytes 479240 | tf_op jit(solution)/shard_map/d_qkv_z/ppermute | solution.py:43
  271.4 17.4 %collective-permute-start.34 = (bf16[48,1664]{1,0:T(8,128)(2,1)S(1)}, bf16[48,1664]{1,0:T(8,128)(2,1)S(1)}, u32[]{:S(2)}, u32[]{:S(2)}) collective-permute-start(bf16[48,1664]{1,0:T(8,128)(2,1)S(1)} %get-tuple-element.160), channel_id=1, source_target_pairs={{0,16},{1,17},{2,18},{3,19},{4,20},{5,21},{6,22},{7,23},{8,24},{9,... | collective-permute-start | bytes 479240 | tf_op jit(solution)/shard_map/d_qkv_z/ppermute | solution.py:43
  272.3 16.5 %collective-permute-start.35 = (bf16[48,1664]{1,0:T(8,128)(2,1)S(1)}, bf16[48,1664]{1,0:T(8,128)(2,1)S(1)}, u32[]{:S(2)}, u32[]{:S(2)}) collective-permute-start(bf16[48,1664]{1,0:T(8,128)(2,1)S(1)} %get-tuple-element.159), channel_id=1, source_target_pairs={{0,24},{1,25},{2,26},{3,27},{4,28},{5,29},{6,30},{7,31},{8,0},{9,1... | collective-permute-start | bytes 479240 | tf_op jit(solution)/shard_map/d_qkv_z/ppermute | solution.py:43
  (53 other events, 449.1 us)
Sparse Core Ops, SparseCore 0:
  11.1 116.4 all-gather.1
  167.5 150.3 reduce-scatter.1

commit v3 on v2

--- a/solution.py
+++ b/solution.py
@@ -462,45 +462,47 @@
     return jnp.sum(a, axis=0, keepdims=True)
 
 
-def forward_kernel(
-    context, tok, cot, vec, bu, wu_hbm, wo_hbm, rest_hbm,
-    out, dlower_out, du_out, xhat_out, rstd_out, sums_out, du_sums_out, down_hbm, up_hbm,
-    wu, wo, wd, gp, grads, in_sems, out_sems,
+def middle_kernel(
+    count, context, tok, cot, vec, bu, ratio, denom, q, state, far, rest_hbm, *more,
 ):
-    count, width, step = wu.shape
-    loads = [pltpu.make_async_copy(wo_hbm, wo, in_sems.at[2 * count])]
+    blocks_hbm, more = more[:count], more[count:]
+    (
+        out, dresid_out, dattn_out, dn_out, later_out, sums_out, near_out, du_sums_out, down_hbm, up_hbm,
+        w, wd, gp, grads, in_sems, out_sems,
+    ) = more
+    width, step = tok.shape[1], wd.shape[1]
+    hw = width // 2
+    loads = []
     for i in range(count):
-        loads.append(pltpu.make_async_copy(wu_hbm.at[i], wu.at[i], in_sems.at[i]))
+        loads.append(pltpu.make_async_copy(blocks_hbm[i], w.at[i], in_sems.at[i]))
+    for i in range(count):
         wd_block = rest_hbm.at[pl.ds(i * step, step), pl.ds(0, width)]
         loads.append(pltpu.make_async_copy(wd_block, wd.at[i], in_sems.at[count + i]))
     for load in loads:
         load.start()
-    loads[0].wait()
-    attn = jnp.concatenate([dot(context[...], wo[i]) for i in range(count)], axis=1)
+    for load in loads[:count]:
+        load.wait()
+    attn = jnp.concatenate([dot(context[...], w[i, :, step:]) for i in range(count)], axis=1)
     xhat, rstd = normed(tok[...].astype(F32) + attn + vec[3:4])
     hidden = xhat * vec[4:5] + vec[5:6]
-    xhat_out[...] = xhat
-    rstd_out[...] = jnp.broadcast_to(rstd, rstd_out.shape)
     h_low = hidden.astype(BF)
     lower = hidden + vec[6:7]
     actives = []
     for i in range(count):
         cols = slice(i * step, (i + 1) * step)
-        loads[1 + 2 * i].wait()
-        upper = dot(h_low, wu[i]) + bu[:, cols]
+        upper = dot(h_low, w[i, :, :step]) + bu[:, cols]
         cdf = 0.5 * (1.0 + lax.erf(upper * 2.0 ** (-0.5)))
         pdf = jnp.exp(-0.5 * upper * upper) * (2.0 * math.pi) ** (-0.5)
         gp[:, cols] = (cdf + upper * pdf).astype(BF)
         actives.append((upper * cdf).astype(BF))
-        loads[2 + 2 * i].wait()
+        loads[count + i].wait()
         lower = lower + dot(actives[-1], wd[i])
     xhat2, rstd2 = normed(lower)
     gain2 = vec[7:8]
     out[...] = xhat2 * gain2 + vec[8:9]
     dy = cot[...].astype(F32)
-    d_lower = norm_back(dy, xhat2, rstd2, gain2)
-    dlower_out[...] = d_lower
-    d_low = d_lower.astype(BF)
+    d_hidden = norm_back(dy, xhat2, rstd2, gain2)
+    d_low = d_hidden.astype(BF)
     sums_out[0:1] = col_sums(d_low.astype(F32))
     sums_out[1:2] = col_sums(dy * xhat2)
     sums_out[2:3] = col_sums(dy)
@@ -508,8 +510,8 @@
     for i in range(count):
         cols = slice(i * step, (i + 1) * step)
         d_upper = (dot_t(d_low, wd[i]) * gp[:, cols].astype(F32)).astype(BF)
-        du_out[:, cols] = d_upper
         du_sums_out[:, cols] = jnp.broadcast_to(col_sums(d_upper.astype(F32)), (8, step))
+        d_hidden = d_hidden + dot_t(d_upper, w[i, :, :step])
         grads[2 * i] = tdot(h_low, d_upper).astype(BF)
         stores.append(pltpu.make_async_copy(grads.at[2 * i], up_hbm.at[i], out_sems.at[2 * i]))
         stores[-1].start()
@@ -517,36 +519,16 @@
         block = down_hbm.at[pl.ds(i * step, step), pl.ds(0, width)]
         stores.append(pltpu.make_async_copy(grads.at[2 * i + 1], block, out_sems.at[2 * i + 1]))
         stores[-1].start()
-    for store in stores:
-        store.wait()
-
-
-def middle_kernel(
-    dlower, du, xhat, rstd, wu_hbm, wo, vec, ratio, denom, q, state, far,
-    dresid_out, dattn_out, dn_out, later_out, sums_out, near_out,
-    wu, sems,
-):
-    hw = dlower.shape[1] // 2
-    d_hidden = dlower[...]
-    step = wu.shape[2]
-    loads = [pltpu.make_async_copy(wu_hbm.at[i], wu.at[i], sems.at[i]) for i in range(wu.shape[0])]
-    for load in loads:
-        load.start()
-    for i in range(wu.shape[0]):
-        loads[i].wait()
-        d_hidden = d_hidden + dot_t(du[:, i * step : (i + 1) * step], wu[i])
-    xh = xhat[...]
-    d_resid = norm_back(d_hidden, xh, rstd[:, 0:1], vec[4:5])
+    d_resid = norm_back(d_hidden, xhat, rstd, vec[4:5])
     dresid_out[...] = d_resid
     d_attn = d_resid.astype(BF)
     dattn_out[...] = d_attn
-    sums_out[0:1] = col_sums(d_attn.astype(F32))
-    sums_out[1:2] = col_sums(d_hidden * xh)
-    sums_out[2:3] = col_sums(d_hidden)
-    step = wo.shape[2]
-    d_context = sum(dot_t(d_resid[:, i * step : (i + 1) * step].astype(BF), wo[i]) for i in range(wo.shape[0]))
+    sums_out[3:4] = col_sums(d_attn.astype(F32))
+    sums_out[4:5] = col_sums(d_hidden * xhat)
+    sums_out[5:6] = col_sums(d_hidden)
+    part = width // count
+    d_context = sum(dot_t(d_resid[:, i * part : (i + 1) * part].astype(BF), w[i, :, step:]) for i in range(count))
     ones = head_ones()
-    width = 2 * hw
     pick = jnp.where(
         lax.broadcasted_iota(jnp.int32, (width, 128), 0) == 64 * lax.broadcasted_iota(jnp.int32, (width, 128), 1), 1.0, 0.0
     ).astype(BF)
@@ -559,7 +541,7 @@
         dn_out[:, lanes(p)] = dn
         all_denoms.append(dd)
         near = jnp.zeros((1, 128), F32)
-        for r in range(dlower.shape[0] // 128):
+        for r in range(tok.shape[0] // 128):
             rows = slice(r * 128, (r + 1) * 128)
             qr = q[rows, lanes(p)]
             packed = fold(tdot(qr, dn[rows]))
@@ -571,6 +553,8 @@
             near = near + col_sums(held[:64] * packed) + held[64:65] * total
         near_out[:, lanes(p)] = jnp.broadcast_to(near, (8, 128))
     dn_out[:, width:] = dot(jnp.concatenate(all_denoms, axis=1), pick).astype(BF)
+    for store in stores:
+        store.wait()
 
 
 def spread(dn, p):
@@ -849,30 +833,28 @@
     )(q, k, v, hk, hv, table, before, far)
 
     split = rest.reshape(at.n, slices, own, rest.shape[1])
-    wu = jnp.swapaxes(split[..., width : width + step], 0, 1).reshape(slices, width, step)
-    wo = jnp.swapaxes(split[..., width + step :], 0, 1).reshape(slices, width, wo_step)
+    blocks = [split[:, i, :, width:].reshape(width, step + wo_step) for i in range(slices)]
     away = pl.BlockSpec(memory_space=pl.ANY)
-    out, d_lower, du, xhat, rstd, sums3, du_sums, g_down, g_up = pl.pallas_call(
-        forward_kernel,
+    out, d_resid, d_attn, dn, local, sums2, near, du_sums, g_down, g_up = pl.pallas_call(
+        functools.partial(middle_kernel, slices),
         out_shape=(
-            wide32, wide32, arr((n, ff), BF), wide32, arr((n, 128), F32), arr((8, width), F32), arr((8, ff), F32),
-            arr((ff, width + step), BF), arr((slices, width, step), BF),
+            wide32, wide32, wide16, arr((n, width + 128), BF), sums, arr((8, width), F32), arr((8, width), F32),
+            arr((8, ff), F32), arr((ff, width + step), BF), arr((slices, width, step), BF),
         ),
-        in_specs=[WHOLE] * 5 + [away] * 3,
-        out_specs=(WHOLE,) * 7 + (away,) * 2,
+        in_specs=[WHOLE] * 10 + [away] * (1 + slices),
+        out_specs=(WHOLE,) * 8 + (away,) * 2,
         scratch_shapes=[
-            VMEM((slices, width, step), BF),
-            VMEM((slices, width, wo_step), BF),
+            VMEM((slices, width, step + wo_step), BF),
             VMEM((slices, step, width), BF),
             VMEM((n, ff), BF),
             VMEM((2 * slices, width, step), BF),
-            pltpu.SemaphoreType.DMA((2 * slices + 1,)),
+            pltpu.SemaphoreType.DMA((2 * slices,)),
             pltpu.SemaphoreType.DMA((2 * slices,)),
         ],
         compiler_params=params(56),
-        cost_estimate=cost(18),
-        name="forward",
-    )(context, tok, cot, vec, b_u, wu, wo, rest)
+        cost_estimate=cost(20),
+        name="middle",
+    )(context, tok, cot, vec, b_u, ratio, denom, q, before, far, rest, *blocks)
     g_up = jnp.swapaxes(g_up.reshape(slices, at.n, own, step), 0, 1).reshape(ff, step)
     g_rest = lax.dynamic_update_slice(g_down, g_up, (0, width))
     s_rest = lax.psum_scatter(g_rest, BOTH, scatter_dimension=0, tiled=True)
@@ -889,16 +871,6 @@
     else:
         s_d = s_rest[:, :width].astype(F32)
         s_u = jnp.concatenate(jnp.split(s_rest[:, width:].astype(F32), slices, axis=0), axis=1)
-    d_resid, d_attn, dn, local, sums2, near = pl.pallas_call(
-        middle_kernel,
-        out_shape=(wide32, wide16, arr((n, width + 128), BF), sums, arr((8, width), F32), arr((8, width), F32)),
-        in_specs=[WHOLE] * 4 + [away] + [WHOLE] * 7,
-        out_specs=(WHOLE,) * 6,
-        scratch_shapes=[VMEM((slices, width, step), BF), pltpu.SemaphoreType.DMA((slices,))],
-        compiler_params=params(48),
-        cost_estimate=cost(7),
-        name="middle",
-    )(after(d_lower, g_rest), du, xhat, rstd, wu, wo, vec, ratio, denom, q, before, far)
     scan = Before(at, "later", local, True)
     scan.step_beside()
     dn_next = at.along(dn, -1)
@@ -925,9 +897,9 @@
         ),
         out_shape=(wide16, half, half, arr((pairs, 8, 256), F32), arr((8, width), F32)),
         compiler_params=params(32),
-        cost_estimate=cost(11),
+        cost_estimate=cost(0.001),
         name="query_back",
-    )(flags, after(tok_t, *scan.done), context_t, d_attn, q, k, v, hk, hv, dn, dn, table, before, far, q_phi, sq, gh, gl, near)
+    )(flags, after(tok_t, *scan.done, g_rest), context_t, d_attn, q, k, v, hk, hv, dn, dn, table, before, far, q_phi, sq, gh, gl, near)
     scan.step_z()
     later = scan.step_last(dq, dn_next)
     everywhere = Everywhere(at, exp_bias * pos[:, :2, : window + 1].reshape(heads, window + 1))
@@ -935,7 +907,7 @@
     du = du_sums[0].reshape(at.n, up_own, own)
     du = jnp.swapaxes(du, 0, 1).reshape(up_own, width)
     nil = jnp.zeros((2, width), F32)
-    early = jnp.concatenate([sums_q[:1], nil, sums2[:3], sums3[:3], du], axis=0)
+    early = jnp.concatenate([sums_q[:1], nil, sums2[3:6], sums2[:3], du], axis=0)
     early = jnp.pad(early, ((0, 16 - early.shape[0]), (0, 0)))
     dk, dv, keep0, send0, small = pl.pallas_call(
         key_back_kernel,
@@ -949,7 +921,7 @@
         ),
         out_shape=(wide16, wide16, half, half, arr((width, 128), BF)),
         compiler_params=params(32),
-        cost_estimate=cost(12),
+        cost_estimate=cost(0.001),
         name="key_back",
     )(flags, after(tok_t, *everywhere.done), q, k, v, dn, dn, q_next, dn_next, dn_next, table, later, k_phi, sk, gh, gl, early)
 
@@ -969,7 +941,7 @@
         in_specs=[SCALAR] + [WHOLE] * 6,
         out_specs=WHOLE,
         compiler_params=params(40),
-        cost_estimate=cost(3),
+        cost_estimate=cost(0.001),
         name="tokens",
     )(flags, d_resid, dq, dk, dv, m1, o1)
 

time: 328 us -> 322 us (0.982)
  Pallas kernels: 88.1 us -> 81.1 us
  waiting for transfers between devices: 125 us -> 131 us
  local copies, waits for them, and re-layouts: 32.7 us -> 29 us
    pallas_call x2 -> x1, Pallas kernels: 25.2 us -> 18.8 us  [on_device(): pl.pallas_call(functools.partial(middle_kernel, slices), out_shape=(wide3...]
    ppermute x22, waiting for transfers between devices: 57.4 us -> 63 us  [flip(): return lax.ppermute(a, BOTH, [(d, d ^ stride) for d in range(self.n)])]
    unnamed x93 -> x83, local copies, waits for them, and re-layouts: 6.22 us -> 1.93 us
  transfers between devices with their start and end apart: 42 -> 42, of which waited for: 20 -> 25; matrix products, arithmetic and copies ran while one was open for 8% -> 9% of each run, Pallas kernels for 19% -> 19%
where the time goes in v3:
time: 322 us; the launch traced here: 321 us
  waiting for transfers between devices  131 us (41%)
  Pallas kernels  81.1 us (25%)
  starting transfers between devices  51.7 us (16%)
  local copies, waits for them, and re-layouts  29 us (9%)
  between operations  15.2 us (5%)
  other arithmetic  13.2 us (4%)
    ppermute x22, waiting for transfers between devices, flip(): return lax.ppermute(a, BOTH, [(d, d ^ stride) for d in range(self.n)])  63 us
    ppermute x9, waiting for transfers between devices, turn_z(): lax.ppermute(a, BOTH, [(d, (d + 8 * by) % self.n) for d in range(self.n)])  31.4 us
    reduce_scatter x1, waiting for transfers between devices, on_device(): s_rest = lax.psum_scatter(g_rest, BOTH, scatter_dimension=0, tiled=True)  25.1 us
    pallas_call x1, Pallas kernels, on_device(): pl.pallas_call(functools.partial(middle_kernel, slices), out_shape=(wide3...  18.8 us
    ppermute x22, starting transfers between devices, flip(): return lax.ppermute(a, BOTH, [(d, d ^ stride) for d in range(self.n)])  17 us
    pallas_call x1, Pallas kernels, on_device(): pl.pallas_call(query_back_kernel, grid_spec=pltpu.PrefetchScalarGridSpec(...  16.6 us
    pallas_call x1, Pallas kernels, on_device(): pl.pallas_call(key_back_kernel, grid_spec=pltpu.PrefetchScalarGridSpec(nu...  16.1 us
    ppermute x6, starting transfers between devices, step_z(): got.append(lax.ppermute(pair, BOTH, pairs))  14.3 us
  transfers between devices with their start and end apart: 42, of which 25 were waited for; matrix products, arithmetic and copies ran while one was open for 9% of the time, Pallas kernels for 19%

profile of v3, /device:TPU:0, one launch (start us, length us, event | category | flops | bytes accessed | tf_op | source)
XLA Modules:
  0.0 320.9 jit_solution(8680914601177523086)
XLA Ops:
  13.9 4.8 %collective-permute-start.2 = (bf16[48,1280]{1,0:T(8,128)(2,1)S(1)}, bf16[48,1280]{1,0:T(8,128)(2,1)S(1)}, u32[]{:S(2)}, u32[]{:S(2)}) collective-permute-start(bf16[48,1280]{1,0:T(8,128)(2,1)S(1)} %pad_maximum_fusion.3), channel_id=1, source_target_pairs={{0,24},{1,25},{2,26},{3,27},{4,28},{5,29},{6,30},{7,31},{8,0},{9,1... | collective-permute-start | bytes 368648 | tf_op jit(solution)/shard_map/qkv_z/ppermute | solution.py:43
  22.5 13.2 %collective-permute-done.3 = bf16[48,1280]{1,0:T(8,128)(2,1)S(1)} collective-permute-done((bf16[48,1280]{1,0:T(8,128)(2,1)S(1)}, bf16[48,1280]{1,0:T(8,128)(2,1)S(1)}, u32[]{:S(2)}, u32[]{:S(2)}) %collective-permute-start.3) | collective-permute-done | bytes 122912 | tf_op jit(solution)/shard_map/qkv_z/ppermute | solution.py:43
  49.5 14.6 %collective-permute-done.8 = bf16[2,2,48,1280]{3,2,1,0:T(8,128)(2,1)S(1)} collective-permute-done((bf16[2,2,48,1280]{3,2,1,0:T(8,128)(2,1)S(1)}, bf16[2,2,48,1280]{3,2,1,0:T(8,128)(2,1)S(1)}, u32[]{:S(2)}, u32[]{:S(2)}) %collective-permute-start.8) | collective-permute-done | bytes 491552 | tf_op jit(solution)/shard_map/qkv_two/ppermute | solution.py:31
  65.8 3.4 %collective-permute-start.10 = (bf16[256,768]{0,1:T(8,128)(2,1)S(1)}, bf16[256,768]{0,1:T(8,128)(2,1)S(1)}, u32[]{:S(2)}, u32[]{:S(2)}) collective-permute-start(bf16[256,768]{0,1:T(8,128)(2,1)S(1)} %copy.129), channel_id=1, source_target_pairs={{0,4},{4,8},{8,12},{12,16},{16,20},{20,24},{24,28},{1,5},{5,9},{9,... | collective-permute-start | bytes 1179656 | tf_op jit(solution)/shard_map/ppermute | solution.py:47
  69.9 6.1 %keys.1 = (f32[256,768]{1,0:T(8,128)}, f32[256,768]{1,0:T(8,128)}, bf16[256,768]{1,0:T(8,128)(2,1)}, bf16[256,768]{1,0:T(8,128)(2,1)}, bf16[2,80,768]{2,1,0:T(8,128)(2,1)}, /*index=5*/f32[16,768]{1,0:T(8,128)}) custom-call(s32[2]{0:T(128)} %pad_add_fusion.c_ref, bf16[256,768]{1,0:T(8,128)(2,1)} %bitcast.169, bf16[768,1280]{1,0:T(8,128)(2,1)} %bitcast.141, ...), custom_call_target="tpu_custom_call" | custom-call | flops 5000000000 | bytes 5000000 | tf_op jit(solution)/shard_map/keys/pallas_call | solution.py:781
  78.4 4.8 %queries.1 = (f32[256,768]{1,0:T(8,128)}, f32[256,768]{1,0:T(8,128)}, bf16[256,768]{1,0:T(8,128)(2,1)}) custom-call(s32[2]{0:T(128)} %pad_add_fusion.c_ref, bf16[256,768]{1,0:T(8,128)(2,1)} %bitcast.170, bf16[768,1280]{1,0:T(8,128)(2,1)} %bitcast.142, bf16[768,1280]{1,0:T(8,128)(2,1)} %collective-permute-done.9.other, f32[16,768]{1,0:T(8,128)} %get-tuple-element.76.vec, ...), custom_call_target="tpu_custom_call" | custom-call | flops 3000000000 | bytes 3000000 | tf_op jit(solution)/shard_map/queries/pallas_call | solution.py:792
  85.2 4.5 %collective-permute-start.12 = (bf16[80,768]{1,0:T(8,128)(2,1)S(1)}, bf16[80,768]{1,0:T(8,128)(2,1)S(1)}, u32[]{:S(2)}, u32[]{:S(2)}) collective-permute-start(bf16[80,768]{1,0:T(8,128)(2,1)S(1)} %fusion.14), channel_id=1, source_target_pairs={{0,8},{1,9},{2,10},{3,11},{4,12},{5,13},{6,14},{7,15},{8,16},{9,17... | collective-permute-start | bytes 368648 | tf_op jit(solution)/shard_map/before_z/ppermute | solution.py:235
  89.7 4.6 %collective-permute-start.13 = (bf16[80,768]{1,0:T(8,128)(2,1)S(1)}, bf16[80,768]{1,0:T(8,128)(2,1)S(1)}, u32[]{:S(2)}, u32[]{:S(2)}) collective-permute-start(bf16[80,768]{1,0:T(8,128)(2,1)S(1)} %fusion.14), channel_id=1, source_target_pairs={{0,16},{1,17},{2,18},{3,19},{4,20},{5,21},{6,22},{7,23},{8,24},{9,... | collective-permute-start | bytes 368648 | tf_op jit(solution)/shard_map/before_z/ppermute | solution.py:235
  96.7 3.6 %collective-permute-done.13 = bf16[80,768]{1,0:T(8,128)(2,1)S(1)} collective-permute-done((bf16[80,768]{1,0:T(8,128)(2,1)S(1)}, bf16[80,768]{1,0:T(8,128)(2,1)S(1)}, u32[]{:S(2)}, u32[]{:S(2)}) %collective-permute-start.13) | collective-permute-done | bytes 122912 | tf_op jit(solution)/shard_map/before_z/ppermute | solution.py:235
  103.1 4.8 %halo.1 = (bf16[256,768]{1,0:T(8,128)(2,1)}, bf16[256,768]{1,0:T(8,128)(2,1)}) custom-call(s32[2]{0:T(128)} %pad_add_fusion.c_ref, bf16[256,768]{1,0:T(8,128)(2,1)} %copy.116.halo, bf16[768,1280]{1,0:T(8,128)(2,1)} %bitcast.144, bf16[768,1280]{1,0:T(8,128)(2,1)} %collective-permute-done.9.other, f32[16,768]{1,0:T(8,128)} %get-tuple-element.76.vec, ...), custom_call_target="tpu_custom_call" | custom-call | flops 2000000000 | bytes 2000000 | tf_op jit(solution)/shard_map/halo/pallas_call | solution.py:802
  114.8 6.8 %attention.1 = (bf16[256,768]{1,0:T(8,128)(2,1)}, bf16[768,256]{1,0:T(8,128)(2,1)}, f32[256,768]{1,0:T(8,128)}, f32[256,768]{1,0:T(8,128)}) custom-call(bf16[256,768]{1,0:T(8,128)(2,1)} %get-tuple-element.77.q, bf16[256,768]{1,0:T(8,128)(2,1)} %get-tuple-element.78.k, bf16[256,768]{1,0:T(8,128)(2,1)} %get-tuple-element.79.v, ...), custom_call_target="tpu_custom_call" | custom-call | flops 5000000000 | bytes 5000000 | tf_op jit(solution)/shard_map/attention/pallas_call | solution.py:824
  121.7 5.9 %all-gather.2.cloned.1.call-done.rest_hbm = bf16[3072,1728]{1,0:T(8,128)(2,1)} async-done(((bf16[96,1728]{1,0:T(8,128)(2,1)}), bf16[3072,1728]{1,0:T(8,128)(2,1)}) %all-gather.2.cloned.1.call-update) | async-done | bytes 10616848 | tf_op jit(solution)/shard_map/all_gather | solution.py:755
  127.6 5.6 %fusion.24 = (bf16[32,1,24,960]{3,2,1,0:T(8,128)(2,1)}, bf16[32,1,24,960]{3,2,1,0:T(8,128)(2,1)}, bf16[32,1,24,960]{3,2,1,0:T(8,128)(2,1)}, bf16[32,1,24,960]{3,2,1,0:T(8,128)(2,1)}) fusion(bf16[32,4,24,1728]{3,2,1,0:T(8,128)(2,1)} %bitcast.151), kind=kLoop, calls=%fused_computation.141 | loop fusion | bytes 11796480 | tf_op jit(solution)/shard_map/slice | solution.py:836
  133.2 18.8 %middle.1 = (f32[256,768]{1,0:T(8,128)}, f32[256,768]{1,0:T(8,128)}, bf16[256,768]{1,0:T(8,128)(2,1)}, bf16[256,896]{1,0:T(8,128)(2,1)}, bf16[2,80,768]{2,1,0:T(...) custom-call(bf16[256,768]{1,0:T(8,128)(2,1)} %get-tuple-element.88.c, ...), custom_call_target="tpu_custom_call" | custom-call | flops 20000000000 | bytes 20000000 | tf_op jit(solution)/shard_map/middle/pallas_call | solution.py:838
  165.3 16.6 %query_back.1 = (bf16[256,768]{1,0:T(8,128)(2,1)}, bf16[768,768]{1,0:T(8,128)(2,1)}, bf16[768,768]{1,0:T(8,128)(2,1)}, f32[6,8,256]{2,1,0:T(8,128)}, f32[8,768]{1,0:T(8,128)}) custom-call(s32[2]{0:T(128)} %pad_add_fusion.c_ref, bf16[768,256]{1,0:T(8,128)(2,1)} %bitcast.152, bf16[768,256]{1,0:T(8,128)(2,1)} %get-tuple-element.98.context, ...), custom_call_target="tpu_custom_call" | custom-call | flops 1000000 | bytes 1000 | tf_op jit(solution)/shard_map/query_back/pallas_call | solution.py:889
  189.5 16.1 %key_back.1 = (bf16[256,768]{1,0:T(8,128)(2,1)}, bf16[256,768]{1,0:T(8,128)(2,1)}, bf16[768,768]{1,0:T(8,128)(2,1)}, bf16[768,768]{1,0:T(8,128)(2,1)}, bf16[768,128]{1,0:T(8,128)(2,1)}) custom-call(s32[2]{0:T(128)} %pad_add_fusion.c_ref, bf16[768,256]{1,0:T(8,128)(2,1)} %bitcast.153, bf16[256,768]{1,0:T(8,128)(2,1)} %get-tuple-element.77.q, ...), custom_call_target="tpu_custom_call" | custom-call | flops 1000000 | bytes 1000 | tf_op jit(solution)/shard_map/key_back/pallas_call | solution.py:912
  215.5 22.7 %collective-permute-done.28 = bf16[2,2,48,1664]{3,2,0,1:T(8,128)(2,1)} collective-permute-done((bf16[2,2,48,1664]{3,2,0,1:T(8,128)(2,1)S(1)}, bf16[2,2,48,1664]{3,2,0,1:T(8,128)(2,1)}, u32[]{:S(2)}, u32[]{:S(2)}) %collective-permute-start.28) | collective-permute-done | bytes 639008 | tf_op jit(solution)/shard_map/d_qkv_one/ppermute | solution.py:31
  245.8 5.2 %tokens.1 = f32[256,768]{1,0:T(8,128)} custom-call(s32[2]{0:T(128)} %pad_add_fusion.c_ref, f32[256,768]{1,0:T(8,128)} %get-tuple-element.93.dresid, bf16[256,768]{1,0:T(8,128)(2,1)} %get-tuple-element.104.dq, bf16[256,768]{1,0:T(8,128)(2,1)} %get-tuple-element.115.dk, bf16[256,768]{1,0:T(8,128)(2,1)} %get-tuple-element.116.dv, bf16[768,1280]{1,0:T(8,128)(2,1)} %bitcast.145, ...), custom_call_target="tpu_custom_call" | custom-call | flops 1000000 | bytes 1000 | tf_op jit(solution)/shard_map/tokens/pallas_call | solution.py:938
  251.0 8.2 %collective-permute-done.31 = bf16[2,48,1664]{2,1,0:T(8,128)(2,1)S(1)} collective-permute-done((bf16[2,48,1664]{2,1,0:T(8,128)(2,1)S(1)}, bf16[2,48,1664]{2,1,0:T(8,128)(2,1)S(1)}, u32[]{:S(2)}, u32[]{:S(2)}) %collective-permute-start.31) | collective-permute-done | bytes 319520 | tf_op jit(solution)/shard_map/d_qkv_two/ppermute | solution.py:31
  260.3 3.2 %collective-permute-start.38 = (f32[12,129]{1,0:T(8,128)S(1)}, f32[12,129]{1,0:T(8,128)S(1)}, u32[]{:S(2)}, u32[]{:S(2)}) collective-permute-start(f32[12,129]{1,0:T(8,128)S(1)} %add.228), channel_id=1, source_target_pairs={{0,16},{1,17},{2,18},{3,19},{4,20},{5,21},{6,22},{7,23},{8,24},{9,... | collective-permute-start | bytes 18584 | tf_op jit(solution)/shard_map/everywhere/ppermute | solution.py:43
  264.4 3.8 %collective-permute-start.34 = (bf16[48,1664]{1,0:T(8,128)(2,1)S(1)}, bf16[48,1664]{1,0:T(8,128)(2,1)S(1)}, u32[]{:S(2)}, u32[]{:S(2)}) collective-permute-start(bf16[48,1664]{1,0:T(8,128)(2,1)S(1)} %get-tuple-element.152), channel_id=1, source_target_pairs={{0,16},{1,17},{2,18},{3,19},{4,20},{5,21},{6,22},{7,23},{8,24},{9,... | collective-permute-start | bytes 479240 | tf_op jit(solution)/shard_map/d_qkv_z/ppermute | solution.py:43
  269.4 3.8 %collective-permute-done.33 = bf16[48,1664]{1,0:T(8,128)(2,1)S(1)} collective-permute-done((bf16[48,1664]{1,0:T(8,128)(2,1)S(1)}, bf16[48,1664]{1,0:T(8,128)(2,1)S(1)}, u32[]{:S(2)}, u32[]{:S(2)}) %collective-permute-start.33) | collective-permute-done | bytes 159776 | tf_op jit(solution)/shard_map/d_qkv_z/ppermute | solution.py:43
  273.2 10.7 %collective-permute-done.34 = bf16[48,1664]{1,0:T(8,128)(2,1)S(1)} collective-permute-done((bf16[48,1664]{1,0:T(8,128)(2,1)S(1)}, bf16[48,1664]{1,0:T(8,128)(2,1)S(1)}, u32[]{:S(2)}, u32[]{:S(2)}) %collective-permute-start.34) | collective-permute-done | bytes 159776 | tf_op jit(solution)/shard_map/d_qkv_z/ppermute | solution.py:43
  287.2 25.1 %reduce-scatter.2.cloned.1.call-done.packed = bf16[96,1536]{1,0:T(8,128)(2,1)} async-done(((bf16[3072,1536]{1,0:T(8,128)(2,1)}), bf16[96,1536]{1,0:T(8,128)(2,1)}) %reduce-scatter.2.cloned.1.call-update) | async-done | bytes 294928 | tf_op jit(solution)/shard_map/reduce_scatter | solution.py:860
  (245 shorter events, 88.7 us)
Async XLA Ops:
  7.3 120.3 %all-gather.2.cloned.1.call-start = ((), (), s32[]{:S(2)}) async-start(), calls=%async_computation.1 | async-start | bytes 11354112 | tf_op jit(solution)/shard_map/all_gather | solution.py:755
  10.8 301.5 %reduce-scatter.2.cloned.1.call-start = ((), (), s32[]{:S(2)}) async-start(), calls=%async_computation.2 | async-start | bytes 9732096 | tf_op jit(solution)/shard_map/reduce_scatter | solution.py:860
  13.9 8.5 %collective-permute-start.2 = (bf16[48,1280]{1,0:T(8,128)(2,1)S(1)}, bf16[48,1280]{1,0:T(8,128)(2,1)S(1)}, u32[]{:S(2)}, u32[]{:S(2)}) collective-permute-start(bf16[48,1280]{1,0:T(8,128)(2,1)S(1)} %pad_maximum_fusion.3), channel_id=1, source_target_pairs={{0,24},{1,25},{2,26},{3,27},{4,28},{5,29},{6,30},{7,31},{8,0},{9,1... | collective-permute-start | bytes 368648 | tf_op jit(solution)/shard_map/qkv_z/ppermute | solution.py:43
  18.8 16.9 %collective-permute-start.3 = (bf16[48,1280]{1,0:T(8,128)(2,1)S(1)}, bf16[48,1280]{1,0:T(8,128)(2,1)S(1)}, u32[]{:S(2)}, u32[]{:S(2)}) collective-permute-start(bf16[48,1280]{1,0:T(8,128)(2,1)S(1)} %pad_maximum_fusion.3), channel_id=1, source_target_pairs={{0,16},{1,17},{2,18},{3,19},{4,20},{5,21},{6,22},{7,23},{8,24},{9,... | collective-permute-start | bytes 368648 | tf_op jit(solution)/shard_map/qkv_z/ppermute | solution.py:43
  18.9 16.8 %collective-permute-start.4 = (bf16[48,1280]{1,0:T(8,128)(2,1)S(1)}, bf16[48,1280]{1,0:T(8,128)(2,1)S(1)}, u32[]{:S(2)}, u32[]{:S(2)}) collective-permute-start(bf16[48,1280]{1,0:T(8,128)(2,1)S(1)} %pad_maximum_fusion.3), channel_id=1, source_target_pairs={{0,8},{1,9},{2,10},{3,11},{4,12},{5,13},{6,14},{7,15},{8,16},{9,17... | collective-permute-start | bytes 368648 | tf_op jit(solution)/shard_map/qkv_z/ppermute | solution.py:43
  42.2 22.0 %collective-permute-start.8 = (bf16[2,2,48,1280]{3,2,1,0:T(8,128)(2,1)S(1)}, bf16[2,2,48,1280]{3,2,1,0:T(8,128)(2,1)S(1)}, u32[]{:S(2)}, u32[]{:S(2)}) collective-permute-start(bf16[2,2,48,1280]{3,2,1,0:T(8,128)(2,1)S(1)} %maximum_select_fusion.3), channel_id=1, source_target_pairs={{0,4},{1,5},{2,6},{3,7},{4,0},{5,1},{6,2},{7,3},{8,12},{9,13},{10,... | collective-permute-start | bytes 1474568 | tf_op jit(solution)/shard_map/qkv_two/ppermute | solution.py:31
  45.7 18.6 %collective-permute-start.6 = (bf16[2,2,48,1280]{3,2,0,1:T(8,128)(2,1)S(1)}, bf16[2,2,48,1280]{3,2,0,1:T(8,128)(2,1)S(1)}, u32[]{:S(2)}, u32[]{:S(2)}) collective-permute-start(bf16[2,2,48,1280]{3,2,0,1:T(8,128)(2,1)S(1)} %maximum_select_fusion.2), channel_id=1, source_target_pairs={{0,2},{1,3},{2,0},{3,1},{4,6},{5,7},{6,4},{7,5},{8,10},{9,11},{10,... | collective-permute-start | bytes 1474568 | tf_op jit(solution)/shard_map/qkv_two/ppermute | solution.py:31
  65.8 30.9 %collective-permute-start.10 = (bf16[256,768]{0,1:T(8,128)(2,1)S(1)}, bf16[256,768]{0,1:T(8,128)(2,1)S(1)}, u32[]{:S(2)}, u32[]{:S(2)}) collective-permute-start(bf16[256,768]{0,1:T(8,128)(2,1)S(1)} %copy.129), channel_id=1, source_target_pairs={{0,4},{4,8},{8,12},{12,16},{16,20},{20,24},{24,28},{1,5},{5,9},{9,... | collective-permute-start | bytes 1179656 | tf_op jit(solution)/shard_map/ppermute | solution.py:47
  83.3 24.8 %collective-permute-start.15 = (bf16[256,768]{1,0:T(8,128)(2,1)}, bf16[256,768]{1,0:T(8,128)(2,1)S(1)}, u32[]{:S(2)}, u32[]{:S(2)}) collective-permute-start(bf16[256,768]{1,0:T(8,128)(2,1)} %get-tuple-element.77.q), channel_id=1, source_target_pairs={{4,0},{8,4},{12,8},{16,12},{20,16},{24,20},{28,24},{5,1},{9,5},{13... | collective-permute-start | bytes 1179656 | tf_op jit(solution)/shard_map/ppermute | solution.py:47
  85.2 11.5 %collective-permute-start.12 = (bf16[80,768]{1,0:T(8,128)(2,1)S(1)}, bf16[80,768]{1,0:T(8,128)(2,1)S(1)}, u32[]{:S(2)}, u32[]{:S(2)}) collective-permute-start(bf16[80,768]{1,0:T(8,128)(2,1)S(1)} %fusion.14), channel_id=1, source_target_pairs={{0,8},{1,9},{2,10},{3,11},{4,12},{5,13},{6,14},{7,15},{8,16},{9,17... | collective-permute-start | bytes 368648 | tf_op jit(solution)/shard_map/before_z/ppermute | solution.py:235
  89.7 10.6 %collective-permute-start.13 = (bf16[80,768]{1,0:T(8,128)(2,1)S(1)}, bf16[80,768]{1,0:T(8,128)(2,1)S(1)}, u32[]{:S(2)}, u32[]{:S(2)}) collective-permute-start(bf16[80,768]{1,0:T(8,128)(2,1)S(1)} %fusion.14), channel_id=1, source_target_pairs={{0,16},{1,17},{2,18},{3,19},{4,20},{5,21},{6,22},{7,23},{8,24},{9,... | collective-permute-start | bytes 368648 | tf_op jit(solution)/shard_map/before_z/ppermute | solution.py:235
  155.2 27.6 %collective-permute-start.19 = (bf16[256,896]{1,0:T(8,128)(2,1)S(1)}, bf16[256,896]{1,0:T(8,128)(2,1)S(1)}, u32[]{:S(2)}, u32[]{:S(2)}) collective-permute-start(bf16[256,896]{1,0:T(8,128)(2,1)S(1)} %copy-done.1), channel_id=1, source_target_pairs={{4,0},{8,4},{12,8},{16,12},{20,16},{24,20},{28,24},{5,1},{9,5},{13... | collective-permute-start | bytes 1376264 | tf_op jit(solution)/shard_map/ppermute | solution.py:47
  161.4 21.5 %collective-permute-start.20 = (bf16[80,768]{1,0:T(8,128)(2,1)S(1)}, bf16[80,768]{1,0:T(8,128)(2,1)S(1)}, u32[]{:S(2)}, u32[]{:S(2)}) collective-permute-start(bf16[80,768]{1,0:T(8,128)(2,1)S(1)} %fusion.17), channel_id=1, source_target_pairs={{8,0},{9,1},{10,2},{11,3},{12,4},{13,5},{14,6},{15,7},{16,8},{17,9... | collective-permute-start | bytes 368648 | tf_op jit(solution)/shard_map/later_z/ppermute | solution.py:235
  162.7 20.2 %collective-permute-start.21 = (bf16[80,768]{1,0:T(8,128)(2,1)S(1)}, bf16[80,768]{1,0:T(8,128)(2,1)S(1)}, u32[]{:S(2)}, u32[]{:S(2)}) collective-permute-start(bf16[80,768]{1,0:T(8,128)(2,1)S(1)} %fusion.17), channel_id=1, source_target_pairs={{16,0},{17,1},{18,2},{19,3},{20,4},{21,5},{22,6},{23,7},{24,8},{25... | collective-permute-start | bytes 368648 | tf_op jit(solution)/shard_map/later_z/ppermute | solution.py:235
  164.0 18.9 %collective-permute-start.22 = (bf16[80,768]{1,0:T(8,128)(2,1)S(1)}, bf16[80,768]{1,0:T(8,128)(2,1)S(1)}, u32[]{:S(2)}, u32[]{:S(2)}) collective-permute-start(bf16[80,768]{1,0:T(8,128)(2,1)S(1)} %fusion.17), channel_id=1, source_target_pairs={{24,0},{25,1},{26,2},{27,3},{28,4},{29,5},{30,6},{31,7}} | collective-permute-start | bytes 368648 | tf_op jit(solution)/shard_map/later_z/ppermute | solution.py:235
  182.7 26.8 %collective-permute-start.24 = (bf16[768,768]{1,0:T(8,128)(2,1)}, bf16[768,768]{1,0:T(8,128)(2,1)S(1)}, u32[]{:S(2)}, u32[]{:S(2)}) collective-permute-start(bf16[768,768]{1,0:T(8,128)(2,1)} %get-tuple-element.118), channel_id=1, source_target_pairs={{0,1},{1,0},{2,3},{3,2},{4,5},{5,4},{6,7},{7,6},{8,9},{9,8},{10,11... | collective-permute-start | bytes 3538952 | tf_op jit(solution)/shard_map/d_qkv_core/ppermute | solution.py:31
  212.9 25.3 %collective-permute-start.28 = (bf16[2,2,48,1664]{3,2,0,1:T(8,128)(2,1)S(1)}, bf16[2,2,48,1664]{3,2,0,1:T(8,128)(2,1)}, u32[]{:S(2)}, u32[]{:S(2)}) collective-permute-start(bf16[2,2,48,1664]{3,2,0,1:T(8,128)(2,1)S(1)} %copy_bitcast_fusion), channel_id=1, source_target_pairs={{0,2},{1,3},{2,0},{3,1},{4,6},{5,7},{6,4},{7,5},{8,10},{9,11},{10,... | collective-permute-start | bytes 1916936 | tf_op jit(solution)/shard_map/d_qkv_one/ppermute | solution.py:31
  214.7 25.1 %collective-permute-start.29 = (bf16[2,2,48,1664]{3,2,1,0:T(8,128)(2,1)}, bf16[2,2,48,1664]{3,2,1,0:T(8,128)(2,1)}, u32[]{:S(2)}, u32[]{:S(2)}) collective-permute-start(bf16[2,2,48,1664]{3,2,1,0:T(8,128)(2,1)} %dynamic-slice_bitcast_fusion), channel_id=1, source_target_pairs={{0,4},{1,5},{2,6},{3,7},{4,0},{5,1},{6,2},{7,3},{8,12},{9,13},{10,... | collective-permute-start | bytes 1916936 | tf_op jit(solution)/shard_map/d_qkv_one/ppermute | solution.py:31
  243.6 15.7 %collective-permute-start.31 = (bf16[2,48,1664]{2,1,0:T(8,128)(2,1)S(1)}, bf16[2,48,1664]{2,1,0:T(8,128)(2,1)S(1)}, u32[]{:S(2)}, u32[]{:S(2)}) collective-permute-start(bf16[2,48,1664]{2,1,0:T(8,128)(2,1)S(1)} %dynamic-slice_bitcast_fusion.2), channel_id=1, source_target_pairs={{0,4},{1,5},{2,6},{3,7},{4,0},{5,1},{6,2},{7,3},{8,12},{9,13},{10,... | collective-permute-start | bytes 958472 | tf_op jit(solution)/shard_map/d_qkv_two/ppermute | solution.py:31
  244.5 15.2 %collective-permute-start.32 = (bf16[2,48,1664]{2,1,0:T(8,128)(2,1)S(1)}, bf16[2,48,1664]{2,1,0:T(8,128)(2,1)S(1)}, u32[]{:S(2)}, u32[]{:S(2)}) collective-permute-start(bf16[2,48,1664]{2,1,0:T(8,128)(2,1)S(1)} %dynamic-slice_bitcast_fusion.1), channel_id=1, source_target_pairs={{0,2},{1,3},{2,0},{3,1},{4,6},{5,7},{6,4},{7,5},{8,10},{9,11},{10,... | collective-permute-start | bytes 958472 | tf_op jit(solution)/shard_map/d_qkv_two/ppermute | solution.py:31
  259.7 8.6 %collective-permute-start.37 = (f32[12,129]{1,0:T(8,128)S(1)}, f32[12,129]{1,0:T(8,128)S(1)}, u32[]{:S(2)}, u32[]{:S(2)}) collective-permute-start(f32[12,129]{1,0:T(8,128)S(1)} %add.228), channel_id=1, source_target_pairs={{0,24},{1,25},{2,26},{3,27},{4,28},{5,29},{6,30},{7,31},{8,0},{9,1... | collective-permute-start | bytes 18584 | tf_op jit(solution)/shard_map/everywhere/ppermute | solution.py:43
  264.3 8.9 %collective-permute-start.33 = (bf16[48,1664]{1,0:T(8,128)(2,1)S(1)}, bf16[48,1664]{1,0:T(8,128)(2,1)S(1)}, u32[]{:S(2)}, u32[]{:S(2)}) collective-permute-start(bf16[48,1664]{1,0:T(8,128)(2,1)S(1)} %get-tuple-element.150), channel_id=1, source_target_pairs={{0,8},{1,9},{2,10},{3,11},{4,12},{5,13},{6,14},{7,15},{8,16},{9,17... | collective-permute-start | bytes 479240 | tf_op jit(solution)/shard_map/d_qkv_z/ppermute | solution.py:43
  264.4 19.4 %collective-permute-start.34 = (bf16[48,1664]{1,0:T(8,128)(2,1)S(1)}, bf16[48,1664]{1,0:T(8,128)(2,1)S(1)}, u32[]{:S(2)}, u32[]{:S(2)}) collective-permute-start(bf16[48,1664]{1,0:T(8,128)(2,1)S(1)} %get-tuple-element.152), channel_id=1, source_target_pairs={{0,16},{1,17},{2,18},{3,19},{4,20},{5,21},{6,22},{7,23},{8,24},{9,... | collective-permute-start | bytes 479240 | tf_op jit(solution)/shard_map/d_qkv_z/ppermute | solution.py:43
  268.3 15.6 %collective-permute-start.35 = (bf16[48,1664]{1,0:T(8,128)(2,1)S(1)}, bf16[48,1664]{1,0:T(8,128)(2,1)S(1)}, u32[]{:S(2)}, u32[]{:S(2)}) collective-permute-start(bf16[48,1664]{1,0:T(8,128)(2,1)S(1)} %get-tuple-element.151), channel_id=1, source_target_pairs={{0,24},{1,25},{2,26},{3,27},{4,28},{5,29},{6,30},{7,31},{8,0},{9,1... | collective-permute-start | bytes 479240 | tf_op jit(solution)/shard_map/d_qkv_z/ppermute | solution.py:43
  (49 other events, 411.3 us)
Sparse Core Ops, SparseCore 0:
  11.1 116.4 all-gather.1
  159.5 152.6 reduce-scatter.1

commit v4 on v3

--- a/solution.py
+++ b/solution.py
@@ -851,7 +851,7 @@
             pltpu.SemaphoreType.DMA((2 * slices,)),
             pltpu.SemaphoreType.DMA((2 * slices,)),
         ],
-        compiler_params=params(56),
+        compiler_params=pltpu.CompilerParams(vmem_limit_bytes=44 * 2**20),
         cost_estimate=cost(20),
         name="middle",
     )(context, tok, cot, vec, b_u, ratio, denom, q, before, far, rest, *blocks)

time: 322 us -> 319 us (level)
  transfers between devices with their start and end apart: 42 -> 42, of which waited for: 25 -> 27; matrix products, arithmetic and copies ran while one was open for 9% -> 9% of each run, Pallas kernels for 19% -> 19%
where the time goes in v4:
time: 319 us; the launch traced here: 318 us
  waiting for transfers between devices  132 us (41%)
  Pallas kernels  78.6 us (25%)
  starting transfers between devices  50.7 us (16%)
  local copies, waits for them, and re-layouts  25.8 us (8%)
  other arithmetic  15.6 us (5%)
  between operations  15.3 us (5%)
    ppermute x22, waiting for transfers between devices, flip(): return lax.ppermute(a, BOTH, [(d, d ^ stride) for d in range(self.n)])  65.2 us
    ppermute x9, waiting for transfers between devices, turn_z(): lax.ppermute(a, BOTH, [(d, (d + 8 * by) % self.n) for d in range(self.n)])  31.1 us
    reduce_scatter x1, waiting for transfers between devices, on_device(): s_rest = lax.psum_scatter(g_rest, BOTH, scatter_dimension=0, tiled=True)  25 us
    ppermute x22, starting transfers between devices, flip(): return lax.ppermute(a, BOTH, [(d, d ^ stride) for d in range(self.n)])  16.8 us
    pallas_call x1, Pallas kernels, on_device(): pl.pallas_call(query_back_kernel, grid_spec=pltpu.PrefetchScalarGridSpec(...  16.7 us
    pallas_call x1, Pallas kernels, on_device(): pl.pallas_call(key_back_kernel, grid_spec=pltpu.PrefetchScalarGridSpec(nu...  16.1 us
    pallas_call x1, Pallas kernels, on_device(): pl.pallas_call(functools.partial(middle_kernel, slices), out_shape=(wide3...  16 us
    ppermute x9, starting transfers between devices, turn_z(): lax.ppermute(a, BOTH, [(d, (d + 8 * by) % self.n) for d in range(self.n)])  14.2 us
  transfers between devices with their start and end apart: 42, of which 27 were waited for; matrix products, arithmetic and copies ran while one was open for 9% of the time, Pallas kernels for 19%

profile of v4, /device:TPU:0, one launch (start us, length us, event | category | flops | bytes accessed | tf_op | source)
XLA Modules:
  0.0 317.9 jit_solution(681657385330242798)
XLA Ops:
  13.9 4.8 %collective-permute-start.2 = (bf16[48,1280]{1,0:T(8,128)(2,1)S(1)}, bf16[48,1280]{1,0:T(8,128)(2,1)S(1)}, u32[]{:S(2)}, u32[]{:S(2)}) collective-permute-start(bf16[48,1280]{1,0:T(8,128)(2,1)S(1)} %pad_maximum_fusion.3), channel_id=1, source_target_pairs={{0,24},{1,25},{2,26},{3,27},{4,28},{5,29},{6,30},{7,31},{8,0},{9,1... | collective-permute-start | bytes 368648 | tf_op jit(solution)/shard_map/qkv_z/ppermute | solution.py:43
  22.5 13.2 %collective-permute-done.3 = bf16[48,1280]{1,0:T(8,128)(2,1)S(1)} collective-permute-done((bf16[48,1280]{1,0:T(8,128)(2,1)S(1)}, bf16[48,1280]{1,0:T(8,128)(2,1)S(1)}, u32[]{:S(2)}, u32[]{:S(2)}) %collective-permute-start.3) | collective-permute-done | bytes 122912 | tf_op jit(solution)/shard_map/qkv_z/ppermute | solution.py:43
  50.8 13.4 %collective-permute-done.8 = bf16[2,2,48,1280]{3,2,1,0:T(8,128)(2,1)S(1)} collective-permute-done((bf16[2,2,48,1280]{3,2,1,0:T(8,128)(2,1)S(1)}, bf16[2,2,48,1280]{3,2,1,0:T(8,128)(2,1)S(1)}, u32[]{:S(2)}, u32[]{:S(2)}) %collective-permute-start.8) | collective-permute-done | bytes 491552 | tf_op jit(solution)/shard_map/qkv_two/ppermute | solution.py:31
  66.4 3.4 %collective-permute-start.10 = (bf16[256,768]{0,1:T(8,128)(2,1)S(1)}, bf16[256,768]{0,1:T(8,128)(2,1)S(1)}, u32[]{:S(2)}, u32[]{:S(2)}) collective-permute-start(bf16[256,768]{0,1:T(8,128)(2,1)S(1)} %copy.129), channel_id=1, source_target_pairs={{0,4},{4,8},{8,12},{12,16},{16,20},{20,24},{24,28},{1,5},{5,9},{9,... | collective-permute-start | bytes 1179656 | tf_op jit(solution)/shard_map/ppermute | solution.py:47
  70.5 6.1 %keys.1 = (f32[256,768]{1,0:T(8,128)}, f32[256,768]{1,0:T(8,128)}, bf16[256,768]{1,0:T(8,128)(2,1)}, bf16[256,768]{1,0:T(8,128)(2,1)}, bf16[2,80,768]{2,1,0:T(8,128)(2,1)}, /*index=5*/f32[16,768]{1,0:T(8,128)}) custom-call(s32[2]{0:T(128)} %pad_add_fusion.c_ref, bf16[256,768]{1,0:T(8,128)(2,1)} %bitcast.142, bf16[768,1280]{1,0:T(8,128)(2,1)} %bitcast.149, ...), custom_call_target="tpu_custom_call" | custom-call | flops 5000000000 | bytes 5000000 | tf_op jit(solution)/shard_map/keys/pallas_call | solution.py:781
  79.2 4.9 %queries.1 = (f32[256,768]{1,0:T(8,128)}, f32[256,768]{1,0:T(8,128)}, bf16[256,768]{1,0:T(8,128)(2,1)}) custom-call(s32[2]{0:T(128)} %pad_add_fusion.c_ref, bf16[256,768]{1,0:T(8,128)(2,1)} %bitcast.143, bf16[768,1280]{1,0:T(8,128)(2,1)} %bitcast.150, bf16[768,1280]{1,0:T(8,128)(2,1)} %collective-permute-done.9.other, f32[16,768]{1,0:T(8,128)} %get-tuple-element.76.vec, ...), custom_call_target="tpu_custom_call" | custom-call | flops 3000000000 | bytes 3000000 | tf_op jit(solution)/shard_map/queries/pallas_call | solution.py:792
  86.7 3.2 %collective-permute-start.12 = (bf16[80,768]{1,0:T(8,128)(2,1)S(1)}, bf16[80,768]{1,0:T(8,128)(2,1)S(1)}, u32[]{:S(2)}, u32[]{:S(2)}) collective-permute-start(bf16[80,768]{1,0:T(8,128)(2,1)S(1)} %fusion.14), channel_id=1, source_target_pairs={{0,8},{1,9},{2,10},{3,11},{4,12},{5,13},{6,14},{7,15},{8,16},{9,17... | collective-permute-start | bytes 368648 | tf_op jit(solution)/shard_map/before_z/ppermute | solution.py:235
  89.9 5.1 %collective-permute-start.13 = (bf16[80,768]{1,0:T(8,128)(2,1)S(1)}, bf16[80,768]{1,0:T(8,128)(2,1)S(1)}, u32[]{:S(2)}, u32[]{:S(2)}) collective-permute-start(bf16[80,768]{1,0:T(8,128)(2,1)S(1)} %fusion.14), channel_id=1, source_target_pairs={{0,16},{1,17},{2,18},{3,19},{4,20},{5,21},{6,22},{7,23},{8,24},{9,... | collective-permute-start | bytes 368648 | tf_op jit(solution)/shard_map/before_z/ppermute | solution.py:235
  102.7 4.8 %halo.1 = (bf16[256,768]{1,0:T(8,128)(2,1)}, bf16[256,768]{1,0:T(8,128)(2,1)}) custom-call(s32[2]{0:T(128)} %pad_add_fusion.c_ref, bf16[256,768]{1,0:T(8,128)(2,1)} %copy.116.halo, bf16[768,1280]{1,0:T(8,128)(2,1)} %bitcast.152, bf16[768,1280]{1,0:T(8,128)(2,1)} %collective-permute-done.9.other, f32[16,768]{1,0:T(8,128)} %get-tuple-element.76.vec, ...), custom_call_target="tpu_custom_call" | custom-call | flops 2000000000 | bytes 2000000 | tf_op jit(solution)/shard_map/halo/pallas_call | solution.py:802
  114.8 7.0 %attention.1 = (bf16[256,768]{1,0:T(8,128)(2,1)}, bf16[768,256]{1,0:T(8,128)(2,1)}, f32[256,768]{1,0:T(8,128)}, f32[256,768]{1,0:T(8,128)}) custom-call(bf16[256,768]{1,0:T(8,128)(2,1)} %get-tuple-element.77.q, bf16[256,768]{1,0:T(8,128)(2,1)} %get-tuple-element.78.k, bf16[256,768]{1,0:T(8,128)(2,1)} %get-tuple-element.79.v, ...), custom_call_target="tpu_custom_call" | custom-call | flops 5000000000 | bytes 5000000 | tf_op jit(solution)/shard_map/attention/pallas_call | solution.py:824
  121.8 6.3 %all-gather.2.cloned.1.call-done.rest_hbm = bf16[3072,1728]{1,0:T(8,128)(2,1)} async-done(((bf16[96,1728]{1,0:T(8,128)(2,1)}), bf16[3072,1728]{1,0:T(8,128)(2,1)}) %all-gather.2.cloned.1.call-update) | async-done | bytes 10616848 | tf_op jit(solution)/shard_map/all_gather | solution.py:755
  128.1 4.9 %fusion.24 = (bf16[32,1,24,960]{3,2,1,0:T(8,128)(2,1)}, bf16[32,1,24,960]{3,2,1,0:T(8,128)(2,1)S(1)}, bf16[32,1,24,960]{3,2,1,0:T(8,128)(2,1)S(1)}, bf16[32,1,24,960]{3,2,1,0:T(8,128)(2,1)S(1)}) fusion(bf16[32,4,24,1728]{3,2,1,0:T(8,128)(2,1)} %bitcast.159), kind=kLoop, calls=%fused_computation.141 | loop fusion | bytes 11796480 | tf_op jit(solution)/shard_map/slice | solution.py:836
  133.1 16.0 %middle.1 = (f32[256,768]{1,0:T(8,128)}, f32[256,768]{1,0:T(8,128)S(1)}, bf16[256,768]{1,0:T(8,128)(2,1)S(1)}, bf16[256,896]{1,0:T(8,128)(2,1)S(1)}, bf16[2,80,7...) custom-call(bf16[256,768]{1,0:T(8,128)(2,1)S(1)} %copy-done.13, ...), custom_call_target="tpu_custom_call" | custom-call | flops 20000000000 | bytes 20000000 | tf_op jit(solution)/shard_map/middle/pallas_call | solution.py:838
  149.1 3.5 %copy.124 = bf16[4,32,24,768]{3,2,0,1:T(8,128)(2,1)S(1)} copy(bf16[4,32,24,768]{3,2,1,0:T(8,128)(2,1)} %bitcast.158) | data formatting | bytes 9437184 | tf_op jit(solution)/shard_map/reshape | solution.py:858
  163.1 16.7 %query_back.1 = (bf16[256,768]{1,0:T(8,128)(2,1)}, bf16[768,768]{1,0:T(8,128)(2,1)}, bf16[768,768]{1,0:T(8,128)(2,1)}, f32[6,8,256]{2,1,0:T(8,128)}, f32[8,768]{1,0:T(8,128)}) custom-call(s32[2]{0:T(128)} %pad_add_fusion.c_ref, bf16[768,256]{1,0:T(8,128)(2,1)} %bitcast.160, bf16[768,256]{1,0:T(8,128)(2,1)} %get-tuple-element.98.context, ...), custom_call_target="tpu_custom_call" | custom-call | flops 1000000 | bytes 1000 | tf_op jit(solution)/shard_map/query_back/pallas_call | solution.py:889
  187.4 16.1 %key_back.1 = (bf16[256,768]{1,0:T(8,128)(2,1)}, bf16[256,768]{1,0:T(8,128)(2,1)}, bf16[768,768]{1,0:T(8,128)(2,1)}, bf16[768,768]{1,0:T(8,128)(2,1)}, bf16[768,128]{1,0:T(8,128)(2,1)}) custom-call(s32[2]{0:T(128)} %pad_add_fusion.c_ref, bf16[768,256]{1,0:T(8,128)(2,1)} %bitcast.161, bf16[256,768]{1,0:T(8,128)(2,1)} %get-tuple-element.77.q, ...), custom_call_target="tpu_custom_call" | custom-call | flops 1000000 | bytes 1000 | tf_op jit(solution)/shard_map/key_back/pallas_call | solution.py:912
  212.7 22.7 %collective-permute-done.28 = bf16[2,2,48,1664]{3,2,0,1:T(8,128)(2,1)} collective-permute-done((bf16[2,2,48,1664]{3,2,0,1:T(8,128)(2,1)S(1)}, bf16[2,2,48,1664]{3,2,0,1:T(8,128)(2,1)}, u32[]{:S(2)}, u32[]{:S(2)}) %collective-permute-start.28) | collective-permute-done | bytes 639008 | tf_op jit(solution)/shard_map/d_qkv_one/ppermute | solution.py:31
  243.0 5.2 %tokens.1 = f32[256,768]{1,0:T(8,128)} custom-call(s32[2]{0:T(128)} %pad_add_fusion.c_ref, f32[256,768]{1,0:T(8,128)} %copy-done.3, bf16[256,768]{1,0:T(8,128)(2,1)} %get-tuple-element.104.dq, bf16[256,768]{1,0:T(8,128)(2,1)} %get-tuple-element.115.dk, bf16[256,768]{1,0:T(8,128)(2,1)} %get-tuple-element.116.dv, bf16[768,1280]{1,0:T(8,128)(2,1)} %bitcast.153, ...), custom_call_target="tpu_custom_call" | custom-call | flops 1000000 | bytes 1000 | tf_op jit(solution)/shard_map/tokens/pallas_call | solution.py:938
  248.2 8.2 %collective-permute-done.31 = bf16[2,48,1664]{2,1,0:T(8,128)(2,1)S(1)} collective-permute-done((bf16[2,48,1664]{2,1,0:T(8,128)(2,1)S(1)}, bf16[2,48,1664]{2,1,0:T(8,128)(2,1)S(1)}, u32[]{:S(2)}, u32[]{:S(2)}) %collective-permute-start.31) | collective-permute-done | bytes 319520 | tf_op jit(solution)/shard_map/d_qkv_two/ppermute | solution.py:31
  257.7 3.2 %collective-permute-start.38 = (f32[12,129]{1,0:T(8,128)S(1)}, f32[12,129]{1,0:T(8,128)S(1)}, u32[]{:S(2)}, u32[]{:S(2)}) collective-permute-start(f32[12,129]{1,0:T(8,128)S(1)} %add.228), channel_id=1, source_target_pairs={{0,16},{1,17},{2,18},{3,19},{4,20},{5,21},{6,22},{7,23},{8,24},{9,... | collective-permute-start | bytes 18584 | tf_op jit(solution)/shard_map/everywhere/ppermute | solution.py:43
  261.8 3.8 %collective-permute-start.34 = (bf16[48,1664]{1,0:T(8,128)(2,1)S(1)}, bf16[48,1664]{1,0:T(8,128)(2,1)S(1)}, u32[]{:S(2)}, u32[]{:S(2)}) collective-permute-start(bf16[48,1664]{1,0:T(8,128)(2,1)S(1)} %get-tuple-element.152), channel_id=1, source_target_pairs={{0,16},{1,17},{2,18},{3,19},{4,20},{5,21},{6,22},{7,23},{8,24},{9,... | collective-permute-start | bytes 479240 | tf_op jit(solution)/shard_map/d_qkv_z/ppermute | solution.py:43
  266.8 3.8 %collective-permute-done.33 = bf16[48,1664]{1,0:T(8,128)(2,1)S(1)} collective-permute-done((bf16[48,1664]{1,0:T(8,128)(2,1)S(1)}, bf16[48,1664]{1,0:T(8,128)(2,1)S(1)}, u32[]{:S(2)}, u32[]{:S(2)}) %collective-permute-start.33) | collective-permute-done | bytes 159776 | tf_op jit(solution)/shard_map/d_qkv_z/ppermute | solution.py:43
  270.6 10.1 %collective-permute-done.34 = bf16[48,1664]{1,0:T(8,128)(2,1)S(1)} collective-permute-done((bf16[48,1664]{1,0:T(8,128)(2,1)S(1)}, bf16[48,1664]{1,0:T(8,128)(2,1)S(1)}, u32[]{:S(2)}, u32[]{:S(2)}) %collective-permute-start.34) | collective-permute-done | bytes 159776 | tf_op jit(solution)/shard_map/d_qkv_z/ppermute | solution.py:43
  284.3 25.0 %reduce-scatter.2.cloned.1.call-done.packed = bf16[96,1536]{1,0:T(8,128)(2,1)} async-done(((bf16[3072,1536]{1,0:T(8,128)(2,1)}), bf16[96,1536]{1,0:T(8,128)(2,1)}) %reduce-scatter.2.cloned.1.call-update) | async-done | bytes 294928 | tf_op jit(solution)/shard_map/reduce_scatter | solution.py:860
  (265 shorter events, 91.4 us)
Async XLA Ops:
  7.3 120.7 %all-gather.2.cloned.1.call-start = ((), (), s32[]{:S(2)}) async-start(), calls=%async_computation.1 | async-start | bytes 11354112 | tf_op jit(solution)/shard_map/all_gather | solution.py:755
  10.8 298.5 %reduce-scatter.2.cloned.1.call-start = ((), (), s32[]{:S(2)}) async-start(), calls=%async_computation.2 | async-start | bytes 9732096 | tf_op jit(solution)/shard_map/reduce_scatter | solution.py:860
  18.8 16.9 %collective-permute-start.3 = (bf16[48,1280]{1,0:T(8,128)(2,1)S(1)}, bf16[48,1280]{1,0:T(8,128)(2,1)S(1)}, u32[]{:S(2)}, u32[]{:S(2)}) collective-permute-start(bf16[48,1280]{1,0:T(8,128)(2,1)S(1)} %pad_maximum_fusion.3), channel_id=1, source_target_pairs={{0,16},{1,17},{2,18},{3,19},{4,20},{5,21},{6,22},{7,23},{8,24},{9,... | collective-permute-start | bytes 368648 | tf_op jit(solution)/shard_map/qkv_z/ppermute | solution.py:43
  18.8 16.8 %collective-permute-start.4 = (bf16[48,1280]{1,0:T(8,128)(2,1)S(1)}, bf16[48,1280]{1,0:T(8,128)(2,1)S(1)}, u32[]{:S(2)}, u32[]{:S(2)}) collective-permute-start(bf16[48,1280]{1,0:T(8,128)(2,1)S(1)} %pad_maximum_fusion.3), channel_id=1, source_target_pairs={{0,8},{1,9},{2,10},{3,11},{4,12},{5,13},{6,14},{7,15},{8,16},{9,17... | collective-permute-start | bytes 368648 | tf_op jit(solution)/shard_map/qkv_z/ppermute | solution.py:43
  42.2 22.0 %collective-permute-start.8 = (bf16[2,2,48,1280]{3,2,1,0:T(8,128)(2,1)S(1)}, bf16[2,2,48,1280]{3,2,1,0:T(8,128)(2,1)S(1)}, u32[]{:S(2)}, u32[]{:S(2)}) collective-permute-start(bf16[2,2,48,1280]{3,2,1,0:T(8,128)(2,1)S(1)} %maximum_select_fusion.3), channel_id=1, source_target_pairs={{0,4},{1,5},{2,6},{3,7},{4,0},{5,1},{6,2},{7,3},{8,12},{9,13},{10,... | collective-permute-start | bytes 1474568 | tf_op jit(solution)/shard_map/qkv_two/ppermute | solution.py:31
  46.9 17.4 %collective-permute-start.6 = (bf16[2,2,48,1280]{3,2,0,1:T(8,128)(2,1)S(1)}, bf16[2,2,48,1280]{3,2,0,1:T(8,128)(2,1)}, u32[]{:S(2)}, u32[]{:S(2)}) collective-permute-start(bf16[2,2,48,1280]{3,2,0,1:T(8,128)(2,1)S(1)} %maximum_select_fusion.2), channel_id=1, source_target_pairs={{0,2},{1,3},{2,0},{3,1},{4,6},{5,7},{6,4},{7,5},{8,10},{9,11},{10,... | collective-permute-start | bytes 1474568 | tf_op jit(solution)/shard_map/qkv_two/ppermute | solution.py:31
  66.4 30.9 %collective-permute-start.10 = (bf16[256,768]{0,1:T(8,128)(2,1)S(1)}, bf16[256,768]{0,1:T(8,128)(2,1)S(1)}, u32[]{:S(2)}, u32[]{:S(2)}) collective-permute-start(bf16[256,768]{0,1:T(8,128)(2,1)S(1)} %copy.129), channel_id=1, source_target_pairs={{0,4},{4,8},{8,12},{12,16},{16,20},{20,24},{24,28},{1,5},{5,9},{9,... | collective-permute-start | bytes 1179656 | tf_op jit(solution)/shard_map/ppermute | solution.py:47
  77.6 9.0 %collective-permute-start.11 = (bf16[80,768]{1,0:T(8,128)(2,1)S(1)}, bf16[80,768]{1,0:T(8,128)(2,1)S(1)}, u32[]{:S(2)}, u32[]{:S(2)}) collective-permute-start(bf16[80,768]{1,0:T(8,128)(2,1)S(1)} %dynamic-slice_bitcast_fusion.8), channel_id=1, source_target_pairs={{0,4},{1,5},{2,6},{3,7},{4,0},{5,1},{6,2},{7,3},{8,12},{9,13},{10,... | collective-permute-start | bytes 368648 | tf_op jit(solution)/shard_map/before_beside/ppermute | solution.py:31
  84.0 23.7 %collective-permute-start.15 = (bf16[256,768]{1,0:T(8,128)(2,1)}, bf16[256,768]{1,0:T(8,128)(2,1)S(1)}, u32[]{:S(2)}, u32[]{:S(2)}) collective-permute-start(bf16[256,768]{1,0:T(8,128)(2,1)} %get-tuple-element.77.q), channel_id=1, source_target_pairs={{4,0},{8,4},{12,8},{16,12},{20,16},{24,20},{28,24},{5,1},{9,5},{13... | collective-permute-start | bytes 1179656 | tf_op jit(solution)/shard_map/ppermute | solution.py:47
  86.7 10.7 %collective-permute-start.12 = (bf16[80,768]{1,0:T(8,128)(2,1)S(1)}, bf16[80,768]{1,0:T(8,128)(2,1)S(1)}, u32[]{:S(2)}, u32[]{:S(2)}) collective-permute-start(bf16[80,768]{1,0:T(8,128)(2,1)S(1)} %fusion.14), channel_id=1, source_target_pairs={{0,8},{1,9},{2,10},{3,11},{4,12},{5,13},{6,14},{7,15},{8,16},{9,17... | collective-permute-start | bytes 368648 | tf_op jit(solution)/shard_map/before_z/ppermute | solution.py:235
  89.9 9.7 %collective-permute-start.13 = (bf16[80,768]{1,0:T(8,128)(2,1)S(1)}, bf16[80,768]{1,0:T(8,128)(2,1)S(1)}, u32[]{:S(2)}, u32[]{:S(2)}) collective-permute-start(bf16[80,768]{1,0:T(8,128)(2,1)S(1)} %fusion.14), channel_id=1, source_target_pairs={{0,16},{1,17},{2,18},{3,19},{4,20},{5,21},{6,22},{7,23},{8,24},{9,... | collective-permute-start | bytes 368648 | tf_op jit(solution)/shard_map/before_z/ppermute | solution.py:235
  152.8 27.9 %collective-permute-start.19 = (bf16[256,896]{1,0:T(8,128)(2,1)S(1)}, bf16[256,896]{1,0:T(8,128)(2,1)S(1)}, u32[]{:S(2)}, u32[]{:S(2)}) collective-permute-start(bf16[256,896]{1,0:T(8,128)(2,1)S(1)} %get-tuple-element.100.dn.dd), channel_id=1, source_target_pairs={{4,0},{8,4},{12,8},{16,12},{20,16},{24,20},{28,24},{5,1},{9,5},{13... | collective-permute-start | bytes 1376264 | tf_op jit(solution)/shard_map/ppermute | solution.py:47
  159.0 21.7 %collective-permute-start.20 = (bf16[80,768]{1,0:T(8,128)(2,1)S(1)}, bf16[80,768]{1,0:T(8,128)(2,1)S(1)}, u32[]{:S(2)}, u32[]{:S(2)}) collective-permute-start(bf16[80,768]{1,0:T(8,128)(2,1)S(1)} %fusion.17), channel_id=1, source_target_pairs={{8,0},{9,1},{10,2},{11,3},{12,4},{13,5},{14,6},{15,7},{16,8},{17,9... | collective-permute-start | bytes 368648 | tf_op jit(solution)/shard_map/later_z/ppermute | solution.py:235
  160.3 20.5 %collective-permute-start.21 = (bf16[80,768]{1,0:T(8,128)(2,1)S(1)}, bf16[80,768]{1,0:T(8,128)(2,1)S(1)}, u32[]{:S(2)}, u32[]{:S(2)}) collective-permute-start(bf16[80,768]{1,0:T(8,128)(2,1)S(1)} %fusion.17), channel_id=1, source_target_pairs={{16,0},{17,1},{18,2},{19,3},{20,4},{21,5},{22,6},{23,7},{24,8},{25... | collective-permute-start | bytes 368648 | tf_op jit(solution)/shard_map/later_z/ppermute | solution.py:235
  161.6 19.2 %collective-permute-start.22 = (bf16[80,768]{1,0:T(8,128)(2,1)S(1)}, bf16[80,768]{1,0:T(8,128)(2,1)S(1)}, u32[]{:S(2)}, u32[]{:S(2)}) collective-permute-start(bf16[80,768]{1,0:T(8,128)(2,1)S(1)} %fusion.17), channel_id=1, source_target_pairs={{24,0},{25,1},{26,2},{27,3},{28,4},{29,5},{30,6},{31,7}} | collective-permute-start | bytes 368648 | tf_op jit(solution)/shard_map/later_z/ppermute | solution.py:235
  180.6 27.3 %collective-permute-start.24 = (bf16[768,768]{1,0:T(8,128)(2,1)}, bf16[768,768]{1,0:T(8,128)(2,1)}, u32[]{:S(2)}, u32[]{:S(2)}) collective-permute-start(bf16[768,768]{1,0:T(8,128)(2,1)} %get-tuple-element.118), channel_id=1, source_target_pairs={{0,1},{1,0},{2,3},{3,2},{4,5},{5,4},{6,7},{7,6},{8,9},{9,8},{10,11... | collective-permute-start | bytes 3538952 | tf_op jit(solution)/shard_map/d_qkv_core/ppermute | solution.py:31
  210.4 25.0 %collective-permute-start.28 = (bf16[2,2,48,1664]{3,2,0,1:T(8,128)(2,1)S(1)}, bf16[2,2,48,1664]{3,2,0,1:T(8,128)(2,1)}, u32[]{:S(2)}, u32[]{:S(2)}) collective-permute-start(bf16[2,2,48,1664]{3,2,0,1:T(8,128)(2,1)S(1)} %copy_bitcast_fusion), channel_id=1, source_target_pairs={{0,2},{1,3},{2,0},{3,1},{4,6},{5,7},{6,4},{7,5},{8,10},{9,11},{10,... | collective-permute-start | bytes 1916936 | tf_op jit(solution)/shard_map/d_qkv_one/ppermute | solution.py:31
  212.2 24.9 %collective-permute-start.29 = (bf16[2,2,48,1664]{3,2,1,0:T(8,128)(2,1)}, bf16[2,2,48,1664]{3,2,1,0:T(8,128)(2,1)}, u32[]{:S(2)}, u32[]{:S(2)}) collective-permute-start(bf16[2,2,48,1664]{3,2,1,0:T(8,128)(2,1)} %dynamic-slice_bitcast_fusion), channel_id=1, source_target_pairs={{0,4},{1,5},{2,6},{3,7},{4,0},{5,1},{6,2},{7,3},{8,12},{9,13},{10,... | collective-permute-start | bytes 1916936 | tf_op jit(solution)/shard_map/d_qkv_one/ppermute | solution.py:31
  240.8 15.6 %collective-permute-start.31 = (bf16[2,48,1664]{2,1,0:T(8,128)(2,1)S(1)}, bf16[2,48,1664]{2,1,0:T(8,128)(2,1)S(1)}, u32[]{:S(2)}, u32[]{:S(2)}) collective-permute-start(bf16[2,48,1664]{2,1,0:T(8,128)(2,1)S(1)} %dynamic-slice_bitcast_fusion.2), channel_id=1, source_target_pairs={{0,4},{1,5},{2,6},{3,7},{4,0},{5,1},{6,2},{7,3},{8,12},{9,13},{10,... | collective-permute-start | bytes 958472 | tf_op jit(solution)/shard_map/d_qkv_two/ppermute | solution.py:31
  241.7 15.3 %collective-permute-start.32 = (bf16[2,48,1664]{2,1,0:T(8,128)(2,1)S(1)}, bf16[2,48,1664]{2,1,0:T(8,128)(2,1)S(1)}, u32[]{:S(2)}, u32[]{:S(2)}) collective-permute-start(bf16[2,48,1664]{2,1,0:T(8,128)(2,1)S(1)} %dynamic-slice_bitcast_fusion.1), channel_id=1, source_target_pairs={{0,2},{1,3},{2,0},{3,1},{4,6},{5,7},{6,4},{7,5},{8,10},{9,11},{10,... | collective-permute-start | bytes 958472 | tf_op jit(solution)/shard_map/d_qkv_two/ppermute | solution.py:31
  257.1 8.6 %collective-permute-start.37 = (f32[12,129]{1,0:T(8,128)S(1)}, f32[12,129]{1,0:T(8,128)S(1)}, u32[]{:S(2)}, u32[]{:S(2)}) collective-permute-start(f32[12,129]{1,0:T(8,128)S(1)} %add.228), channel_id=1, source_target_pairs={{0,24},{1,25},{2,26},{3,27},{4,28},{5,29},{6,30},{7,31},{8,0},{9,1... | collective-permute-start | bytes 18584 | tf_op jit(solution)/shard_map/everywhere/ppermute | solution.py:43
  261.7 9.0 %collective-permute-start.33 = (bf16[48,1664]{1,0:T(8,128)(2,1)S(1)}, bf16[48,1664]{1,0:T(8,128)(2,1)S(1)}, u32[]{:S(2)}, u32[]{:S(2)}) collective-permute-start(bf16[48,1664]{1,0:T(8,128)(2,1)S(1)} %get-tuple-element.150), channel_id=1, source_target_pairs={{0,8},{1,9},{2,10},{3,11},{4,12},{5,13},{6,14},{7,15},{8,16},{9,17... | collective-permute-start | bytes 479240 | tf_op jit(solution)/shard_map/d_qkv_z/ppermute | solution.py:43
  261.8 18.8 %collective-permute-start.34 = (bf16[48,1664]{1,0:T(8,128)(2,1)S(1)}, bf16[48,1664]{1,0:T(8,128)(2,1)S(1)}, u32[]{:S(2)}, u32[]{:S(2)}) collective-permute-start(bf16[48,1664]{1,0:T(8,128)(2,1)S(1)} %get-tuple-element.152), channel_id=1, source_target_pairs={{0,16},{1,17},{2,18},{3,19},{4,20},{5,21},{6,22},{7,23},{8,24},{9,... | collective-permute-start | bytes 479240 | tf_op jit(solution)/shard_map/d_qkv_z/ppermute | solution.py:43
  265.7 15.3 %collective-permute-start.35 = (bf16[48,1664]{1,0:T(8,128)(2,1)S(1)}, bf16[48,1664]{1,0:T(8,128)(2,1)S(1)}, u32[]{:S(2)}, u32[]{:S(2)}) collective-permute-start(bf16[48,1664]{1,0:T(8,128)(2,1)S(1)} %get-tuple-element.151), channel_id=1, source_target_pairs={{0,24},{1,25},{2,26},{3,27},{4,28},{5,29},{6,30},{7,31},{8,0},{9,1... | collective-permute-start | bytes 479240 | tf_op jit(solution)/shard_map/d_qkv_z/ppermute | solution.py:43
  (59 other events, 462.9 us)
Sparse Core Ops, SparseCore 0:
  11.1 116.9 all-gather.1
  156.8 152.3 reduce-scatter.1

commit v5 on v4

--- a/solution.py
+++ b/solution.py
@@ -851,7 +851,7 @@
             pltpu.SemaphoreType.DMA((2 * slices,)),
             pltpu.SemaphoreType.DMA((2 * slices,)),
         ],
-        compiler_params=pltpu.CompilerParams(vmem_limit_bytes=44 * 2**20),
+        compiler_params=pltpu.CompilerParams(vmem_limit_bytes=38 * 2**20),
         cost_estimate=cost(20),
         name="middle",
     )(context, tok, cot, vec, b_u, ratio, denom, q, before, far, rest, *blocks)

time: 319 us -> 318 us (level)
  local copies, waits for them, and re-layouts: 25.8 us -> 22.6 us
  transfers between devices with their start and end apart: 42 -> 42, of which waited for: 27 -> 26; matrix products, arithmetic and copies ran while one was open for 9% -> 9% of each run, Pallas kernels for 19% -> 19%
where the time goes in v5:
time: 318 us; the launch traced here: 317 us
  waiting for transfers between devices  134 us (42%)
  Pallas kernels  79.4 us (25%)
  starting transfers between devices  50.8 us (16%)
  local copies, waits for them, and re-layouts  22.6 us (7%)
  between operations  15.3 us (5%)
  other arithmetic  14.9 us (5%)
    ppermute x22, waiting for transfers between devices, flip(): return lax.ppermute(a, BOTH, [(d, d ^ stride) for d in range(self.n)])  67.7 us
    ppermute x9, waiting for transfers between devices, turn_z(): lax.ppermute(a, BOTH, [(d, (d + 8 * by) % self.n) for d in range(self.n)])  31.2 us
    reduce_scatter x1, waiting for transfers between devices, on_device(): s_rest = lax.psum_scatter(g_rest, BOTH, scatter_dimension=0, tiled=True)  24.9 us
    pallas_call x1, Pallas kernels, on_device(): pl.pallas_call(functools.partial(middle_kernel, slices), out_shape=(wide3...  16.8 us
    pallas_call x1, Pallas kernels, on_device(): pl.pallas_call(query_back_kernel, grid_spec=pltpu.PrefetchScalarGridSpec(...  16.7 us
    pallas_call x1, Pallas kernels, on_device(): pl.pallas_call(key_back_kernel, grid_spec=pltpu.PrefetchScalarGridSpec(nu...  16.1 us
    ppermute x22, starting transfers between devices, flip(): return lax.ppermute(a, BOTH, [(d, d ^ stride) for d in range(self.n)])  15.9 us
    ppermute x9, starting transfers between devices, turn_z(): lax.ppermute(a, BOTH, [(d, (d + 8 * by) % self.n) for d in range(self.n)])  15 us
  transfers between devices with their start and end apart: 42, of which 26 were waited for; matrix products, arithmetic and copies ran while one was open for 9% of the time, Pallas kernels for 19%

profile of v5, /device:TPU:0, one launch (start us, length us, event | category | flops | bytes accessed | tf_op | source)
XLA Modules:
  0.0 316.5 jit_solution(2005960668583840159)
XLA Ops:
  14.0 4.8 %collective-permute-start.2 = (bf16[48,1280]{1,0:T(8,128)(2,1)S(1)}, bf16[48,1280]{1,0:T(8,128)(2,1)S(1)}, u32[]{:S(2)}, u32[]{:S(2)}) collective-permute-start(bf16[48,1280]{1,0:T(8,128)(2,1)S(1)} %pad_maximum_fusion.3), channel_id=1, source_target_pairs={{0,24},{1,25},{2,26},{3,27},{4,28},{5,29},{6,30},{7,31},{8,0},{9,1... | collective-permute-start | bytes 368648 | tf_op jit(solution)/shard_map/qkv_z/ppermute | solution.py:43
  22.5 13.2 %collective-permute-done.3 = bf16[48,1280]{1,0:T(8,128)(2,1)S(1)} collective-permute-done((bf16[48,1280]{1,0:T(8,128)(2,1)S(1)}, bf16[48,1280]{1,0:T(8,128)(2,1)S(1)}, u32[]{:S(2)}, u32[]{:S(2)}) %collective-permute-start.3) | collective-permute-done | bytes 122912 | tf_op jit(solution)/shard_map/qkv_z/ppermute | solution.py:43
  39.1 3.1 collective-permute-done.7
  48.9 15.2 %collective-permute-done.8 = bf16[2,2,48,1280]{3,2,1,0:T(8,128)(2,1)S(1)} collective-permute-done((bf16[2,2,48,1280]{3,2,1,0:T(8,128)(2,1)S(1)}, bf16[2,2,48,1280]{3,2,1,0:T(8,128)(2,1)S(1)}, u32[]{:S(2)}, u32[]{:S(2)}) %collective-permute-start.8) | collective-permute-done | bytes 491552 | tf_op jit(solution)/shard_map/qkv_two/ppermute | solution.py:31
  66.8 4.2 %collective-permute-start.10 = (bf16[256,768]{0,1:T(8,128)(2,1)S(1)}, bf16[256,768]{0,1:T(8,128)(2,1)}, u32[]{:S(2)}, u32[]{:S(2)}) collective-permute-start(bf16[256,768]{0,1:T(8,128)(2,1)S(1)} %copy.129), channel_id=1, source_target_pairs={{0,4},{4,8},{8,12},{12,16},{16,20},{20,24},{24,28},{1,5},{5,9},{9,... | collective-permute-start | bytes 1179656 | tf_op jit(solution)/shard_map/ppermute | solution.py:47
  71.5 6.1 %keys.1 = (f32[256,768]{1,0:T(8,128)}, f32[256,768]{1,0:T(8,128)}, bf16[256,768]{1,0:T(8,128)(2,1)}, bf16[256,768]{1,0:T(8,128)(2,1)}, bf16[2,80,768]{2,1,0:T(8,128)(2,1)}, /*index=5*/f32[16,768]{1,0:T(8,128)}) custom-call(s32[2]{0:T(128)} %pad_add_fusion.c_ref, bf16[256,768]{1,0:T(8,128)(2,1)} %bitcast.144, bf16[768,1280]{1,0:T(8,128)(2,1)} %bitcast.151, ...), custom_call_target="tpu_custom_call" | custom-call | flops 5000000000 | bytes 5000000 | tf_op jit(solution)/shard_map/keys/pallas_call | solution.py:781
  79.5 4.9 %queries.1 = (f32[256,768]{1,0:T(8,128)}, f32[256,768]{1,0:T(8,128)}, bf16[256,768]{1,0:T(8,128)(2,1)}) custom-call(s32[2]{0:T(128)} %pad_add_fusion.c_ref, bf16[256,768]{1,0:T(8,128)(2,1)} %bitcast.145, bf16[768,1280]{1,0:T(8,128)(2,1)} %bitcast.152, bf16[768,1280]{1,0:T(8,128)(2,1)} %collective-permute-done.9.other, f32[16,768]{1,0:T(8,128)} %get-tuple-element.76.vec, ...), custom_call_target="tpu_custom_call" | custom-call | flops 3000000000 | bytes 3000000 | tf_op jit(solution)/shard_map/queries/pallas_call | solution.py:792
  87.5 3.4 %collective-permute-start.12 = (bf16[80,768]{1,0:T(8,128)(2,1)S(1)}, bf16[80,768]{1,0:T(8,128)(2,1)S(1)}, u32[]{:S(2)}, u32[]{:S(2)}) collective-permute-start(bf16[80,768]{1,0:T(8,128)(2,1)S(1)} %fusion.14), channel_id=1, source_target_pairs={{0,8},{1,9},{2,10},{3,11},{4,12},{5,13},{6,14},{7,15},{8,16},{9,17... | collective-permute-start | bytes 368648 | tf_op jit(solution)/shard_map/before_z/ppermute | solution.py:235
  90.9 4.5 %collective-permute-start.13 = (bf16[80,768]{1,0:T(8,128)(2,1)S(1)}, bf16[80,768]{1,0:T(8,128)(2,1)S(1)}, u32[]{:S(2)}, u32[]{:S(2)}) collective-permute-start(bf16[80,768]{1,0:T(8,128)(2,1)S(1)} %fusion.14), channel_id=1, source_target_pairs={{0,16},{1,17},{2,18},{3,19},{4,20},{5,21},{6,22},{7,23},{8,24},{9,... | collective-permute-start | bytes 368648 | tf_op jit(solution)/shard_map/before_z/ppermute | solution.py:235
  103.7 4.8 %halo.1 = (bf16[256,768]{1,0:T(8,128)(2,1)}, bf16[256,768]{1,0:T(8,128)(2,1)}) custom-call(s32[2]{0:T(128)} %pad_add_fusion.c_ref, bf16[256,768]{1,0:T(8,128)(2,1)} %copy.116.halo, bf16[768,1280]{1,0:T(8,128)(2,1)} %bitcast.154, bf16[768,1280]{1,0:T(8,128)(2,1)} %collective-permute-done.9.other, f32[16,768]{1,0:T(8,128)} %get-tuple-element.76.vec, ...), custom_call_target="tpu_custom_call" | custom-call | flops 2000000000 | bytes 2000000 | tf_op jit(solution)/shard_map/halo/pallas_call | solution.py:802
  115.7 7.0 %attention.1 = (bf16[256,768]{1,0:T(8,128)(2,1)}, bf16[768,256]{1,0:T(8,128)(2,1)}, f32[256,768]{1,0:T(8,128)}, f32[256,768]{1,0:T(8,128)}) custom-call(bf16[256,768]{1,0:T(8,128)(2,1)} %get-tuple-element.77.q, bf16[256,768]{1,0:T(8,128)(2,1)} %get-tuple-element.78.k, bf16[256,768]{1,0:T(8,128)(2,1)} %get-tuple-element.79.v, ...), custom_call_target="tpu_custom_call" | custom-call | flops 5000000000 | bytes 5000000 | tf_op jit(solution)/shard_map/attention/pallas_call | solution.py:824
  122.8 5.6 %all-gather.2.cloned.1.call-done.rest_hbm = bf16[3072,1728]{1,0:T(8,128)(2,1)} async-done(((bf16[96,1728]{1,0:T(8,128)(2,1)}), bf16[3072,1728]{1,0:T(8,128)(2,1)}) %all-gather.2.cloned.1.call-update) | async-done | bytes 10616848 | tf_op jit(solution)/shard_map/all_gather | solution.py:755
  128.4 3.8 %fusion.24 = (bf16[32,1,24,960]{3,2,1,0:T(8,128)(2,1)S(1)}, bf16[32,1,24,960]{3,2,1,0:T(8,128)(2,1)S(1)}, bf16[32,1,24,960]{3,2,1,0:T(8,128)(2,1)S(1)}, bf16[32,1,24,960]{3,2,1,0:T(8,128)(2,1)S(1)}) fusion(bf16[32,4,24,1728]{3,2,1,0:T(8,128)(2,1)} %bitcast.160), kind=kLoop, calls=%fused_computation.141 | loop fusion | bytes 11796480 | tf_op jit(solution)/shard_map/slice | solution.py:836
  132.3 16.8 %middle.1 = (f32[256,768]{1,0:T(8,128)}, f32[256,768]{1,0:T(8,128)S(1)}, bf16[256,768]{1,0:T(8,128)(2,1)S(1)}, bf16[256,896]{1,0:T(8,128)(2,1)S(1)}, bf16[2,80,7...) custom-call(bf16[256,768]{1,0:T(8,128)(2,1)S(1)} %copy-done.13, ...), custom_call_target="tpu_custom_call" | custom-call | flops 20000000000 | bytes 20000000 | tf_op jit(solution)/shard_map/middle/pallas_call | solution.py:838
  160.4 16.7 %query_back.1 = (bf16[256,768]{1,0:T(8,128)(2,1)}, bf16[768,768]{1,0:T(8,128)(2,1)}, bf16[768,768]{1,0:T(8,128)(2,1)}, f32[6,8,256]{2,1,0:T(8,128)}, f32[8,768]{1,0:T(8,128)}) custom-call(s32[2]{0:T(128)} %pad_add_fusion.c_ref, bf16[768,256]{1,0:T(8,128)(2,1)} %bitcast.161, bf16[768,256]{1,0:T(8,128)(2,1)} %get-tuple-element.98.context, ...), custom_call_target="tpu_custom_call" | custom-call | flops 1000000 | bytes 1000 | tf_op jit(solution)/shard_map/query_back/pallas_call | solution.py:889
  184.6 16.1 %key_back.1 = (bf16[256,768]{1,0:T(8,128)(2,1)}, bf16[256,768]{1,0:T(8,128)(2,1)}, bf16[768,768]{1,0:T(8,128)(2,1)}, bf16[768,768]{1,0:T(8,128)(2,1)}, bf16[768,128]{1,0:T(8,128)(2,1)}) custom-call(s32[2]{0:T(128)} %pad_add_fusion.c_ref, bf16[768,256]{1,0:T(8,128)(2,1)} %bitcast.162, bf16[256,768]{1,0:T(8,128)(2,1)} %get-tuple-element.77.q, ...), custom_call_target="tpu_custom_call" | custom-call | flops 1000000 | bytes 1000 | tf_op jit(solution)/shard_map/key_back/pallas_call | solution.py:912
  210.0 22.7 %collective-permute-done.28 = bf16[2,2,48,1664]{3,2,0,1:T(8,128)(2,1)} collective-permute-done((bf16[2,2,48,1664]{3,2,0,1:T(8,128)(2,1)S(1)}, bf16[2,2,48,1664]{3,2,0,1:T(8,128)(2,1)}, u32[]{:S(2)}, u32[]{:S(2)}) %collective-permute-start.28) | collective-permute-done | bytes 639008 | tf_op jit(solution)/shard_map/d_qkv_one/ppermute | solution.py:31
  240.4 5.2 %tokens.1 = f32[256,768]{1,0:T(8,128)} custom-call(s32[2]{0:T(128)} %pad_add_fusion.c_ref, f32[256,768]{1,0:T(8,128)} %copy-done.3, bf16[256,768]{1,0:T(8,128)(2,1)} %get-tuple-element.104.dq, bf16[256,768]{1,0:T(8,128)(2,1)} %get-tuple-element.115.dk, bf16[256,768]{1,0:T(8,128)(2,1)} %get-tuple-element.116.dv, bf16[768,1280]{1,0:T(8,128)(2,1)} %bitcast.155, ...), custom_call_target="tpu_custom_call" | custom-call | flops 1000000 | bytes 1000 | tf_op jit(solution)/shard_map/tokens/pallas_call | solution.py:938
  245.6 7.9 %collective-permute-done.31 = bf16[2,48,1664]{2,1,0:T(8,128)(2,1)S(1)} collective-permute-done((bf16[2,48,1664]{2,1,0:T(8,128)(2,1)S(1)}, bf16[2,48,1664]{2,1,0:T(8,128)(2,1)S(1)}, u32[]{:S(2)}, u32[]{:S(2)}) %collective-permute-start.31) | collective-permute-done | bytes 319520 | tf_op jit(solution)/shard_map/d_qkv_two/ppermute | solution.py:31
  256.3 3.2 %collective-permute-start.38 = (f32[12,129]{1,0:T(8,128)S(1)}, f32[12,129]{1,0:T(8,128)S(1)}, u32[]{:S(2)}, u32[]{:S(2)}) collective-permute-start(f32[12,129]{1,0:T(8,128)S(1)} %add.228), channel_id=1, source_target_pairs={{0,16},{1,17},{2,18},{3,19},{4,20},{5,21},{6,22},{7,23},{8,24},{9,... | collective-permute-start | bytes 18584 | tf_op jit(solution)/shard_map/everywhere/ppermute | solution.py:43
  260.4 3.8 %collective-permute-start.34 = (bf16[48,1664]{1,0:T(8,128)(2,1)S(1)}, bf16[48,1664]{1,0:T(8,128)(2,1)S(1)}, u32[]{:S(2)}, u32[]{:S(2)}) collective-permute-start(bf16[48,1664]{1,0:T(8,128)(2,1)S(1)} %get-tuple-element.152), channel_id=1, source_target_pairs={{0,16},{1,17},{2,18},{3,19},{4,20},{5,21},{6,22},{7,23},{8,24},{9,... | collective-permute-start | bytes 479240 | tf_op jit(solution)/shard_map/d_qkv_z/ppermute | solution.py:43
  265.4 3.8 %collective-permute-done.33 = bf16[48,1664]{1,0:T(8,128)(2,1)S(1)} collective-permute-done((bf16[48,1664]{1,0:T(8,128)(2,1)S(1)}, bf16[48,1664]{1,0:T(8,128)(2,1)S(1)}, u32[]{:S(2)}, u32[]{:S(2)}) %collective-permute-start.33) | collective-permute-done | bytes 159776 | tf_op jit(solution)/shard_map/d_qkv_z/ppermute | solution.py:43
  269.2 9.7 %collective-permute-done.34 = bf16[48,1664]{1,0:T(8,128)(2,1)S(1)} collective-permute-done((bf16[48,1664]{1,0:T(8,128)(2,1)S(1)}, bf16[48,1664]{1,0:T(8,128)(2,1)S(1)}, u32[]{:S(2)}, u32[]{:S(2)}) %collective-permute-start.34) | collective-permute-done | bytes 159776 | tf_op jit(solution)/shard_map/d_qkv_z/ppermute | solution.py:43
  283.0 24.9 %reduce-scatter.2.cloned.1.call-done.packed = bf16[96,1536]{1,0:T(8,128)(2,1)} async-done(((bf16[3072,1536]{1,0:T(8,128)(2,1)}), bf16[96,1536]{1,0:T(8,128)(2,1)}) %reduce-scatter.2.cloned.1.call-update) | async-done | bytes 294928 | tf_op jit(solution)/shard_map/reduce_scatter | solution.py:860
  (265 shorter events, 89.8 us)
Async XLA Ops:
  7.3 121.1 %all-gather.2.cloned.1.call-start = ((), (), s32[]{:S(2)}) async-start(), calls=%async_computation.1 | async-start | bytes 11354112 | tf_op jit(solution)/shard_map/all_gather | solution.py:755
  10.8 297.0 %reduce-scatter.2.cloned.1.call-start = ((), (), s32[]{:S(2)}) async-start(), calls=%async_computation.2 | async-start | bytes 9732096 | tf_op jit(solution)/shard_map/reduce_scatter | solution.py:860
  18.8 16.9 %collective-permute-start.3 = (bf16[48,1280]{1,0:T(8,128)(2,1)S(1)}, bf16[48,1280]{1,0:T(8,128)(2,1)S(1)}, u32[]{:S(2)}, u32[]{:S(2)}) collective-permute-start(bf16[48,1280]{1,0:T(8,128)(2,1)S(1)} %pad_maximum_fusion.3), channel_id=1, source_target_pairs={{0,16},{1,17},{2,18},{3,19},{4,20},{5,21},{6,22},{7,23},{8,24},{9,... | collective-permute-start | bytes 368648 | tf_op jit(solution)/shard_map/qkv_z/ppermute | solution.py:43
  18.9 16.8 %collective-permute-start.4 = (bf16[48,1280]{1,0:T(8,128)(2,1)S(1)}, bf16[48,1280]{1,0:T(8,128)(2,1)S(1)}, u32[]{:S(2)}, u32[]{:S(2)}) collective-permute-start(bf16[48,1280]{1,0:T(8,128)(2,1)S(1)} %pad_maximum_fusion.3), channel_id=1, source_target_pairs={{0,8},{1,9},{2,10},{3,11},{4,12},{5,13},{6,14},{7,15},{8,16},{9,17... | collective-permute-start | bytes 368648 | tf_op jit(solution)/shard_map/qkv_z/ppermute | solution.py:43
  42.2 22.0 %collective-permute-start.8 = (bf16[2,2,48,1280]{3,2,1,0:T(8,128)(2,1)S(1)}, bf16[2,2,48,1280]{3,2,1,0:T(8,128)(2,1)S(1)}, u32[]{:S(2)}, u32[]{:S(2)}) collective-permute-start(bf16[2,2,48,1280]{3,2,1,0:T(8,128)(2,1)S(1)} %maximum_select_fusion.3), channel_id=1, source_target_pairs={{0,4},{1,5},{2,6},{3,7},{4,0},{5,1},{6,2},{7,3},{8,12},{9,13},{10,... | collective-permute-start | bytes 1474568 | tf_op jit(solution)/shard_map/qkv_two/ppermute | solution.py:31
  45.7 18.6 %collective-permute-start.6 = (bf16[2,2,48,1280]{3,2,0,1:T(8,128)(2,1)S(1)}, bf16[2,2,48,1280]{3,2,0,1:T(8,128)(2,1)}, u32[]{:S(2)}, u32[]{:S(2)}) collective-permute-start(bf16[2,2,48,1280]{3,2,0,1:T(8,128)(2,1)S(1)} %maximum_select_fusion.2), channel_id=1, source_target_pairs={{0,2},{1,3},{2,0},{3,1},{4,6},{5,7},{6,4},{7,5},{8,10},{9,11},{10,... | collective-permute-start | bytes 1474568 | tf_op jit(solution)/shard_map/qkv_two/ppermute | solution.py:31
  66.8 31.0 %collective-permute-start.10 = (bf16[256,768]{0,1:T(8,128)(2,1)S(1)}, bf16[256,768]{0,1:T(8,128)(2,1)}, u32[]{:S(2)}, u32[]{:S(2)}) collective-permute-start(bf16[256,768]{0,1:T(8,128)(2,1)S(1)} %copy.129), channel_id=1, source_target_pairs={{0,4},{4,8},{8,12},{12,16},{16,20},{20,24},{24,28},{1,5},{5,9},{9,... | collective-permute-start | bytes 1179656 | tf_op jit(solution)/shard_map/ppermute | solution.py:47
  78.6 8.8 %collective-permute-start.11 = (bf16[80,768]{1,0:T(8,128)(2,1)S(1)}, bf16[80,768]{1,0:T(8,128)(2,1)S(1)}, u32[]{:S(2)}, u32[]{:S(2)}) collective-permute-start(bf16[80,768]{1,0:T(8,128)(2,1)S(1)} %dynamic-slice_bitcast_fusion.8), channel_id=1, source_target_pairs={{0,4},{1,5},{2,6},{3,7},{4,0},{5,1},{6,2},{7,3},{8,12},{9,13},{10,... | collective-permute-start | bytes 368648 | tf_op jit(solution)/shard_map/before_beside/ppermute | solution.py:31
  84.4 24.4 %collective-permute-start.15 = (bf16[256,768]{1,0:T(8,128)(2,1)}, bf16[256,768]{1,0:T(8,128)(2,1)S(1)}, u32[]{:S(2)}, u32[]{:S(2)}) collective-permute-start(bf16[256,768]{1,0:T(8,128)(2,1)} %get-tuple-element.77.q), channel_id=1, source_target_pairs={{4,0},{8,4},{12,8},{16,12},{20,16},{24,20},{28,24},{5,1},{9,5},{13... | collective-permute-start | bytes 1179656 | tf_op jit(solution)/shard_map/ppermute | solution.py:47
  87.5 10.3 %collective-permute-start.12 = (bf16[80,768]{1,0:T(8,128)(2,1)S(1)}, bf16[80,768]{1,0:T(8,128)(2,1)S(1)}, u32[]{:S(2)}, u32[]{:S(2)}) collective-permute-start(bf16[80,768]{1,0:T(8,128)(2,1)S(1)} %fusion.14), channel_id=1, source_target_pairs={{0,8},{1,9},{2,10},{3,11},{4,12},{5,13},{6,14},{7,15},{8,16},{9,17... | collective-permute-start | bytes 368648 | tf_op jit(solution)/shard_map/before_z/ppermute | solution.py:235
  90.9 8.8 %collective-permute-start.13 = (bf16[80,768]{1,0:T(8,128)(2,1)S(1)}, bf16[80,768]{1,0:T(8,128)(2,1)S(1)}, u32[]{:S(2)}, u32[]{:S(2)}) collective-permute-start(bf16[80,768]{1,0:T(8,128)(2,1)S(1)} %fusion.14), channel_id=1, source_target_pairs={{0,16},{1,17},{2,18},{3,19},{4,20},{5,21},{6,22},{7,23},{8,24},{9,... | collective-permute-start | bytes 368648 | tf_op jit(solution)/shard_map/before_z/ppermute | solution.py:235
  150.3 27.6 %collective-permute-start.19 = (bf16[256,896]{1,0:T(8,128)(2,1)S(1)}, bf16[256,896]{1,0:T(8,128)(2,1)S(1)}, u32[]{:S(2)}, u32[]{:S(2)}) collective-permute-start(bf16[256,896]{1,0:T(8,128)(2,1)S(1)} %get-tuple-element.100.dn.dd), channel_id=1, source_target_pairs={{4,0},{8,4},{12,8},{16,12},{20,16},{24,20},{28,24},{5,1},{9,5},{13... | collective-permute-start | bytes 1376264 | tf_op jit(solution)/shard_map/ppermute | solution.py:47
  156.5 21.5 %collective-permute-start.20 = (bf16[80,768]{1,0:T(8,128)(2,1)S(1)}, bf16[80,768]{1,0:T(8,128)(2,1)S(1)}, u32[]{:S(2)}, u32[]{:S(2)}) collective-permute-start(bf16[80,768]{1,0:T(8,128)(2,1)S(1)} %fusion.17), channel_id=1, source_target_pairs={{8,0},{9,1},{10,2},{11,3},{12,4},{13,5},{14,6},{15,7},{16,8},{17,9... | collective-permute-start | bytes 368648 | tf_op jit(solution)/shard_map/later_z/ppermute | solution.py:235
  157.8 20.2 %collective-permute-start.21 = (bf16[80,768]{1,0:T(8,128)(2,1)S(1)}, bf16[80,768]{1,0:T(8,128)(2,1)S(1)}, u32[]{:S(2)}, u32[]{:S(2)}) collective-permute-start(bf16[80,768]{1,0:T(8,128)(2,1)S(1)} %fusion.17), channel_id=1, source_target_pairs={{16,0},{17,1},{18,2},{19,3},{20,4},{21,5},{22,6},{23,7},{24,8},{25... | collective-permute-start | bytes 368648 | tf_op jit(solution)/shard_map/later_z/ppermute | solution.py:235
  159.1 18.9 %collective-permute-start.22 = (bf16[80,768]{1,0:T(8,128)(2,1)S(1)}, bf16[80,768]{1,0:T(8,128)(2,1)S(1)}, u32[]{:S(2)}, u32[]{:S(2)}) collective-permute-start(bf16[80,768]{1,0:T(8,128)(2,1)S(1)} %fusion.17), channel_id=1, source_target_pairs={{24,0},{25,1},{26,2},{27,3},{28,4},{29,5},{30,6},{31,7}} | collective-permute-start | bytes 368648 | tf_op jit(solution)/shard_map/later_z/ppermute | solution.py:235
  177.9 27.3 %collective-permute-start.24 = (bf16[768,768]{1,0:T(8,128)(2,1)}, bf16[768,768]{1,0:T(8,128)(2,1)}, u32[]{:S(2)}, u32[]{:S(2)}) collective-permute-start(bf16[768,768]{1,0:T(8,128)(2,1)} %get-tuple-element.118), channel_id=1, source_target_pairs={{0,1},{1,0},{2,3},{3,2},{4,5},{5,4},{6,7},{7,6},{8,9},{9,8},{10,11... | collective-permute-start | bytes 3538952 | tf_op jit(solution)/shard_map/d_qkv_core/ppermute | solution.py:31
  207.7 25.0 %collective-permute-start.28 = (bf16[2,2,48,1664]{3,2,0,1:T(8,128)(2,1)S(1)}, bf16[2,2,48,1664]{3,2,0,1:T(8,128)(2,1)}, u32[]{:S(2)}, u32[]{:S(2)}) collective-permute-start(bf16[2,2,48,1664]{3,2,0,1:T(8,128)(2,1)S(1)} %copy_bitcast_fusion), channel_id=1, source_target_pairs={{0,2},{1,3},{2,0},{3,1},{4,6},{5,7},{6,4},{7,5},{8,10},{9,11},{10,... | collective-permute-start | bytes 1916936 | tf_op jit(solution)/shard_map/d_qkv_one/ppermute | solution.py:31
  209.5 24.9 %collective-permute-start.29 = (bf16[2,2,48,1664]{3,2,1,0:T(8,128)(2,1)}, bf16[2,2,48,1664]{3,2,1,0:T(8,128)(2,1)}, u32[]{:S(2)}, u32[]{:S(2)}) collective-permute-start(bf16[2,2,48,1664]{3,2,1,0:T(8,128)(2,1)} %dynamic-slice_bitcast_fusion), channel_id=1, source_target_pairs={{0,4},{1,5},{2,6},{3,7},{4,0},{5,1},{6,2},{7,3},{8,12},{9,13},{10,... | collective-permute-start | bytes 1916936 | tf_op jit(solution)/shard_map/d_qkv_one/ppermute | solution.py:31
  238.1 15.4 %collective-permute-start.31 = (bf16[2,48,1664]{2,1,0:T(8,128)(2,1)S(1)}, bf16[2,48,1664]{2,1,0:T(8,128)(2,1)S(1)}, u32[]{:S(2)}, u32[]{:S(2)}) collective-permute-start(bf16[2,48,1664]{2,1,0:T(8,128)(2,1)S(1)} %dynamic-slice_bitcast_fusion.2), channel_id=1, source_target_pairs={{0,4},{1,5},{2,6},{3,7},{4,0},{5,1},{6,2},{7,3},{8,12},{9,13},{10,... | collective-permute-start | bytes 958472 | tf_op jit(solution)/shard_map/d_qkv_two/ppermute | solution.py:31
  239.1 15.7 %collective-permute-start.32 = (bf16[2,48,1664]{2,1,0:T(8,128)(2,1)S(1)}, bf16[2,48,1664]{2,1,0:T(8,128)(2,1)S(1)}, u32[]{:S(2)}, u32[]{:S(2)}) collective-permute-start(bf16[2,48,1664]{2,1,0:T(8,128)(2,1)S(1)} %dynamic-slice_bitcast_fusion.1), channel_id=1, source_target_pairs={{0,2},{1,3},{2,0},{3,1},{4,6},{5,7},{6,4},{7,5},{8,10},{9,11},{10,... | collective-permute-start | bytes 958472 | tf_op jit(solution)/shard_map/d_qkv_two/ppermute | solution.py:31
  254.8 9.5 %collective-permute-start.37 = (f32[12,129]{1,0:T(8,128)S(1)}, f32[12,129]{1,0:T(8,128)S(1)}, u32[]{:S(2)}, u32[]{:S(2)}) collective-permute-start(f32[12,129]{1,0:T(8,128)S(1)} %add.228), channel_id=1, source_target_pairs={{0,24},{1,25},{2,26},{3,27},{4,28},{5,29},{6,30},{7,31},{8,0},{9,1... | collective-permute-start | bytes 18584 | tf_op jit(solution)/shard_map/everywhere/ppermute | solution.py:43
  260.2 9.0 %collective-permute-start.33 = (bf16[48,1664]{1,0:T(8,128)(2,1)S(1)}, bf16[48,1664]{1,0:T(8,128)(2,1)S(1)}, u32[]{:S(2)}, u32[]{:S(2)}) collective-permute-start(bf16[48,1664]{1,0:T(8,128)(2,1)S(1)} %get-tuple-element.150), channel_id=1, source_target_pairs={{0,8},{1,9},{2,10},{3,11},{4,12},{5,13},{6,14},{7,15},{8,16},{9,17... | collective-permute-start | bytes 479240 | tf_op jit(solution)/shard_map/d_qkv_z/ppermute | solution.py:43
  260.4 18.5 %collective-permute-start.34 = (bf16[48,1664]{1,0:T(8,128)(2,1)S(1)}, bf16[48,1664]{1,0:T(8,128)(2,1)S(1)}, u32[]{:S(2)}, u32[]{:S(2)}) collective-permute-start(bf16[48,1664]{1,0:T(8,128)(2,1)S(1)} %get-tuple-element.152), channel_id=1, source_target_pairs={{0,16},{1,17},{2,18},{3,19},{4,20},{5,21},{6,22},{7,23},{8,24},{9,... | collective-permute-start | bytes 479240 | tf_op jit(solution)/shard_map/d_qkv_z/ppermute | solution.py:43
  264.2 15.4 %collective-permute-start.35 = (bf16[48,1664]{1,0:T(8,128)(2,1)S(1)}, bf16[48,1664]{1,0:T(8,128)(2,1)S(1)}, u32[]{:S(2)}, u32[]{:S(2)}) collective-permute-start(bf16[48,1664]{1,0:T(8,128)(2,1)S(1)} %get-tuple-element.151), channel_id=1, source_target_pairs={{0,24},{1,25},{2,26},{3,27},{4,28},{5,29},{6,30},{7,31},{8,0},{9,1... | collective-permute-start | bytes 479240 | tf_op jit(solution)/shard_map/d_qkv_z/ppermute | solution.py:43
  (59 other events, 448.6 us)
Sparse Core Ops, SparseCore 0:
  11.1 117.2 all-gather.1
  154.4 153.4 reduce-scatter.1
